TPU v7x, 128 devices: a whole 4x4x4 slice. The times are simulated.
128 devices in a mesh: seq: 2 (over core), dp: 64 (over z, x, y).
Axes of the slice: x: 4, y: 4, z: 4, core: 2. Of those that a mesh axis runs over, the one named last changes fastest.
Arguments:
- tokens: bfloat16 [16384, 1536], P(('dp', 'seq')), may hold values from -6 to 6
- out_grad: bfloat16 [16384, 1536], P(('dp', 'seq')), may hold values from -6 to 6
- lengths: int32 [64, 4], P('dp'), may hold values from 1 to 192, 256 in all within a row
- routes: int32 [16384, 6], P(('dp', 'seq')), may hold values from 0 to 63, all different within a row; in each aligned block of 128 rows (0 to 127, 128 to 255, ...) at most 24 rows name the same one
- in_norm: bfloat16 [1536], P(('seq', 'dp')), may hold values from 0.5 to 1.5
- in_proj: bfloat16 [1536, 6448], P(('seq', 'dp')), may hold values from -0.15625 to 0.15625
- conv_weight: bfloat16 [3328, 4], P(('seq', 'dp')), may hold values from -3 to 3
- conv_bias: bfloat16 [3328], P(('seq', 'dp')), may hold values from -2 to 2
- head_params: bfloat16 [3, 48], replicated, may hold values from -5 to 1.5, as said below
- mixer_norm: bfloat16 [3072], P(('seq', 'dp')), may hold values from 0.5 to 1.5
- out_proj: bfloat16 [3072, 1536], P(('seq', 'dp')), may hold values from -0.109375 to 0.109375
- ffn_norm: bfloat16 [1536], P(('seq', 'dp')), may hold values from 0.5 to 1.5
- router: bfloat16 [1536, 64], P(('seq', 'dp')), may hold values from -0.078125 to 0.078125
- shared_gate_up: bfloat16 [1536, 2048], P(('seq', 'dp')), may hold values from -0.15625 to 0.15625
- shared_down: bfloat16 [1024, 1536], P(('seq', 'dp')), may hold values from -0.25 to 0.25
- expert_gate_up: bfloat16 [64, 1536, 1024], P('dp', 'seq'), may hold values from -0.15625 to 0.15625
- expert_down: bfloat16 [64, 512, 1536], P('dp', 'seq'), may hold values from -0.5 to 0.5
Outputs:
- block_out: bfloat16 [16384, 1536], P(('dp', 'seq'))
- token_grad: bfloat16 [16384, 1536], P(('dp', 'seq'))
- in_norm_grad: float32 [1536], P(('seq', 'dp'))
- in_proj_grad: float32 [1536, 6448], P(('seq', 'dp'))
- conv_weight_grad: float32 [3328, 4], P(('seq', 'dp'))
- conv_bias_grad: float32 [3328], P(('seq', 'dp'))
- head_grad: float32 [3, 48], replicated
- mixer_norm_grad: float32 [3072], P(('seq', 'dp'))
- out_proj_grad: float32 [3072, 1536], P(('seq', 'dp'))
- ffn_norm_grad: float32 [1536], P(('seq', 'dp'))
- router_grad: float32 [1536, 64], P(('seq', 'dp'))
- shared_gate_up_grad: float32 [1536, 2048], P(('seq', 'dp'))
- shared_down_grad: float32 [1024, 1536], P(('seq', 'dp'))
- expert_gate_up_grad: float32 [64, 1536, 1024], P('dp', 'seq')
- expert_down_grad: float32 [64, 512, 1536], P('dp', 'seq')
Inputs may be any that keep to these rules, and one draw needn't show every extreme that they name: Row g holds the lengths of the 4 sequences packed in order into the 256 tokens of group g; each row sums to 256, and its longest sequence has exactly 192 tokens. `routes`: each row names 6 different experts. Among the rows of one device (aligned blocks of 128 rows) no expert is named more than 24 times, and 24 is reached. `head_params`: row 0 holds the logarithms of the heads' decay rates, row 1 the biases of their step sizes, row 2 their skip weights.
All inputs are finite; a program needn't handle non-finite values.
Results may differ from a plain program's by a relative error of at most 0.022.
Values may be sent and summed in bfloat16 or wider, within the bound.
A program may use at most 448 MiB of HBM per device.

v0:
```python
import jax
import jax.numpy as jnp
from jax import lax
from jax.sharding import Mesh
from jax.sharding import PartitionSpec as P

BLOCK = 128
SEQ_DP = ("seq", "dp_0", "dp_1", "dp_2")
DP = ("dp_0", "dp_1", "dp_2")
DP_SEQ = ("dp_0", "dp_1", "dp_2", "seq")


epsilon = 1e-05
highest = lax.Precision.HIGHEST


def in_one_piece(arrays, axis, dim, along):
    columns = [a.reshape(*a.shape[:along], -1) for a in arrays]
    both = jnp.concatenate(columns, axis=along)
    filled, at, done = (lax.all_gather(both, axis, axis=dim, tiled=True), 0, [])
    for a, column in zip(arrays, columns):
        piece = filled[..., at : at + column.shape[along]]
        done.append(piece.reshape(*piece.shape[:along], *a.shape[along:]))
        at += column.shape[along]
    return tuple(done)


def joined_along(pieces, dim):
    pieces = jnp.moveaxis(pieces, 0, dim)
    lengths = pieces.shape
    return pieces.reshape(*lengths[:dim], lengths[dim] * lengths[dim + 1], *lengths[dim + 2 :])


def gather_together(arrays, axis, dims):
    vector = jnp.concatenate([a.reshape(-1) for a in arrays])
    lines, at, done = (lax.all_gather(vector, axis), 0, [])
    for a, dim in zip(arrays, dims):
        pieces = lines[:, at : at + a.size].reshape(-1, *a.shape)
        done.append(joined_along(pieces, dim))
        at += a.size
    return tuple(done)


def shifted(block, axis, distance):
    devices = range(lax.axis_size(axis))
    route = [(i - distance, i) for i in devices if i - distance in devices]
    return lax.ppermute(block, axis, route)


def entering_2(value, axis, combine, identity):
    peers, mine = (lax.axis_size(axis), lax.axis_index(axis))
    everything = jax.tree.map(
        lambda part, kind: lax.all_gather(part.astype(kind), axis),
        value,
        (jnp.bfloat16, jnp.bfloat16),
    )
    start = jax.tree.map(
        lambda part, zero: jnp.broadcast_to(jnp.asarray(zero, part.dtype), part.shape),
        value,
        identity,
    )

    def lap(k, before):
        reached = k < mine
        new = combine(
            before, jax.tree.map(lambda part, own: part[k].astype(own.dtype), everything, value)
        )
        return jax.tree.map(lambda a, b: jnp.where(reached, a, b), new, before)

    return lax.fori_loop(0, peers, lap, start)


def entering_3(value, axis, combine, identity):
    peers, mine = (lax.axis_size(axis), lax.axis_index(axis))
    everything = jax.tree.map(
        lambda part, kind: lax.all_gather(part.astype(kind), axis),
        value,
        jax.tree.map(lambda a: jnp.bfloat16 if a.dtype == jnp.float32 else a.dtype, value),
    )
    start = jax.tree.map(
        lambda part, zero: jnp.broadcast_to(jnp.asarray(zero, part.dtype), part.shape),
        value,
        identity,
    )

    def lap(k, before):
        at = peers - 1 - k
        reached = at > mine
        new = combine(
            before, jax.tree.map(lambda part, own: part[at].astype(own.dtype), everything, value)
        )
        return jax.tree.map(lambda a, b: jnp.where(reached, a, b), new, before)

    return lax.fori_loop(0, peers, lap, start)


def cut_along(value, dim, peers):
    before, after = (value.shape[:dim], value.shape[dim + 1 :])
    return jnp.moveaxis(value.reshape(*before, peers, -1, *after), dim, 0)


def one_scatter(arrays, axis, dims):
    peers = lax.axis_size(axis)
    pieces = [cut_along(a, dim, peers) for a, dim in zip(arrays, dims)]
    lines = jnp.concatenate([b.reshape(peers, -1) for b in pieces], axis=1)
    width = max(16, -(-lines.shape[1] // 1024) * 8)
    lines = jnp.pad(lines, ((0, 0), (0, width * 128 - lines.shape[1]))).reshape(-1, 128)
    vector, at, done = (lax.psum_scatter(lines, axis, tiled=True).reshape(-1), 0, [])
    for b in pieces:
        part = b[0]
        done.append(vector[at : at + part.size].reshape(part.shape))
        at += part.size
    return tuple(done)


def over_axes(value, axes):
    for axis in axes:
        value = lax.psum(value, axis)
    return value


def summed_on_arrival(value, axis, dim):
    peers = lax.axis_size(axis)
    pieces = lax.all_to_all(cut_along(value, dim, peers), axis, 0, 0, tiled=True)
    return jnp.sum(pieces.astype(jnp.float32), axis=0)


def product(left_op, right_op):
    return jnp.dot(left_op, right_op, preferred_element_type=jnp.float32)


def rms_scale(values, gain_vec):
    return (
        values * lax.rsqrt(jnp.mean(values * values, axis=-1, keepdims=True) + epsilon) * gain_vec
    )


def swish_product(gate_up):
    half_width = gate_up.shape[-1] // 2
    return jax.nn.silu(gate_up[..., :half_width]) * gate_up[..., half_width:]


def conv_taps(padded, pad_segment, segment, conv_w, conv_b):
    length = segment.shape[0]
    running = jnp.zeros((length, conv_w.shape[0]), jnp.float32) + conv_b[None, :]
    for tap_index in range(conv_w.shape[1]):
        same_doc = (pad_segment[tap_index : tap_index + length] == segment).astype(jnp.float32)
        running = (
            running
            + conv_w[:, tap_index][None, :]
            * padded[tap_index : tap_index + length]
            * same_doc[:, None]
        )
    return jax.nn.silu(running)


def ssd_blocks(x_heads, b_mat, c_mat, rate_vals, step_vals, skip_vals, segment):
    length, head_count, head_dim = x_heads.shape
    state_dim = b_mat.shape[1]
    blocks = length // BLOCK
    positions = jnp.arange(BLOCK, dtype=jnp.int32)
    causal = positions[:, None] >= positions[None, :]

    def one_block(carry_in, pieces):
        held_state, held_segment = carry_in
        x_blk, b_blk, c_blk, r_blk, s_blk, g_blk = pieces
        cum_rate = jnp.cumsum(r_blk, axis=0)
        inside = (g_blk[:, None] == g_blk[None, :]) & causal
        inside_f = inside.astype(jnp.float32)[:, :, None]
        spread = cum_rate[:, None, :] - cum_rate[None, :, :]
        decays = jnp.exp(jnp.where(inside[:, :, None], spread, -80.0)) * inside_f
        scores = jnp.dot(c_blk, b_blk.T, precision=highest, preferred_element_type=jnp.float32)
        mixing = decays * scores[:, :, None] * s_blk[None, :, :]
        inner_part = jnp.einsum("tsh,shp->thp", mixing, x_blk, precision=highest)
        carried = (g_blk == held_segment).astype(jnp.float32)[:, None] * jnp.exp(cum_rate)
        outer_part = (
            jnp.einsum("tn,hpn->thp", c_blk, held_state, precision=highest) * carried[:, :, None]
        )
        outputs = inner_part + outer_part + skip_vals[None, :, None] * x_blk
        last_segment = g_blk[-1]
        tail_w = (
            jnp.exp(cum_rate[-1][None, :] - cum_rate)
            * (g_blk == last_segment).astype(jnp.float32)[:, None]
            * s_blk
        )
        keep_old = (last_segment == held_segment).astype(jnp.float32) * jnp.exp(cum_rate[-1])
        new_state = keep_old[:, None, None] * held_state + jnp.einsum(
            "sh,shp,sn->hpn", tail_w, x_blk, b_blk, precision=highest
        )
        return ((new_state, last_segment), outputs)

    pieces = (
        x_heads.reshape(blocks, BLOCK, head_count, head_dim),
        b_mat.reshape(blocks, BLOCK, state_dim),
        c_mat.reshape(blocks, BLOCK, state_dim),
        rate_vals.reshape(blocks, BLOCK, head_count),
        step_vals.reshape(blocks, BLOCK, head_count),
        segment.reshape(blocks, BLOCK),
    )
    initial = (jnp.zeros((head_count, head_dim, state_dim), jnp.float32), jnp.array(-1, jnp.int32))
    final_carry, outputs = lax.scan(jax.checkpoint(one_block), initial, pieces)
    return (outputs.reshape(length, head_count, head_dim), final_carry[0])


def combine_state(earlier, later):
    return (earlier[0] * later[0], later[0][:, None, None] * earlier[1] + later[1])


def local(
    tokens,
    out_grad,
    lengths,
    routes,
    in_norm,
    in_proj,
    conv_weight,
    conv_bias,
    head_params,
    mixer_norm,
    out_proj,
    ffn_norm,
    router,
    shared_gate_up,
    shared_down,
    expert_gate_up,
    expert_down,
):
    dense_full = (
        *in_one_piece((in_norm, in_proj), SEQ_DP, 0, 1),
        *in_one_piece((conv_weight, conv_bias), SEQ_DP, 0, 1),
        *in_one_piece((mixer_norm, out_proj), SEQ_DP, 0, 1),
        *in_one_piece((ffn_norm, router, shared_gate_up), SEQ_DP, 0, 1),
        lax.all_gather(shared_down, SEQ_DP, axis=0, tiled=True),
    )
    g_in, w_in, w_conv, b_conv, g_mix, w_out, g_ffn, w_router, w_sgu, w_sdown = dense_full
    w_egu, w_edown = gather_together((expert_gate_up, expert_down), "seq", (1, 1))
    rows_dev = tokens.shape[0]
    model_w = tokens.shape[1]
    inner_w = g_mix.shape[0]
    xbc_width = w_conv.shape[0]
    kernel = w_conv.shape[1]
    head_count = head_params.shape[1]
    head_dim = inner_w // head_count
    state_dim = (xbc_width - inner_w) // 2
    top_count = routes.shape[1]
    local_experts = w_egu.shape[0]
    expert_total = local_experts * lax.axis_size(DP)
    capacity = 2 * rows_dev * top_count // expert_total
    seq_ends = jnp.cumsum(lengths[0])
    positions = lax.axis_index("seq") * rows_dev + jnp.arange(
        -(kernel - 1), rows_dev, dtype=jnp.int32
    )
    pad_segment = jnp.sum((positions[:, None] >= seq_ends[None, :]).astype(jnp.int32), axis=1)
    pad_segment = jnp.where(positions >= 0, pad_segment, -1)
    segment = pad_segment[kernel - 1 :]
    prior_segment = pad_segment[kernel - 2]
    block_in = tokens.astype(jnp.float32)
    normed32, in_norm_back = jax.vjp(rms_scale, block_in, g_in.astype(jnp.float32))
    normed = normed32.astype(jnp.bfloat16)
    projected = product(normed, w_in).astype(jnp.bfloat16)
    edge_rows = shifted(
        projected[rows_dev - (kernel - 1) :, inner_w : inner_w + xbc_width], "seq", 1
    )

    def prepare(proj_vals, edge_vals, conv_w, conv_b, heads_p):
        gate_z = proj_vals[:, :inner_w]
        padded = jnp.concatenate([edge_vals, proj_vals[:, inner_w : inner_w + xbc_width]], axis=0)
        conv_out = conv_taps(padded, pad_segment, segment, conv_w, conv_b)
        step_vals = jax.nn.softplus(proj_vals[:, inner_w + xbc_width :] + heads_p[1][None, :])
        rate_vals = -step_vals * jnp.exp(heads_p[0])[None, :]
        return (
            gate_z,
            conv_out[:, :inner_w],
            conv_out[:, inner_w : inner_w + state_dim],
            conv_out[:, inner_w + state_dim :],
            rate_vals,
            step_vals,
        )

    prepared, prepare_back = jax.vjp(
        prepare,
        projected.astype(jnp.float32),
        edge_rows.astype(jnp.float32),
        w_conv.astype(jnp.float32),
        b_conv.astype(jnp.float32),
        head_params.astype(jnp.float32),
    )
    gate_z, x_part, b_mat, c_mat, rate_vals, step_vals = prepared

    def local_scan(x_vals, b_vals, c_vals, r_vals, s_vals, skip_vals):
        outputs, held_state = ssd_blocks(
            x_vals.reshape(rows_dev, head_count, head_dim),
            b_vals,
            c_vals,
            r_vals,
            s_vals,
            skip_vals,
            segment,
        )
        through = (segment[-1] == prior_segment).astype(jnp.float32) * jnp.exp(
            jnp.sum(r_vals, axis=0)
        )
        return (outputs, held_state, through)

    (local_y, held_state, through), scan_back = jax.vjp(
        local_scan, x_part, b_mat, c_mat, rate_vals, step_vals, head_params[2].astype(jnp.float32)
    )
    identity = (jnp.ones((head_count,), jnp.float32), jnp.zeros_like(held_state))
    entering = entering_2((through, held_state), "seq", combine_state, identity)[1]

    def carried_in(c_vals, r_vals, state_in):
        factor = (segment == prior_segment).astype(jnp.float32)[:, None] * jnp.exp(
            jnp.cumsum(r_vals, axis=0)
        )
        return jnp.einsum("tn,hpn->thp", c_vals, state_in, precision=highest) * factor[:, :, None]

    carried_y, carried_back = jax.vjp(carried_in, c_mat, rate_vals, entering)

    def finish(own_y, extra_y, gate_vals, gain_vec):
        gated = (own_y + extra_y).reshape(rows_dev, inner_w) * jax.nn.silu(gate_vals)
        return rms_scale(gated, gain_vec)

    mixer_out32, finish_back = jax.vjp(
        finish, local_y, carried_y, gate_z, g_mix.astype(jnp.float32)
    )
    mixer_out = mixer_out32.astype(jnp.bfloat16)
    residual = block_in + product(mixer_out, w_out)
    ffn_in32, ffn_norm_back = jax.vjp(rms_scale, residual, g_ffn.astype(jnp.float32))
    ffn_in = ffn_in32.astype(jnp.bfloat16)
    logits = product(ffn_in, w_router)
    expert_ids = jnp.arange(expert_total, dtype=jnp.int32)
    choose = (routes[:, :, None] == expert_ids[None, None, :]).astype(jnp.float32)
    chosen = jnp.einsum("tke,te->tk", choose, logits, precision=highest)
    gating = jax.nn.softmax(chosen, axis=-1)
    shared_gu = product(ffn_in, w_sgu)
    shared_act = swish_product(shared_gu).astype(jnp.bfloat16)
    shared_out = product(shared_act, w_sdown)
    route_count = rows_dev * top_count
    flat_routes = routes.reshape(route_count)
    route_hits = (flat_routes[:, None] == expert_ids[None, :]).astype(jnp.int32)
    slot_rank = jnp.sum(route_hits * (jnp.cumsum(route_hits, axis=0) - 1), axis=1)
    slot_index = flat_routes * capacity + slot_rank
    slot_route = (
        jnp.full((expert_total * capacity,), route_count, jnp.int32)
        .at[slot_index]
        .set(jnp.arange(route_count, dtype=jnp.int32))
    )
    ffn_pad = jnp.concatenate([ffn_in, jnp.zeros((1, model_w), jnp.bfloat16)], axis=0)
    outbound = ffn_pad[slot_route // top_count].reshape(expert_total, capacity, model_w)
    arrived = lax.all_to_all(outbound, DP, split_axis=0, concat_axis=0, tiled=True)
    sources = arrived.shape[0] // local_experts
    row_block = arrived.reshape(sources, local_experts, arrived.shape[1], model_w)
    expert_gu = jnp.einsum("secd,edf->secf", row_block, w_egu, preferred_element_type=jnp.float32)
    expert_act = swish_product(expert_gu).astype(jnp.bfloat16)
    expert_out = jnp.einsum(
        "secf,efd->secd", expert_act, w_edown, preferred_element_type=jnp.float32
    ).astype(jnp.bfloat16)
    returned = lax.all_to_all(
        expert_out.reshape(arrived.shape), DP, split_axis=0, concat_axis=0, tiled=True
    )
    returned, arrived, kept_gu = (
        returned,
        arrived,
        expert_gu.reshape(arrived.shape[0], arrived.shape[1], expert_gu.shape[-1]),
    )
    routed_back = returned.reshape(expert_total * capacity, model_w)[slot_index].reshape(
        rows_dev, top_count, model_w
    )
    routed = jnp.sum(gating[:, :, None] * routed_back.astype(jnp.float32), axis=1)
    block_out = (residual + shared_out + routed).astype(jnp.bfloat16)
    w_in_b, w_out_b, w_router_b, w_sgu_b, w_sdown_b = (w_in, w_out, w_router, w_sgu, w_sdown)
    cotangent = out_grad.astype(jnp.float32)
    d_shared_act = product(out_grad, w_sdown_b.T)
    d_sdown = product(shared_act.T, out_grad)
    _, swish_back = jax.vjp(swish_product, shared_gu)
    d_shared_gu = swish_back(d_shared_act)[0].astype(jnp.bfloat16)
    d_sgu = product(ffn_in.T, d_shared_gu)
    d_ffn = product(d_shared_gu, w_sgu_b.T)
    d_gating = jnp.einsum(
        "td,tkd->tk", cotangent, routed_back.astype(jnp.float32), precision=highest
    )
    d_chosen = gating * (d_gating - jnp.sum(gating * d_gating, axis=1, keepdims=True))
    d_logits = jnp.einsum("tk,tke->te", d_chosen, choose, precision=highest)
    d_router = jnp.dot(ffn_in.astype(jnp.float32).T, d_logits, precision=highest)
    d_ffn = d_ffn + jnp.dot(d_logits, w_router_b.astype(jnp.float32).T, precision=highest)
    d_route = (
        (gating[:, :, None] * cotangent[:, None, :])
        .astype(jnp.bfloat16)
        .reshape(route_count, model_w)
    )
    d_pad = jnp.concatenate([d_route, jnp.zeros((1, model_w), jnp.bfloat16)], axis=0)
    d_outbound = d_pad[slot_route].reshape(expert_total, capacity, model_w)
    d_arrived = lax.all_to_all(d_outbound, DP, split_axis=0, concat_axis=0, tiled=True)
    sources = expert_total // local_experts
    block_shape = (sources, local_experts, capacity, model_w)
    d_rows = d_arrived.reshape(block_shape)
    row_block = arrived.reshape(block_shape)
    expert_gu = kept_gu.reshape(sources, local_experts, capacity, kept_gu.shape[-1])
    expert_act32, expert_swish_back = jax.vjp(swish_product, expert_gu)
    expert_act = expert_act32.astype(jnp.bfloat16)
    d_act = jnp.einsum("secd,efd->secf", d_rows, w_edown, preferred_element_type=jnp.float32)
    d_edown = jnp.einsum("secf,secd->efd", expert_act, d_rows, preferred_element_type=jnp.float32)
    d_expert_gu = expert_swish_back(d_act)[0].astype(jnp.bfloat16)
    d_egu = jnp.einsum("secd,secf->edf", row_block, d_expert_gu, preferred_element_type=jnp.float32)
    d_sent = jnp.einsum(
        "secf,edf->secd", d_expert_gu, w_egu, preferred_element_type=jnp.float32
    ).astype(jnp.bfloat16)
    d_returned = lax.all_to_all(
        d_sent.reshape(expert_total, capacity, model_w), DP, split_axis=0, concat_axis=0, tiled=True
    )
    d_routes_back = d_returned.reshape(expert_total * capacity, model_w)[slot_index].reshape(
        rows_dev, top_count, model_w
    )
    d_ffn = d_ffn + jnp.sum(d_routes_back.astype(jnp.float32), axis=1)
    d_residual_norm, d_gffn = ffn_norm_back(d_ffn)
    d_residual = cotangent + d_residual_norm
    d_mixed = d_residual.astype(jnp.bfloat16)
    d_wout = product(mixer_out.T, d_mixed)
    d_mixer_out = product(d_mixed, w_out_b.T)
    d_local_y, d_carried_y, d_gate_z, d_gmix = finish_back(d_mixer_out)
    d_c_in, d_rate_in, d_entering = carried_back(d_carried_y)
    leaving = entering_3((through, d_entering), "seq", combine_state, identity)[1]
    d_through = jnp.sum(leaving * entering, axis=(1, 2))
    d_x_part, d_b_mat, d_c_mat, d_rate, d_step, d_skip = scan_back((d_local_y, leaving, d_through))
    d_proj, d_edge, d_cw, d_cb, d_heads = prepare_back(
        (d_gate_z, d_x_part, d_b_mat, d_c_mat + d_c_in, d_rate + d_rate_in, d_step)
    )
    d_heads = d_heads.at[2].add(d_skip)
    d_tail = shifted(d_edge.astype(jnp.bfloat16), "seq", -1).astype(d_edge.dtype)
    d_proj = d_proj.at[rows_dev - (kernel - 1) :, inner_w : inner_w + xbc_width].add(d_tail)
    d_proj_low = d_proj.astype(jnp.bfloat16)
    d_win = product(normed.T, d_proj_low)
    d_normed = product(d_proj_low, w_in_b.T)
    d_block_norm, d_gin = in_norm_back(d_normed)
    token_grad = (d_residual + d_block_norm).astype(jnp.bfloat16)
    grads_dense = one_scatter(
        (d_gin, d_win, d_cw, d_cb, d_gmix, d_wout, d_gffn, d_router, d_sgu, d_sdown),
        SEQ_DP,
        (0, 0, 0, 0, 0, 0, 0, 0, 0, 0),
    )
    head_grad = over_axes(d_heads, SEQ_DP)
    d_egu_part, d_edown_part = (
        summed_on_arrival(d_egu.astype(jnp.bfloat16), "seq", 1),
        summed_on_arrival(d_edown.astype(jnp.bfloat16), "seq", 1),
    )
    return (
        block_out,
        token_grad,
        grads_dense[0],
        grads_dense[1],
        grads_dense[2],
        grads_dense[3],
        head_grad,
        grads_dense[4],
        grads_dense[5],
        grads_dense[6],
        grads_dense[7],
        grads_dense[8],
        grads_dense[9],
        d_egu_part,
        d_edown_part,
    )


def solution(mesh):
    finer = Mesh(mesh.devices.reshape(mesh.shape["seq"], 4, 4, 4), ("seq", "dp_0", "dp_1", "dp_2"))
    placed = (
        P(DP_SEQ, None),
        P(DP_SEQ, None),
        P(DP, None),
        P(DP_SEQ, None),
        P(SEQ_DP),
        P(SEQ_DP, None),
        P(SEQ_DP, None),
        P(SEQ_DP),
        P(),
        P(SEQ_DP),
        P(SEQ_DP, None),
        P(SEQ_DP),
        P(SEQ_DP, None),
        P(SEQ_DP, None),
        P(SEQ_DP, None),
        P(DP, "seq", None),
        P(DP, "seq", None),
    )
    return jax.shard_map(
        local,
        mesh=finer,
        in_specs=placed,
        out_specs=(
            P(DP_SEQ, None),
            P(DP_SEQ, None),
            P(SEQ_DP),
            P(SEQ_DP, None),
            P(SEQ_DP, None),
            P(SEQ_DP),
            P(),
            P(SEQ_DP),
            P(SEQ_DP, None),
            P(SEQ_DP),
            P(SEQ_DP, None),
            P(SEQ_DP, None),
            P(SEQ_DP, None),
            P(DP, "seq", None),
            P(DP, "seq", None),
        ),
        check_vma=False,
    )
```

profile of v0, /device:TPU:32, one launch (start us, length us, event | category | flops | bytes accessed | tf_op | source)
XLA Modules:
  0.0 2394.4 jit_solution(10038718027799470139)
XLA Ops:
  19.2 307.1 %all-gather.4 = bf16[128,26,5]{1,2,0:T(8,128)(2,1)S(1)} all-gather(bf16[1,26,5]{1,2,0:T(8,128)(2,1)S(1)} %maximum_bitcast_fusion.1), channel_id=1, replica_groups=mesh['seq'=2,'dp_0'=4,'dp_1'=4,'dp_2'=4] {'seq','dp_0','dp_1','dp_2'}, dimensions={0}, use_global_device_ids=true | all-gather | bytes 33540 | tf_op jit(solution)/shard_map/all_gather | solution.py:20
  330.0 29.4 %reshape.822 = bf16[1536,6449]{1,0:T(8,128)(2,1)} reshape(bf16[128,12,6449]{2,1,0:T(8,128)(2,1)} %all-gather.25.cloned.1.call-done) | data formatting | bytes 39622656
  360.6 10.8 fusion.203
  411.9 12.2 reshape.824
  440.2 8.3 fusion.37
  479.3 19.5 all-to-all-start
  518.2 45.3 %all-to-all-done = bf16[64,24,1536]{2,1,0:T(8,128)(2,1)} async-done(((bf16[64,24,1536]{2,1,0:T(8,128)(2,1)}), bf16[64,24,1536]{2,1,0:T(8,128)(2,1)}, u32[]{:S(2)}, u32[]{:S(2)}) %all-to-all-start) | async-done | bytes 4718624 | tf_op jit(solution)/shard_map/all_to_all | solution.py:350
  582.8 11.6 all-to-all-start.1
  607.3 48.2 %all-to-all-done.1 = bf16[64,24,1536]{2,1,0:T(8,128)(2,1)} async-done(((bf16[64,24,1536]{2,1,0:T(8,128)(2,1)}), bf16[64,24,1536]{2,1,0:T(8,128)(2,1)}, u32[]{:S(2)}, u32[]{:S(2)}) %all-to-all-start.1) | async-done | bytes 4718624 | tf_op jit(solution)/shard_map/all_to_all | solution.py:358
  655.5 8.8 gather_fusion.1
  688.6 57.6 %all-to-all-done.2 = bf16[64,24,1536]{2,1,0:T(8,128)(2,1)} async-done(((bf16[64,24,1536]{2,1,0:T(8,128)(2,1)}), bf16[64,24,1536]{2,1,0:T(8,128)(2,1)}, u32[]{:S(2)}, u32[]{:S(2)}) %all-to-all-start.2) | async-done | bytes 4718624 | tf_op jit(solution)/shard_map/all_to_all | solution.py:393
  746.1 8.4 bitcast_multiply_fusion.3
  781.9 52.2 %all-gather.17.cloned.1.call-done = bf16[1024,1536]{1,0:T(8,128)(2,1)} async-done(((bf16[8,1536]{1,0:T(8,128)(2,1)}), bf16[1024,1536]{1,0:T(8,128)(2,1)}) %all-gather.17.cloned.1.call-update) | async-done | bytes 3145744 | tf_op jit(solution)/shard_map/all_gather | solution.py:233
  844.8 14.3 reshape_reshape.22
  877.9 8.8 gather_fusion.3
  900.7 8.3 multiply_reduce_fusion.8
  927.1 10.8 fusion.148
  938.0 19.8 reshape_reshape.20
  979.0 9.7 fusion.62
  1036.5 13.1 fusion.121
  1049.6 15.6 fusion.117
  1065.3 39.5 %reshape_reshape.18 = f32[128,77376]{1,0:T(8,128)} reshape(f32[1536,6448]{1,0:T(8,128)} %fusion.117) | data formatting | bytes 79233024 | tf_op jit(solution)/shard_map/reshape;reshape | solution.py:105
  1106.3 112.0 %dynamic-update-slice.7 = f32[128,152050]{1,0:T(8,128)} dynamic-update-slice(f32[128,152050]{1,0:T(8,128)} %dynamic-update-slice.6, f32[128,77376]{1,0:T(8,128)} %reshape_reshape.18, s32[]{} %constant.349, s32[]{} %constant.350) | dynamic-update-slice | bytes 79233024
  1223.5 56.3 %dynamic-update-slice.11 = f32[128,152050]{1,0:T(8,128)} dynamic-update-slice(f32[128,152050]{1,0:T(8,128)} %dynamic-update-slice.10, f32[128,36864]{1,0:T(8,128)} %reshape_reshape.20, s32[]{} %constant.349, s32[]{} %constant.354) | dynamic-update-slice | bytes 37748740
  1285.1 45.2 %dynamic-update-slice.14 = f32[128,152050]{1,0:T(8,128)} dynamic-update-slice(f32[128,152050]{1,0:T(8,128)} %dynamic-update-slice.13, f32[128,24576]{1,0:T(8,128)} %reshape_reshape.22, s32[]{} %constant.349, s32[]{} %constant.357) | dynamic-update-slice | bytes 25165828
  1330.3 22.9 dynamic-update-slice.15
  1353.2 51.0 %pad.100 = f32[128,152576]{1,0:T(8,128)} pad(f32[128,152050]{1,0:T(8,128)} %dynamic-update-slice.15, f32[]{:T(128)} %constant.240.clone.1), padding=0_0x0_526 | pad | bytes 155968512 | tf_op jit(solution)/shard_map/jit(_pad)/pad | solution.py:107
  1404.2 85.0 %reshape.750 = f32[152576,128]{1,0:T(8,128)} reshape(f32[128,152576]{1,0:T(8,128)} %pad.100) | data formatting | bytes 156237824 | tf_op jit(solution)/shard_map/reshape | solution.py:107
  1505.2 9.7 bitcast_convert_fusion.2
  1530.6 20.2 psum.29
  1558.5 784.9 %psum.31 = f32[3,48]{1,0:T(4,128)} all-reduce(f32[3,48]{1,0:T(4,128)S(1)} %psum.30), channel_id=1, replica_groups=mesh['seq'=2,'dp_0'=4,'dp_1'=4,'dp_2'=4] {'dp_2'}, use_global_device_ids=true, to_apply=%region_50.51 | all-reduce | flops 144 | bytes 1152 | tf_op jit(solution)/shard_map/psum | solution.py:118
  2356.1 26.9 %slice.264 = f32[38144,4]{1,0:T(8,128)} reshape(f32[1192,128]{1,0:T(8,128)S(1)} %copy-done.40) | data formatting | bytes 1220608 | tf_op jit(solution)/shard_map/slice | solution.py:111
  (568 shorter events, 408.2 us)
Async XLA Ops:
  7.2 322.8 %all-gather.25.cloned.1.call-start = ((), (), s32[]{:S(2)}) async-start(), calls=%async_computation.12 | async-start | bytes 26947584 | tf_op jit(solution)/shard_map/all_gather | solution.py:20
  9.9 402.1 %all-gather.27.cloned.1.call-start = ((), (), s32[]{:S(2)}) async-start(), calls=%async_computation.13 | async-start | bytes 8982528 | tf_op jit(solution)/shard_map/all_gather | solution.py:20
  12.3 413.6 %all-gather.15.cloned.1.call-start = ((), (), s32[]{:S(2)}) async-start(), calls=%async_computation.7 | async-start | bytes 10303488 | tf_op jit(solution)/shard_map/all_gather | solution.py:20
  14.7 433.8 %all-gather.19.cloned.1.call-start = ((), (), s32[]{:S(2)}) async-start(), calls=%async_computation.9 | async-start | bytes 2359296 | tf_op jit(solution)/shard_map/all_gather | solution.py:53
  17.5 309.0 %copy-start.139 = (bf16[3,48]{1,0:T(4,128)(2,1)S(1)}, bf16[3,48]{1,0:T(4,128)(2,1)}, u32[]{:S(2)}) copy-start(bf16[3,48]{1,0:T(4,128)(2,1)} %param.33) | copy-start | bytes 868
  17.5 309.0 %copy-start.148 = (s32[1,4]{1,0:T(1,128)S(1)}, s32[1,4]{1,0:T(1,128)}, u32[]{:S(2)}) copy-start(s32[1,4]{1,0:T(1,128)} %param.27) | copy-start | bytes 52
  17.6 310.8 %copy-start.28 = (bf16[128,1536]{1,0:T(8,128)(2,1)S(1)}, bf16[128,1536]{1,0:T(8,128)(2,1)}, u32[]{:S(2)}) copy-start(bf16[128,1536]{1,0:T(8,128)(2,1)} %param.25) | copy-start | bytes 1179652
  371.5 5.5 collective-permute-start
  381.2 74.7 %copy-start.5 = (f32[128,3072]{0,1:T(8,128)}, f32[128,3072]{0,1:T(8,128)S(1)}, u32[]{:S(2)}) copy-start(f32[128,3072]{0,1:T(8,128)S(1)} %copy.314) | copy-start | bytes 4718596
  384.7 114.2 %all-gather.21.cloned.1.call-start = ((), (), s32[]{:S(2)}) async-start(), calls=%async_computation.10 | async-start | bytes 7077888 | tf_op jit(solution)/shard_map/all_gather | solution.py:36
  479.3 84.2 %all-to-all-start = ((bf16[64,24,1536]{2,1,0:T(8,128)(2,1)}), bf16[64,24,1536]{2,1,0:T(8,128)(2,1)}, u32[]{:S(2)}, u32[]{:S(2)}) async-start(bf16[64,24,1536]{2,1,0:T(8,128)(2,1)} %bitcast.245), calls=%async_computation | async-start | bytes 9437184 | tf_op jit(solution)/shard_map/all_to_all | solution.py:350
  518.2 52.8 %copy-start.36 = (bf16[1536,1024,1]{1,0,2:T(8,128)(2,1)}, bf16[1536,1024,1]{1,0,2:T(8,128)(2,1)S(1)}, u32[]{:S(2)}) copy-start(bf16[1536,1024,1]{1,0,2:T(8,128)(2,1)S(1)} %reshape.835) | copy-start | bytes 9437188
  582.8 72.7 %all-to-all-start.1 = ((bf16[64,24,1536]{2,1,0:T(8,128)(2,1)}), bf16[64,24,1536]{2,1,0:T(8,128)(2,1)}, u32[]{:S(2)}, u32[]{:S(2)}) async-start(bf16[64,24,1536]{2,1,0:T(8,128)(2,1)} %copy.330), calls=%async_computation.1 | async-start | bytes 9437184 | tf_op jit(solution)/shard_map/all_to_all | solution.py:358
  606.5 49.1 %copy-start.60 = (f32[128,1,6]{2,1,0:T(1,128)}, f32[128,1,6]{2,1,0:T(1,128)S(1)}, u32[]{:S(2)}) copy-start(f32[128,1,6]{2,1,0:T(1,128)S(1)} %fusion.139) | copy-start | bytes 9220
  606.6 48.9 %copy-start.122 = (f32[128]{0:T(128)}, f32[128]{0:T(128)S(1)}, u32[]{:S(2)}) copy-start(f32[128]{0:T(128)S(1)} %reduce_max.9) | copy-start | bytes 1540
  671.9 204.6 %copy-start.52 = (f32[128,6]{1,0:T(8,128)}, f32[128,6]{1,0:T(8,128)S(1)}, u32[]{:S(2)}) copy-start(f32[128,6]{1,0:T(8,128)S(1)} %get-tuple-element.566) | copy-start | bytes 9220
  681.6 64.5 %copy-start.46 = (bf16[512,1536,1]{1,0,2:T(8,128)(2,1)S(1)}, bf16[512,1536,1]{1,0,2:T(8,128)(2,1)}, u32[]{:S(2)}) copy-start(bf16[512,1536,1]{1,0,2:T(8,128)(2,1)} %reshape.836) | copy-start | bytes 4718596
  681.6 64.5 %all-to-all-start.2 = ((bf16[64,24,1536]{2,1,0:T(8,128)(2,1)}), bf16[64,24,1536]{2,1,0:T(8,128)(2,1)}, u32[]{:S(2)}, u32[]{:S(2)}) async-start(bf16[64,24,1536]{2,1,0:T(8,128)(2,1)} %bitcast.246), calls=%async_computation.2 | async-start | bytes 9437184 | tf_op jit(solution)/shard_map/all_to_all | solution.py:393
  688.0 146.2 %all-gather.17.cloned.1.call-start = ((), (), s32[]{:S(2)}) async-start(), calls=%async_computation.8 | async-start | bytes 3170304 | tf_op jit(solution)/shard_map/all_gather | solution.py:233
  766.4 111.5 %all-to-all-start.3 = ((bf16[64,24,1536]{2,1,0:T(8,128)(2,1)}), bf16[64,24,1536]{2,1,0:T(8,128)(2,1)}, u32[]{:S(2)}, u32[]{:S(2)}) async-start(bf16[64,24,1536]{2,1,0:T(8,128)(2,1)} %copy.332), calls=%async_computation.3 | async-start | bytes 9437184 | tf_op jit(solution)/shard_map/all_to_all | solution.py:408
  773.7 188.9 %all-gather.23.cloned.1.call-start = ((), (), s32[]{:S(2)}) async-start(), calls=%async_computation.11 | async-start | bytes 2359296 | tf_op jit(solution)/shard_map/all_gather | solution.py:76
  775.9 58.2 %copy-start.32 = (bf16[128,1536]{1,0:T(8,128)(2,1)S(1)}, bf16[128,1536]{1,0:T(8,128)(2,1)}, u32[]{:S(2)}) copy-start(bf16[128,1536]{1,0:T(8,128)(2,1)} %param.26) | copy-start | bytes 1179652
  918.2 1428.3 %reduce-scatter.5.cloned.1.call-start = ((), (), s32[]{:S(2)}) async-start(), calls=%async_computation.14 | async-start | bytes 78729216
  1025.5 8.9 collective-permute-start.1
  1106.3 115.4 %copy-start.73 = (f32[128,24]{1,0:T(8,128)S(1)}, f32[128,24]{1,0:T(8,128)}, u32[]{:S(2)}) copy-start(f32[128,24]{1,0:T(8,128)} %reshape.748) | copy-start | bytes 36868
  1223.5 56.3 %copy-start.74 = (f32[128,12]{1,0:T(8,128)S(1)}, f32[128,12]{1,0:T(8,128)}, u32[]{:S(2)}) copy-start(f32[128,12]{1,0:T(8,128)} %reshape.749) | copy-start | bytes 18436
  1223.5 58.0 %copy-start.47 = (f32[128,768]{1,0:T(8,128)S(1)}, f32[128,768]{1,0:T(8,128)}, u32[]{:S(2)}) copy-start(f32[128,768]{1,0:T(8,128)} %reshape_reshape.21) | copy-start | bytes 1179652
  1501.5 13.4 all-to-all-start.5
  1516.2 8.8 all-to-all-start.4
  1523.1 821.1 %copy-start.30 = (bf16[128,1536]{1,0:T(8,128)(2,1)S(1)}, bf16[128,1536]{1,0:T(8,128)(2,1)}, u32[]{:S(2)}) copy-start(bf16[128,1536]{1,0:T(8,128)(2,1)} %param.25) | copy-start | bytes 1179652
  1523.1 821.1 %copy-start.78 = (f32[1536]{0:T(1024)S(1)}, f32[1536]{0:T(1024)}, u32[]{:S(2)}) copy-start(f32[1536]{0:T(1024)} %copy-done.76) | copy-start | bytes 18436
  1523.1 821.1 %copy-start.110 = (f32[128]{0:T(128)S(1)}, f32[128]{0:T(128)}, u32[]{:S(2)}) copy-start(f32[128]{0:T(128)} %copy-done.108) | copy-start | bytes 1540
  (137 other events, 1195.4 us)
Sparse Core Ops, SparseCore 0:
  11.6 97.1 all-gather.24
  112.3 69.1 all-gather.26
  185.1 68.9 all-gather.14
  384.8 19.6 all-gather.18
  406.6 18.4 all-gather.20
  691.6 142.5 all-gather.16
  918.3 13.0 all-gather.22
  1489.5 853.0 reduce-scatter.4
where the time goes:
time: 2430 us; the launch traced here: 2390 us
  blocking collectives  1120 us (46%)
  local copies, waits for them, and re-layouts  699 us (29%)
  waiting for transfers between devices  206 us (8%)
  matrix products  203 us (8%)
  other arithmetic  85.1 us (4%)
  starting transfers between devices  55.7 us (2%)
    psum x4, blocking collectives, over_axes(): value = lax.psum(value, axis)  815 us
    all_gather x1, blocking collectives, in_one_piece(): filled, at, done = (lax.all_gather(both, axis, axis=dim, tiled=True), 0, [])  307 us
    unnamed x322, local copies, waits for them, and re-layouts  287 us
    dot_general x13, matrix products, product(): return jnp.dot(left_op, right_op, preferred_element_type=jnp.float32)  94.4 us
    another operation x6, local copies, waits for them, and re-layouts, one_scatter(): lines = jnp.concatenate([b.reshape(peers, -1) for b in pieces], axis=1)  85.1 us
    reshape x1, local copies, waits for them, and re-layouts, one_scatter(): jnp.pad(lines, ((0, 0), (0, width * 128 - lines.shape[1]))).reshape(-1, 128)  85 us
    all_to_all x1, waiting for transfers between devices, local(): lax.all_to_all(d_outbound, DP, split_axis=0, concat_axis=0, tiled=True)  57.6 us
    all_gather x1, waiting for transfers between devices, local(): lax.all_gather(shared_down, SEQ_DP, axis=0, tiled=True)  52.2 us
  transfers between devices with their start and end apart: 16, of which 5 were waited for; matrix products, arithmetic and copies ran while one was open for 14% of the time, Pallas kernels for 0%

commit v1 on v0

v1 whole, which is shorter than its diff:
```python
import functools

import jax
import jax.numpy as jnp
import numpy as np
from jax import lax
from jax.experimental import pallas as pl
from jax.experimental.pallas import tpu as pltpu
from jax.sharding import Mesh
from jax.sharding import PartitionSpec as P

DP = ("z", "x", "y")
ALL = ("seq", "z", "x", "y")
DP_SEQ = ("z", "x", "y", "seq")
ORDER = (("z", "x", "y"), ("x", "y", "z"), ("y", "z", "x"))
REM = (("z", "x"), ("y", "x"), ("y", "z"))
MESH_ID = pl.DeviceIdType.MESH
EPS = 1e-05
f32 = jnp.float32
bf16 = jnp.bfloat16

ROWS_FIRST = (("y", "s", "z", "x"), "rows")
CHANNELS = (("y", "z", "x", "s"), "cols")
SPECS = (ROWS_FIRST, ROWS_FIRST, CHANNELS, CHANNELS)


def dot(a, b, dims=((1,), (0,))):
    return lax.dot_general(a, b, (dims, ((), ())), preferred_element_type=f32)


def neighbours():
    pos = {a: lax.axis_index(a) for a in DP}
    right = {a: lax.rem(pos[a] + 1, 4) for a in DP}
    left = {a: lax.rem(pos[a] + 3, 4) for a in DP}
    opp = {a: lax.rem(pos[a] + 2, 4) for a in DP}
    return pos, right, left, opp


def greet(right, left):
    barrier = pltpu.get_barrier_semaphore()
    for a in DP:
        for n in (right[a], left[a]):
            pl.semaphore_signal(barrier, inc=1, device_id={a: n}, device_id_type=MESH_ID)
    pl.semaphore_wait(barrier, 6)


def third(shape, split, a):
    rows, cols = shape[-2:]
    if split == "rows":
        return (pl.ds(rows // 3 * a, rows // 3), slice(None))
    return (slice(None), pl.ds(cols // 3 * a, cols // 3))


def third_shape(shape, split):
    rows, cols = shape[-2:]
    return (rows // 3, cols) if split == "rows" else (rows, cols // 3)


def region(ref, spec, free, fixed, a, s=None):
    order, split = spec
    ix = []
    for d in order:
        if d == "s":
            ix.append(slice(None) if s is None else s)
        else:
            ix.append(slice(None) if d in free else fixed[d])
    return ref.at[tuple(ix) + third(ref.shape, split, a)]


def gather_kernel(specs, *refs):
    n = len(specs)
    ins, outs, (send, recv, loc) = refs[:n], refs[n : 2 * n], refs[2 * n :]
    pos, right, left, opp = neighbours()
    own = []
    for i in range(n):
        ix = tuple(slice(None) if d == "s" else pos[d] for d in specs[i][0])
        c = pltpu.make_async_copy(ins[i], outs[i].at[ix], loc.at[i])
        c.start()
        own.append(c)
    greet(right, left)
    sends = []

    def remote(i, st, a, k, src, dst, ax, to):
        c = pltpu.make_async_remote_copy(
            src_ref=src,
            dst_ref=dst,
            send_sem=send.at[i, st, a, k],
            recv_sem=recv.at[i, st, a, k],
            device_id={ax: to},
            device_id_type=MESH_ID,
        )
        c.start()
        sends.append(c)
        return c

    for st in range(3):
        first, later = {}, []
        for i in range(n):
            for a in range(3):
                ax, free = ORDER[a][st], ORDER[a][:st]
                dst = region(outs[i], specs[i], free, pos, a)
                src = dst
                if st == 0:
                    src = ins[i].at[(slice(None),) + third(ins[i].shape, specs[i][1], a)]
                for d, to in enumerate((right[ax], left[ax])):
                    first[i, a, d] = remote(i, st, a, d, src, dst, ax, to)
        for i in range(n):
            for a in range(3):
                ax, free = ORDER[a][st], ORDER[a][:st]
                for d, (to, frm) in enumerate(((right[ax], left[ax]), (left[ax], right[ax]))):
                    first[i, a, d].wait_recv()
                    r = region(outs[i], specs[i], free, {**pos, ax: frm}, a, s=d)
                    later.append(remote(i, st, a, 2 + d, r, r, ax, to))
        for c in later:
            c.wait_recv()
        if st == 0:
            for c in own:
                c.wait()
    for c in sends:
        c.wait_send()


def gather(arrays, specs, collective_id):
    n = len(arrays)
    sizes = {"y": 4, "z": 4, "x": 4, "s": 2}
    outs = [
        jax.ShapeDtypeStruct(tuple(sizes[d] for d in spec[0]) + v.shape[1:], v.dtype)
        for v, spec in zip(arrays, specs)
    ]
    moved = sum(int(np.prod(o.shape)) for o in outs) * 2
    return pl.pallas_call(
        functools.partial(gather_kernel, specs),
        out_shape=outs,
        in_specs=[pl.BlockSpec(memory_space=pl.ANY)] * n,
        out_specs=[pl.BlockSpec(memory_space=pl.ANY)] * n,
        scratch_shapes=[
            pltpu.SemaphoreType.DMA((n, 3, 3, 4)),
            pltpu.SemaphoreType.DMA((n, 3, 3, 4)),
            pltpu.SemaphoreType.DMA((n,)),
        ],
        compiler_params=pltpu.CompilerParams(collective_id=collective_id, has_side_effects=True),
        cost_estimate=pl.CostEstimate(flops=0, bytes_accessed=2 * moved, transcendentals=0),
        name="gather_weights",
    )(*arrays)


def each(lead, fn):
    if not lead:
        fn((Ellipsis,))
        return

    @pl.loop(0, int(np.prod(lead)))
    def _(i):
        ix = []
        for d in reversed(lead):
            ix.append(lax.rem(i, d))
            i = lax.div(i, d)
        fn(tuple(reversed(ix)))


def scatter_kernel(specs, *refs):
    n = len(specs)
    gs, outs = refs[:n], refs[n : 2 * n]
    held, got = refs[2 * n : 3 * n], [refs[3 * n + 3 * i : 3 * n + 3 * i + 3] for i in range(n)]
    send, recv, loc = refs[6 * n :]
    pos, right, left, opp = neighbours()

    def source(i, st, a, idx, s):
        ax = ORDER[a][2 - st]
        if st == 0:
            return region(gs[i], specs[i], [d for d in DP if d != ax], {ax: idx}, a, s)
        part = held[i].at[a, 2 + s]
        if st == 1:
            return part.at[:, idx] if REM[a][1] == ax else part.at[idx]
        me = pos[ORDER[a][1]]
        return part.at[me, idx] if REM[a][1] == ax else part.at[idx, me]

    local = {}
    for i in range(n):
        for a in range(3):
            ax = ORDER[a][2]
            for k, (idx, s) in enumerate(((right[ax], 0), (left[ax], 1), (pos[ax], 0), (pos[ax], 1))):
                c = pltpu.make_async_copy(source(i, 0, a, idx, s), held[i].at[a, k], loc.at[i, a, k])
                c.start()
                local[i, a, k] = c
    greet(right, left)
    sends = []

    def remote(i, st, a, k, src, ax, to):
        c = pltpu.make_async_remote_copy(
            src_ref=src,
            dst_ref=got[i][st].at[a, k],
            send_sem=send.at[i, st, a, k],
            recv_sem=recv.at[i, st, a, k],
            device_id={ax: to},
            device_id_type=MESH_ID,
        )
        c.start()
        sends.append(c)
        return c

    every = [(i, a) for i in range(n) for a in range(3)]
    for st in range(3):
        lead = ((4, 4), (4,), ())[st]
        cp = {}
        for i, a in every:
            ax = ORDER[a][2 - st]
            cp[i, a, 0] = remote(i, st, a, 0, source(i, st, a, opp[ax], 0), ax, right[ax])
            cp[i, a, 1] = remote(i, st, a, 1, source(i, st, a, opp[ax], 1), ax, left[ax])
        for i, a in every:
            ax = ORDER[a][2 - st]
            cp[i, a, 2] = remote(i, st, a, 2, source(i, st, a, right[ax], 1), ax, right[ax])
            cp[i, a, 3] = remote(i, st, a, 3, source(i, st, a, left[ax], 0), ax, left[ax])
        for i, a in every:
            ax = ORDER[a][2 - st]
            for d, to in enumerate((right[ax], left[ax])):
                cp[i, a, d].wait_recv()
                if st == 0:
                    local[i, a, d].wait()
                    acc = held[i].at[a, d]
                else:
                    acc = source(i, st, a, to, d)
                more = got[i][st].at[a, d]

                def add(ix, acc=acc, more=more):
                    acc[ix] = (acc[ix].astype(f32) + more[ix].astype(f32)).astype(acc.dtype)

                each(lead, add)
                cp[i, a, 4 + d] = remote(i, st, a, 4 + d, acc, ax, to)
        for i, a in every:
            ax = ORDER[a][2 - st]
            if st == 0:
                local[i, a, 2].wait()
                local[i, a, 3].wait()
            for s, (p, q) in enumerate(((4, 3), (2, 5))):
                cp[i, a, p].wait_recv()
                cp[i, a, q].wait_recv()
                acc = held[i].at[a, 2 + s] if st == 0 else source(i, st, a, pos[ax], s)
                one, two = got[i][st].at[a, p], got[i][st].at[a, q]
                if st == 2:
                    ix = (s,) + third(outs[i].shape, specs[i][1], a)
                    outs[i][ix] = acc[...].astype(f32) + one[...].astype(f32) + two[...].astype(f32)
                else:

                    def finish(ix, acc=acc, one=one, two=two):
                        total = acc[ix].astype(f32) + one[ix].astype(f32) + two[ix].astype(f32)
                        acc[ix] = total.astype(acc.dtype)

                    each(lead, finish)
    for c in sends:
        c.wait_send()


def scatter(arrays, specs, collective_id):
    n = len(arrays)
    outs = [jax.ShapeDtypeStruct((2,) + v.shape[4:], f32) for v in arrays]
    pieces = [third_shape(v.shape, spec[1]) for v, spec in zip(arrays, specs)]
    moved = sum(int(np.prod(v.shape)) for v in arrays) * 2
    return pl.pallas_call(
        functools.partial(scatter_kernel, specs),
        out_shape=outs,
        in_specs=[pl.BlockSpec(memory_space=pl.ANY)] * n,
        out_specs=[pl.BlockSpec(memory_space=pltpu.VMEM)] * n,
        scratch_shapes=[pltpu.VMEM((3, 4, 4, 4) + p, bf16) for p in pieces]
        + [pltpu.VMEM((3, 6) + lead + p, bf16) for p in pieces for lead in ((4, 4), (4,), ())]
        + [
            pltpu.SemaphoreType.DMA((n, 3, 3, 6)),
            pltpu.SemaphoreType.DMA((n, 3, 3, 6)),
            pltpu.SemaphoreType.DMA((n, 3, 4)),
        ],
        compiler_params=pltpu.CompilerParams(
            collective_id=collective_id, has_side_effects=True, vmem_limit_bytes=56 * 2**20
        ),
        cost_estimate=pl.CostEstimate(flops=0, bytes_accessed=2 * moved, transcendentals=0),
        name="scatter_grads",
    )(*arrays)


def swap(v):
    return lax.ppermute(v, "seq", [(0, 1), (1, 0)])


def both_halves(own, other, s):
    first = jnp.where(s == 0, own, other)
    second = jnp.where(s == 0, other, own)
    return jnp.concatenate([first, second], axis=0)


def halves(v, s):
    rows = v.shape[0] // 2
    return (
        lax.dynamic_slice_in_dim(v, s * rows, rows, 0),
        lax.dynamic_slice_in_dim(v, (1 - s) * rows, rows, 0),
    )


def hi_lo(v):
    hi = v.astype(bf16)
    return hi, (v - hi.astype(f32)).astype(bf16)


def rms(v):
    return lax.rsqrt(jnp.mean(v * v, axis=-1, keepdims=True) + EPS)


def silu_grad(v):
    sig = jax.nn.sigmoid(v)
    return sig * (1.0 + v * (1.0 - sig))


def shift_down(v, d):
    return jnp.pad(v, [(0, 0)] * (v.ndim - 2) + [(d, 0), (0, 0)])[..., : v.shape[-2], :] if d else v


def shift_up(v, d):
    return jnp.pad(v, [(0, 0)] * (v.ndim - 2) + [(0, d), (0, 0)])[..., d:, :] if d else v


def conv_pre(v, same, w, b):
    total = b
    for k in range(4):
        d = 3 - k
        total = total + w[k] * (shift_down(v, d) * same[d])
    return total


def conv_back(d_pre, v, same, w):
    d_w = [jnp.sum(d_pre * (shift_down(v, 3 - k) * same[3 - k]), axis=-2) for k in range(4)]
    d_b = jnp.sum(d_pre, axis=-2)
    d_v = 0.0
    for k in range(4):
        d = 3 - k
        d_v = d_v + w[k] * shift_up(d_pre * same[d], d)
    return d_v, jnp.stack(d_w + [d_b], axis=0)


def local(
    tokens,
    out_grad,
    lengths,
    routes,
    in_norm,
    in_proj,
    conv_weight,
    conv_bias,
    head_params,
    mixer_norm,
    out_proj,
    ffn_norm,
    router,
    shared_gate_up,
    shared_down,
    expert_gate_up,
    expert_down,
):
    s = lax.axis_index("seq")
    dp = lax.axis_index(DP)
    device = s * 64 + dp
    experts, slots = 64, 24
    n_slots = experts * slots

    pieces = []
    for c in range(2):
        for j in range(4):
            at = c * 1536 + j * 384
            misc = jnp.concatenate(
                [
                    in_proj[:, 6144 + j * 64 : 6208 + j * 64],
                    router[:, j * 16 : j * 16 + 16],
                    in_proj[:, 6400 + c * 24 + j * 6 : 6406 + c * 24 + j * 6],
                    jnp.zeros((12, 42), bf16),
                ],
                axis=1,
            )
            up = 1024 + c * 512 + j * 128
            pieces.append(
                jnp.concatenate(
                    [
                        in_proj[:, at : at + 384],
                        in_proj[:, 3072 + at : 3456 + at],
                        misc,
                        shared_gate_up[:, up - 1024 : up - 896],
                        shared_gate_up[:, up : up + 128],
                    ],
                    axis=1,
                )
            )
    rows_in = lax.all_to_all(jnp.stack(pieces), ("seq", "y"), 0, 0, tiled=True).reshape(2, 48, 1152)
    out_rows = jnp.concatenate(
        [out_proj.reshape(24, 4, 384), shared_down.reshape(8, 4, 384)], axis=0
    ).transpose(1, 0, 2)
    out_rows = lax.all_to_all(out_rows, "y", 0, 0, tiled=True)
    vec = jnp.concatenate(
        [
            in_norm,
            ffn_norm,
            mixer_norm,
            conv_weight.T.reshape(-1),
            conv_bias,
            jnp.zeros((78,), bf16),
        ]
    )
    vecs = lax.all_gather(vec[None], ALL, axis=0, tiled=True)
    other_tokens = swap(tokens)
    other_grad = swap(out_grad)
    other_gate_up = swap(expert_gate_up[0])
    other_down = swap(expert_down[0])

    w_in, w_sgu, w_out, w_sdown = gather(
        (
            rows_in[:, :, :896],
            rows_in[:, :, 896:],
            out_rows[:, :24].reshape(2, 48, 384),
            out_rows[:, 24:].reshape(2, 16, 384),
        ),
        SPECS,
        1,
    )
    w_in = w_in.reshape(4, 1536, 896)
    w_sgu = w_sgu.reshape(4, 1536, 256)
    w_out = w_out.reshape(4, 1536, 384)
    w_sdown = w_sdown.reshape(4, 512, 384)

    vecs = vecs.astype(f32)
    g_in = vecs[:, :12].reshape(1536)
    g_ffn = vecs[:, 12:24].reshape(1536)
    g_mix = lax.dynamic_slice_in_dim(vecs[:, 24:48].reshape(3072), s * 1536, 1536)
    conv = vecs[:, 48:178].reshape(128, 5, 26).transpose(1, 0, 2).reshape(5, 3328)
    conv_x = lax.dynamic_slice_in_dim(conv[:, :3072], s * 1536, 1536, 1).reshape(5, 4, 1, 384)
    conv_bc = conv[:, 3072:].reshape(5, 4, 1, 64)
    heads = lax.dynamic_slice_in_dim(head_params.astype(f32), s * 24, 24, 1)
    w_eg = both_halves(expert_gate_up[0], other_gate_up, s)
    w_ed = both_halves(expert_down[0], other_down, s)

    ids = jnp.arange(experts, dtype=jnp.int32)
    named = jnp.sum((routes[:, :, None] == ids).astype(f32), axis=1)
    t128 = jnp.arange(128)
    before = (t128[:, None] > t128[None, :]).astype(bf16)
    rank = dot(before, named.astype(bf16))
    slot = jnp.arange(n_slots, dtype=jnp.int32)
    spread = (slot[None, :] // slots == ids[:, None]).astype(bf16)
    is_named = dot(named.astype(bf16), spread) > 0.5
    in_slot = dot(rank.astype(bf16), spread) == (slot % slots).astype(f32)[None, :]
    place = (is_named & in_slot).astype(bf16)

    def to_slots(v):
        return dot(place, v, ((0,), (0,))).astype(bf16).reshape(experts, slots, v.shape[1])

    grad_rows = lax.all_to_all(to_slots(out_grad), DP, 0, 0, tiled=True).reshape(n_slots, 1536)

    ends = jnp.cumsum(lengths[0])
    t256 = jnp.arange(256, dtype=jnp.int32)
    segment = jnp.sum((t256[:, None] >= ends[None, :]).astype(jnp.int32), axis=1)
    same = [
        (jnp.pad(segment, (d, 0), constant_values=-1)[:256] == segment).astype(f32)[:, None]
        for d in range(4)
    ]
    inside = (segment[:, None] == segment[None, :]) & (t256[:, None] >= t256[None, :])
    x_full = both_halves(tokens, other_tokens, s).astype(f32)
    normed = (x_full * rms(x_full) * g_in).astype(bf16)
    proj = jnp.stack([dot(normed, w_in[j]) for j in range(4)]).astype(bf16).astype(f32)
    z, x_raw, bc_raw, dt = (
        proj[..., :384],
        proj[..., 384:768],
        proj[..., 768:832],
        proj[..., 848:854],
    )
    x_pre = conv_pre(x_raw, same, conv_x[:4], conv_x[4])
    bc_pre = conv_pre(bc_raw, same, conv_bc[:4], conv_bc[4])
    x = jax.nn.silu(x_pre)
    bc = jax.nn.silu(bc_pre)
    b_mat = jnp.concatenate([bc[0], bc[1]], axis=1)
    c_mat = jnp.concatenate([bc[2], bc[3]], axis=1)
    raw = dt.transpose(1, 0, 2).reshape(256, 24) + heads[1]
    step = jax.nn.softplus(raw)
    decay = jnp.exp(heads[0])
    rate = -step * decay
    tri = (t256[:, None] >= t256[None, :]).astype(f32)
    cum = jnp.dot(tri, rate, precision=lax.Precision.HIGHEST, preferred_element_type=f32).T
    scores = dot(c_mat.astype(bf16), b_mat.astype(bf16), ((1,), (1,)))
    fade = jnp.where(inside, jnp.exp(jnp.where(inside, cum[:, :, None] - cum[:, None, :], 0.0)), 0.0)
    mixing = fade * scores * step.T[:, None, :]
    x_heads = x.reshape(4, 256, 6, 64).transpose(0, 2, 1, 3).reshape(24, 256, 64)
    x_low = x_heads.astype(bf16)
    y_heads = jnp.einsum("hts,hsp->htp", mixing.astype(bf16), x_low, preferred_element_type=f32)
    y_heads = y_heads + heads[2][:, None, None] * x_heads
    y = y_heads.reshape(4, 6, 256, 64).transpose(0, 2, 1, 3).reshape(4, 256, 384)
    gate = jax.nn.silu(z)
    gated = y * gate
    g_mix = g_mix.reshape(4, 1, 384)
    scaled = (gated * g_mix).astype(bf16)
    squares = jnp.sum(gated * gated, axis=(0, 2))[:, None]
    scaled_flat = scaled.transpose(1, 0, 2).reshape(256, 1536)
    part = jnp.concatenate([dot(scaled_flat, w_out[j]) for j in range(4)], axis=1)
    part_own, part_other = halves(part, s)
    sq_own, sq_other = halves(squares, s)
    part = part_own + swap(part_other)
    q = lax.rsqrt((sq_own + swap(sq_other)) / 3072.0 + EPS)
    residual = tokens.astype(f32) + q * part

    r = rms(residual)
    ffn_in = (residual * r * g_ffn).astype(bf16)
    w_router = w_in[:, :, 832:848].transpose(1, 0, 2).reshape(1536, 64)
    logits = dot(ffn_in, w_router)
    logits = jnp.where(named > 0.5, logits, -1e30)
    top = jnp.max(logits, axis=1, keepdims=True)
    weights = jnp.where(named > 0.5, jnp.exp(logits - top), 0.0)
    gating = weights / jnp.sum(weights, axis=1, keepdims=True)
    gate_hi, gate_lo = hi_lo(gating)
    sent = to_slots(jnp.concatenate([ffn_in, gate_hi, gate_lo], axis=1))
    arrived = lax.all_to_all(sent, DP, 0, 0, tiled=True).reshape(n_slots, 1664)

    ffn_full = both_halves(ffn_in, swap(ffn_in), s)
    og_full = both_halves(out_grad, other_grad, s)
    sgu = jnp.stack([dot(ffn_full, w_sgu[j]) for j in range(4)])
    sg, su = sgu[..., :128], sgu[..., 128:]
    s_act = (jax.nn.silu(sg) * su).astype(bf16)
    s_flat = s_act.transpose(1, 0, 2).reshape(256, 512)
    s_out = jnp.concatenate([dot(s_flat, w_sdown[j]) for j in range(4)], axis=1)
    s_own, s_other = halves(s_out, s)
    s_out = s_own + swap(s_other.astype(bf16)).astype(f32)
    og_cols = og_full.reshape(256, 4, 384).transpose(1, 0, 2)
    d_s_act = sum(dot(og_cols[j], w_sdown[j], ((1,), (1,))) for j in range(4))
    d_s_act = d_s_act.reshape(256, 4, 128).transpose(1, 0, 2)
    d_sgu = jnp.concatenate([d_s_act * su * silu_grad(sg), d_s_act * jax.nn.silu(sg)], axis=-1)
    d_sgu = d_sgu.astype(bf16)
    grad_sdown = jnp.stack([dot(s_flat, og_cols[j], ((0,), (0,))) for j in range(4)]).astype(bf16)
    grad_sgu = jnp.stack([dot(ffn_full, d_sgu[j], ((0,), (0,))) for j in range(4)]).astype(bf16)
    d_ffn = sum(dot(d_sgu[j], w_sgu[j], ((1,), (1,))) for j in range(4))
    df_own, df_other = halves(d_ffn, s)
    d_ffn = df_own + swap(df_other.astype(bf16)).astype(f32)

    rows = arrived[:, :1536]
    lane = jnp.arange(128, dtype=jnp.int32) % 64
    slot_gate = jnp.sum(
        jnp.where(lane == dp, arrived[:, 1536:].astype(f32), 0.0), axis=1, keepdims=True
    )
    e_gu = dot(rows, w_eg)
    eg, eu = e_gu[:, :512], e_gu[:, 512:]
    e_act32 = jax.nn.silu(eg) * eu
    e_act = e_act32.astype(bf16)
    e_out = dot(e_act, w_ed).astype(bf16)
    d_act = dot(grad_rows, w_ed, ((1,), (1,)))
    d_gate = jnp.sum(e_act.astype(f32) * d_act, axis=1, keepdims=True)
    d_gu32 = jnp.concatenate([d_act * eu * silu_grad(eg), d_act * jax.nn.silu(eg)], axis=1)
    d_gu = d_gu32.astype(bf16)
    d_rows = dot(d_gu, w_eg, ((1,), (1,))).astype(bf16)
    dg_hi, dg_lo = hi_lo(d_gate)
    d_rows = jnp.concatenate([d_rows, dg_hi, dg_lo, jnp.zeros((n_slots, 126), bf16)], axis=1)
    d_back = lax.all_to_all(d_rows.reshape(experts, slots, 1664), DP, 0, 0, tiled=True)
    d_back = d_back.reshape(n_slots, 1664)
    out_back = lax.all_to_all(e_out.reshape(experts, slots, 1536), DP, 0, 0, tiled=True)
    out_back = out_back.reshape(n_slots, 1536)
    grad_ed = dot((e_act.astype(f32) * slot_gate).astype(bf16), grad_rows, ((0,), (0,)))
    grad_eg = dot(rows, (d_gu32 * slot_gate).astype(bf16), ((0,), (0,)))
    ge_own, ge_other = halves(grad_eg, s)
    grad_eg = ge_own + swap(ge_other.astype(bf16)).astype(f32)
    gd_own, gd_other = halves(grad_ed, s)
    grad_ed = gd_own + swap(gd_other.astype(bf16)).astype(f32)

    wide_gate = dot(gate_hi, spread) + dot(gate_lo, spread)
    weighted = (place.astype(f32) * wide_gate).astype(bf16)
    routed = dot(weighted, out_back)
    block_out = (residual + s_out + routed).astype(bf16)
    d_route = dot(weighted, d_back[:, :1536])
    dg = d_back[:, 1536:1538].T
    d_gating = dot(place * dg[0:1], spread, ((1,), (1,))) + dot(
        place * dg[1:2], spread, ((1,), (1,))
    )
    d_logits = gating * (d_gating - jnp.sum(gating * d_gating, axis=1, keepdims=True))
    d_logits_low = d_logits.astype(bf16)
    d_ffn = d_ffn + dot(d_logits_low, w_router, ((1,), (1,))) + d_route
    ffn_norm_grad = jnp.sum(d_ffn * residual * r, axis=0)
    u = d_ffn * g_ffn
    d_residual = (
        out_grad.astype(f32)
        + r * u
        - r * r * r * residual * jnp.mean(u * residual, axis=1, keepdims=True)
    )

    d_mixed = (q * d_residual).astype(bf16)
    kappa = q * q / 3072.0 * jnp.sum(d_mixed.astype(f32) * part, axis=1, keepdims=True)
    d_mixed_full = both_halves(d_mixed, swap(d_mixed), s)
    kappa = both_halves(kappa, swap(kappa), s)
    dm_cols = d_mixed_full.reshape(256, 4, 384).transpose(1, 0, 2)
    grad_out = jnp.stack([dot(scaled_flat, dm_cols[j], ((0,), (0,))) for j in range(4)])
    grad_out = grad_out.astype(bf16)
    d_scaled = sum(dot(dm_cols[j], w_out[j], ((1,), (1,))) for j in range(4))
    d_scaled = d_scaled.reshape(256, 4, 384).transpose(1, 0, 2)
    mixer_norm_grad = jnp.sum(d_scaled * gated, axis=1)
    d_gated = d_scaled * g_mix - kappa * gated
    d_y = d_gated * gate
    d_z = d_gated * y * silu_grad(z)
    dy_heads = d_y.reshape(4, 256, 6, 64).transpose(0, 2, 1, 3).reshape(24, 256, 64)
    dy_low = dy_heads.astype(bf16)
    d_skip = jnp.sum(x_heads * dy_heads, axis=(1, 2))
    dx_heads = jnp.einsum("hts,htp->hsp", mixing.astype(bf16), dy_low, preferred_element_type=f32)
    dx_heads = dx_heads + heads[2][:, None, None] * dy_heads
    pair = jnp.einsum("htp,hsp->hts", dy_low, x_low, preferred_element_type=f32)
    pair_fade = pair * fade
    d_scores = jnp.sum(pair_fade * step.T[:, None, :], axis=0).astype(bf16)
    q_pair = pair_fade * scores
    d_step = jnp.sum(q_pair, axis=1).T
    w_pair = q_pair * step.T[:, None, :]
    d_cum = (jnp.sum(w_pair, axis=2) - jnp.sum(w_pair, axis=1)).T
    d_rate = jnp.dot(tri.T, d_cum, precision=lax.Precision.HIGHEST, preferred_element_type=f32)
    d_c = dot(d_scores, b_mat.astype(bf16))
    d_b = dot(d_scores, c_mat.astype(bf16), ((0,), (0,)))
    d_raw = (d_step - d_rate * decay) * jax.nn.sigmoid(raw)
    head_grad = jnp.stack([jnp.sum(d_rate * rate, axis=0), jnp.sum(d_raw, axis=0), d_skip])
    dx = dx_heads.reshape(4, 6, 256, 64).transpose(0, 2, 1, 3).reshape(4, 256, 384)
    d_bc = jnp.stack([d_b[:, :64], d_b[:, 64:], d_c[:, :64], d_c[:, 64:]])
    d_x_raw, conv_x_grad = conv_back(dx * silu_grad(x_pre), x_raw, same, conv_x[:4])
    d_bc_raw, conv_bc_grad = conv_back(d_bc * silu_grad(bc_pre), bc_raw, same, conv_bc[:4])
    d_dt = d_raw.reshape(256, 4, 6).transpose(1, 0, 2)
    d_proj = jnp.concatenate(
        [d_z, d_x_raw, d_bc_raw, jnp.zeros((4, 256, 16), f32), d_dt, jnp.zeros((4, 256, 42), f32)],
        axis=2,
    ).astype(bf16)
    d_normed = sum(dot(d_proj[j], w_in[j], ((1,), (1,))) for j in range(4))
    dn_own, dn_other = halves(d_normed, s)
    d_normed = dn_own + swap(dn_other.astype(bf16)).astype(f32)
    x_own = tokens.astype(f32)
    p = rms(x_own)
    in_norm_grad = jnp.sum(d_normed * x_own * p, axis=0)
    v = d_normed * g_in
    token_grad = (
        d_residual + p * v - p * p * p * x_own * jnp.mean(v * x_own, axis=1, keepdims=True)
    ).astype(bf16)

    lhs = jnp.concatenate([normed, ffn_in], axis=0)
    d_route_cols = jnp.pad(
        d_logits_low.reshape(128, 4, 16).transpose(1, 0, 2), ((0, 0), (0, 0), (832, 48))
    )
    rhs = jnp.concatenate([d_proj, d_route_cols], axis=1)
    grad_in = jnp.stack([dot(lhs, rhs[j], ((0,), (0,))) for j in range(4)]).astype(bf16)
    small = jnp.concatenate(
        [
            in_norm_grad,
            ffn_norm_grad,
            lax.dynamic_update_slice(
                jnp.zeros((3072,), f32), mixer_norm_grad.reshape(1536), (s * 1536,)
            ),
            lax.dynamic_update_slice(
                jnp.zeros((5, 3328), f32), conv_x_grad.reshape(5, 1536), (0, s * 1536)
            )
            .at[:, 3072:]
            .add(conv_bc_grad.reshape(5, 256))
            .reshape(-1),
            lax.dynamic_update_slice(jnp.zeros((3, 48), f32), head_grad, (0, s * 24)).reshape(-1),
        ]
    )
    small = lax.psum(small, ALL)
    sum_in, sum_sgu, sum_out, sum_sdown = scatter(
        (
            grad_in.reshape(4, 2, 4, 4, 48, 896),
            grad_sgu.reshape(4, 2, 4, 4, 48, 256),
            grad_out.reshape(4, 4, 4, 2, 48, 384),
            grad_sdown.reshape(4, 4, 4, 2, 16, 384),
        ),
        SPECS,
        2,
    )
    back = jnp.concatenate([sum_in, sum_sgu], axis=2).reshape(8, 12, 1152)
    back = lax.all_to_all(back, ("seq", "y"), 0, 0, tiled=True).reshape(2, 4, 12, 1152)
    back = back.transpose(2, 0, 1, 3)
    bc_dt = back[..., 768:896]
    both_cores = bc_dt[:, 0] + bc_dt[:, 1]
    in_proj_grad = jnp.concatenate(
        [
            back[..., :384].reshape(12, 3072),
            back[..., 384:768].reshape(12, 3072),
            both_cores[..., :64].reshape(12, 256),
            bc_dt[..., 80:86].reshape(12, 48),
        ],
        axis=1,
    )
    router_grad = both_cores[..., 64:80].reshape(12, 64)
    sgu_grad = jnp.concatenate(
        [back[..., 896:1024].reshape(12, 1024), back[..., 1024:].reshape(12, 1024)], axis=1
    )
    rows_out = jnp.concatenate(
        [sum_out.reshape(4, 24, 384), sum_sdown.reshape(4, 8, 384)], axis=1
    )
    rows_out = lax.all_to_all(rows_out, "y", 0, 0, tiled=True).transpose(1, 0, 2).reshape(32, 1536)

    def mine(at, width):
        return lax.dynamic_slice_in_dim(small, at + device * width, width)

    conv_grad = lax.dynamic_slice_in_dim(small[6144:22784].reshape(5, 3328), device * 26, 26, 1)
    return (
        block_out,
        token_grad,
        mine(0, 12),
        in_proj_grad,
        conv_grad[:4].T,
        conv_grad[4],
        small[22784:].reshape(3, 48),
        mine(3072, 24),
        rows_out[:24],
        mine(1536, 12),
        router_grad,
        sgu_grad,
        rows_out[24:],
        grad_eg[None],
        grad_ed[None],
    )


def solution(mesh):
    finer = Mesh(mesh.devices.reshape(2, 4, 4, 4), ALL)
    placed = (
        P(DP_SEQ, None),
        P(DP_SEQ, None),
        P(DP, None),
        P(DP_SEQ, None),
        P(ALL),
        P(ALL, None),
        P(ALL, None),
        P(ALL),
        P(),
        P(ALL),
        P(ALL, None),
        P(ALL),
        P(ALL, None),
        P(ALL, None),
        P(ALL, None),
        P(DP, "seq", None),
        P(DP, "seq", None),
    )
    return jax.shard_map(
        local,
        mesh=finer,
        in_specs=placed,
        out_specs=(
            P(DP_SEQ, None),
            P(DP_SEQ, None),
            P(ALL),
            P(ALL, None),
            P(ALL, None),
            P(ALL),
            P(),
            P(ALL),
            P(ALL, None),
            P(ALL),
            P(ALL, None),
            P(ALL, None),
            P(ALL, None),
            P(DP, "seq", None),
            P(DP, "seq", None),
        ),
        check_vma=False,
    )
```

time: 2430 us -> 1210 us (0.50); the launches traced: 2390 us -> 1200 us
  blocking collectives: 1120 us -> 304 us
  local copies, waits for them, and re-layouts: 699 us -> 141 us
  Pallas kernels: 0 us -> 190 us
  waiting for transfers between devices: 206 us -> 284 us
  matrix products: 203 us -> 137 us
    psum x4 -> x0, blocking collectives: 815 us -> none  [over_axes(): value = lax.psum(value, axis)]
    unnamed x322 -> x390, local copies, waits for them, and re-layouts: 287 us -> 27 us
    pallas_call x0 -> x2, Pallas kernels: none -> 190 us  [the longest x1 100 us: gather(): pl.pallas_call(functools.partial(gather_kernel, specs), out_shape=outs, i...]
    psum x0 -> x1, waiting for transfers between devices: none -> 136 us  [local(): small = lax.psum(small, ALL)]
    another operation x13 -> x11, local copies, waits for them, and re-layouts: 96.3 us -> 1.32 us  [the longest x1 0.62 us: local(): jnp.stack(pieces)]
    reshape x19 -> x30, local copies, waits for them, and re-layouts: 113 us -> 25 us  [the longest x1 3.15 us: local(): d_scaled = d_scaled.reshape(256, 4, 384).transpose(1, 0, 2)]
    dot_general x40 -> x74, matrix products: 203 us -> 137 us  [the longest x69 121 us: dot(): return lax.dot_general(a, b, (dims, ((), ())), preferred_element_type=f32)]
    all_gather x7 -> x0, waiting for transfers between devices: 52.3 us -> none  [the longest x1 52.2 us: local(): lax.all_gather(shared_down, SEQ_DP, axis=0, tiled=True)]
  transfers between devices with their start and end apart: 16 -> 23, of which waited for: 5 -> 7; matrix products, arithmetic and copies ran while one was open for 14% -> 16% of each run, Pallas kernels for 0% -> 8%
where the time goes in v1:
time: 1210 us; the launch traced here: 1200 us
  blocking collectives  304 us (25%)
  waiting for transfers between devices  284 us (23%)
  Pallas kernels  190 us (16%)
  local copies, waits for them, and re-layouts  141 us (12%)
  matrix products  137 us (11%)
  other arithmetic  73.7 us (6%)
  starting transfers between devices  54.3 us (4%)
  between operations  17.2 us (1%)
    all_gather x1, blocking collectives, local(): vecs = lax.all_gather(vec[None], ALL, axis=0, tiled=True)  304 us
    psum x1, waiting for transfers between devices, local(): small = lax.psum(small, ALL)  136 us
    dot_general x69, matrix products, dot(): return lax.dot_general(a, b, (dims, ((), ())), preferred_element_type=f32)  121 us
    pallas_call x1, Pallas kernels, gather(): pl.pallas_call(functools.partial(gather_kernel, specs), out_shape=outs, i...  100 us
    pallas_call x1, Pallas kernels, scatter(): pl.pallas_call(functools.partial(scatter_kernel, specs), out_shape=outs,...  89.7 us
    all_to_all x1, waiting for transfers between devices, local(): arrived = lax.all_to_all(sent, DP, 0, 0, tiled=True).reshape(n_slots, 1664)  47.2 us
    all_to_all x1, waiting for transfers between devices, local(): lax.all_to_all(to_slots(out_grad), DP, 0, 0, tiled=True)  34.7 us
    all_to_all x1, waiting for transfers between devices, local(): lax.all_to_all(d_rows.reshape(experts, slots, 1664), DP, 0, 0, tiled=True)  31.1 us
  transfers between devices with their start and end apart: 23, of which 7 were waited for; matrix products, arithmetic and copies ran while one was open for 16% of the time, Pallas kernels for 8%

profile of v1, /device:TPU:32, one launch (start us, length us, event | category | flops | bytes accessed | tf_op | source)
XLA Modules:
  0.0 1201.2 jit_solution(607471719451936224)
XLA Ops:
  9.5 4.5 all-to-all-start.1
  20.3 304.2 %all-gather.1 = bf16[128,1,256]{2,1,0:T(2,128)(2,1)S(1)} all-gather(bf16[1,1,256]{2,1,0:T(2,128)(2,1)S(1)} %reshape.650), channel_id=2, replica_groups=mesh['seq'=2,'z'=4,'x'=4,'y'=4] {'seq','z','x','y'}, dimensions={0}, use_global_device_ids=true | all-gather | bytes 66048 | tf_op jit(solution)/shard_map/all_gather | solution.py:403
  346.5 5.4 all-to-all-done
  353.3 100.2 %gather_weights.1 = (bf16[4,2,4,4,48,896]{5,4,3,2,1,0:T(8,128)(2,1)}, bf16[4,2,4,4,48,256]{5,4,3,2,1,0:T(8,128)(2,1)}, bf16[4,4,4,2,48,384]{5,4,3,2,1,0:T(8,128)(2,1)}, bf16[4,4,4,2,16,384]{5,4,3,2,1,0:T(8,128)(2,1)}) custom-call(bf16[2,48,896]{2,1,0:T(8,128)(2,1)} %slice.767.refs_0_, bf16[2,48,256]{2,1,0:T(8,128)(2,1)} %slice.768.refs_1_, ...), custom_call_target="tpu_custom_call" | custom-call | bytes 40894464 | tf_op jit(solution)/shard_map/gather_weights/pallas_call | solution.py:131
  453.5 5.0 fusion.204
  479.6 4.6 multiply_add_fusion.1
  512.4 5.0 convolution_convert_fusion.2
  517.4 7.5 all-to-all-start.2
  526.1 4.8 convolution_convert_fusion.3
  545.9 47.2 %all-to-all-done.2 = bf16[64,24,1664]{2,1,0:T(8,128)(2,1)} async-done(((bf16[64,24,1664]{2,1,0:T(8,128)(2,1)}), bf16[64,24,1664]{2,1,0:T(8,128)(2,1)}, u32[]{:S(2)}, u32[]{:S(2)}) %all-to-all-start.2) | async-done | bytes 5111840 | tf_op jit(solution)/shard_map/all_to_all | solution.py:511
  593.1 12.3 %all-to-all-start.4 = ((bf16[64,24,1536]{2,1,0:T(8,128)(2,1)}), bf16[64,24,1536]{2,1,0:T(8,128)(2,1)}, u32[]{:S(2)}, u32[]{:S(2)}) async-start(bf16[64,24,1536]{2,1,0:T(8,128)(2,1)} %bitcast.510), calls=%async_computation.4 | async-start | bytes 9437184 | tf_op jit(solution)/shard_map/all_to_all | solution.py:449
  622.8 9.4 fusion.7
  632.2 34.7 %all-to-all-done.4 = bf16[64,24,1536]{2,1,0:T(8,128)(2,1)} async-done(((bf16[64,24,1536]{2,1,0:T(8,128)(2,1)}), bf16[64,24,1536]{2,1,0:T(8,128)(2,1)}, u32[]{:S(2)}, u32[]{:S(2)}) %all-to-all-start.4) | async-done | bytes 4718624 | tf_op jit(solution)/shard_map/all_to_all | solution.py:449
  666.9 11.3 fusion.9
  678.2 4.4 convolution_convert_fusion.1
  682.6 9.1 all-to-all-start.3
  707.9 9.6 convolution_convert_fusion
  718.3 8.6 concatenate.141
  726.9 22.6 %all-to-all-done.3 = bf16[64,24,1536]{2,1,0:T(8,128)(2,1)} async-done(((bf16[64,24,1536]{2,1,0:T(8,128)(2,1)}), bf16[64,24,1536]{2,1,0:T(8,128)(2,1)}, u32[]{:S(2)}, u32[]{:S(2)}) %all-to-all-start.3) | async-done | bytes 4718624 | tf_op jit(solution)/shard_map/all_to_all | solution.py:552
  749.6 5.6 all-to-all-start.5
  766.5 4.7 fusion.40
  772.3 7.0 fusion.5
  787.8 31.1 %all-to-all-done.5 = bf16[64,24,1664]{2,1,0:T(8,128)(2,1)} async-done(((bf16[64,24,1664]{2,1,0:T(8,128)(2,1)}), bf16[64,24,1664]{2,1,0:T(8,128)(2,1)}, u32[]{:S(2)}, u32[]{:S(2)}) %all-to-all-start.5) | async-done | bytes 5111840 | tf_op jit(solution)/shard_map/all_to_all | solution.py:550
  822.3 4.4 multiply_reduce_fusion.10
  851.9 4.5 fusion.71
  859.7 5.5 multiply_reduce_fusion.1
  885.1 4.1 concatenate.144
  902.2 5.3 pad_maximum_fusion.refs_0_
  907.5 89.7 %scatter_grads.1 = (f32[2,48,896]{2,1,0:T(8,128)}, f32[2,48,256]{2,1,0:T(8,128)}, f32[2,48,384]{2,1,0:T(8,128)}, f32[2,16,384]{2,1,0:T(8,128)}) custom-call(bf16[4,2,4,4,48,896]{5,4,3,2,1,0:T(8,128)(2,1)} %pad_maximum_fusion.refs_0_, bf16[4,2,4,4,48,256]{5,4,3,2,1,0:T(8,128)(2,1)} %pad_maximum_fusion.4.refs_1_, ...), custom_call_target="tpu_custom_call" | custom-call | bytes 40894464 | tf_op jit(solution)/shard_map/scatter_grads/pallas_call | solution.py:259
  1015.1 4.8 all-to-all-start.6
  1022.8 7.5 all-to-all-done.6
  1052.2 135.6 %all-reduce.18.cloned.1.call-done = f32[22928]{0:T(1024)} async-done(((f32[22928]{0:T(1024)}), f32[22928]{0:T(1024)}) %all-reduce.18.cloned.1.call-update) | async-done | bytes 91728 | tf_op jit(solution)/shard_map/psum | solution.py:653
  (701 shorter events, 263.9 us)
Async XLA Ops:
  8.1 317.9 %copy-start.175 = (s32[1,4]{1,0:T(1,128)S(1)}, s32[1,4]{1,0:T(1,128)}, u32[]{:S(2)}) copy-start(s32[1,4]{1,0:T(1,128)} %param.21) | copy-start | bytes 52
  9.5 331.5 %all-to-all-start.1 = ((bf16[4,32,384]{2,1,0:T(8,128)(2,1)}), bf16[4,32,384]{2,1,0:T(8,128)(2,1)S(1)}, u32[]{:S(2)}, u32[]{:S(2)}) async-start(bf16[4,32,384]{2,1,0:T(8,128)(2,1)} %maximum_bitcast_fusion.1), calls=%async_computation.1 | async-start | bytes 196608 | tf_op jit(solution)/shard_map/all_to_all | solution.py:392
  13.9 313.2 %copy-start.118 = (bf16[12,2048]{1,0:T(8,128)(2,1)S(1)}, bf16[12,2048]{1,0:T(8,128)(2,1)}, u32[]{:S(2)}) copy-start(bf16[12,2048]{1,0:T(8,128)(2,1)} %param.32) | copy-start | bytes 147460
  13.9 313.2 %copy-start.121 = (bf16[12,64]{1,0:T(8,128)(2,1)S(1)}, bf16[12,64]{1,0:T(8,128)(2,1)}, u32[]{:S(2)}) copy-start(bf16[12,64]{1,0:T(8,128)(2,1)} %param.31) | copy-start | bytes 4612
  13.9 447.0 %collective-permute-start = (bf16[128,1536]{1,0:T(8,128)(2,1)}, bf16[128,1536]{1,0:T(8,128)(2,1)S(1)}, u32[]{:S(2)}, u32[]{:S(2)}) collective-permute-start(bf16[128,1536]{1,0:T(8,128)(2,1)} %param.19), channel_id=1, source_target_pairs={{0,64},{64,0},{1,65},{65,1},{2,66},{66,2},{3,67},{67,3},{4,68},{68... | collective-permute-start | bytes 1179656 | tf_op jit(solution)/shard_map/ppermute | solution.py:280
  14.9 316.5 %copy-start.166 = (bf16[3,48]{1,0:T(4,128)(2,1)S(1)}, bf16[3,48]{1,0:T(4,128)(2,1)}, u32[]{:S(2)}) copy-start(bf16[3,48]{1,0:T(4,128)(2,1)} %param.27) | copy-start | bytes 868
  326.3 140.6 %copy-start.129 = (f32[256]{0:T(256)}, f32[256]{0:T(256)S(1)}, u32[]{:S(2)}) copy-start(f32[256]{0:T(256)S(1)} %get-tuple-element.210) | copy-start | bytes 3076
  326.3 140.6 %copy-start.131 = (f32[256]{0:T(256)}, f32[256]{0:T(256)S(1)}, u32[]{:S(2)}) copy-start(f32[256]{0:T(256)S(1)} %get-tuple-element.211) | copy-start | bytes 3076
  326.3 140.6 %copy-start.133 = (f32[256]{0:T(256)}, f32[256]{0:T(256)S(1)}, u32[]{:S(2)}) copy-start(f32[256]{0:T(256)S(1)} %get-tuple-element.212) | copy-start | bytes 3076
  328.1 133.2 %copy-start.110 = (f32[1536]{0:T(1024)}, f32[1536]{0:T(1024)S(1)}, u32[]{:S(2)}) copy-start(f32[1536]{0:T(1024)S(1)} %mul.784) | copy-start | bytes 18436
  331.6 142.0 %copy-start.122 = (f32[4,384]{1,0:T(4,128)}, f32[4,384]{1,0:T(4,128)S(1)}, u32[]{:S(2)}) copy-start(f32[4,384]{1,0:T(4,128)S(1)} %mul.816) | copy-start | bytes 18436
  341.0 10.9 all-to-all-start
  495.9 9.7 collective-permute-start.2
  498.3 6.5 collective-permute-start.1
  517.4 75.7 %all-to-all-start.2 = ((bf16[64,24,1664]{2,1,0:T(8,128)(2,1)}), bf16[64,24,1664]{2,1,0:T(8,128)(2,1)}, u32[]{:S(2)}, u32[]{:S(2)}) async-start(bf16[64,24,1664]{2,1,0:T(8,128)(2,1)} %bitcast.509), calls=%async_computation.2 | async-start | bytes 10223616 | tf_op jit(solution)/shard_map/all_to_all | solution.py:511
  524.8 94.7 %collective-permute-start.5 = (bf16[768,1024]{1,0:T(8,128)(2,1)}, bf16[768,1024]{1,0:T(8,128)(2,1)}, u32[]{:S(2)}, u32[]{:S(2)}) collective-permute-start(bf16[768,1024]{1,0:T(8,128)(2,1)} %bitcast.602), channel_id=1, source_target_pairs={{0,64},{64,0},{1,65},{65,1},{2,66},{66,2},{3,67},{67,3},{4,68},{68... | collective-permute-start | bytes 4718600 | tf_op jit(solution)/shard_map/ppermute | solution.py:280
  524.9 15.6 %collective-permute-start.6 = (bf16[256,1536]{1,0:T(8,128)(2,1)}, bf16[256,1536]{1,0:T(8,128)(2,1)}, u32[]{:S(2)}, u32[]{:S(2)}) collective-permute-start(bf16[256,1536]{1,0:T(8,128)(2,1)} %bitcast.610), channel_id=1, source_target_pairs={{0,64},{64,0},{1,65},{65,1},{2,66},{66,2},{3,67},{67,3},{4,68},{68... | collective-permute-start | bytes 2359304 | tf_op jit(solution)/shard_map/ppermute | solution.py:280
  525.4 9.6 collective-permute-start.7
  543.3 68.0 %collective-permute-start.3 = (bf16[128,1536]{1,0:T(8,128)(2,1)S(1)}, bf16[128,1536]{1,0:T(8,128)(2,1)}, u32[]{:S(2)}, u32[]{:S(2)}) collective-permute-start(bf16[128,1536]{1,0:T(8,128)(2,1)S(1)} %multiply_convert_fusion.12), channel_id=1, source_target_pairs={{0,64},{64,0},{1,65},{65,1},{2,66},{66,2},{3,67},{67,3},{4,68},{68... | collective-permute-start | bytes 1179656 | tf_op jit(solution)/shard_map/ppermute | solution.py:280
  593.1 73.8 %all-to-all-start.4 = ((bf16[64,24,1536]{2,1,0:T(8,128)(2,1)}), bf16[64,24,1536]{2,1,0:T(8,128)(2,1)}, u32[]{:S(2)}, u32[]{:S(2)}) async-start(bf16[64,24,1536]{2,1,0:T(8,128)(2,1)} %bitcast.510), calls=%async_computation.4 | async-start | bytes 9437184 | tf_op jit(solution)/shard_map/all_to_all | solution.py:449
  682.6 66.9 %all-to-all-start.3 = ((bf16[64,24,1536]{2,1,0:T(8,128)(2,1)}), bf16[64,24,1536]{2,1,0:T(8,128)(2,1)}, u32[]{:S(2)}, u32[]{:S(2)}) async-start(bf16[64,24,1536]{2,1,0:T(8,128)(2,1)} %bitcast.569), calls=%async_computation.3 | async-start | bytes 9437184 | tf_op jit(solution)/shard_map/all_to_all | solution.py:552
  695.4 131.2 %collective-permute-start.4 = (bf16[128,1536]{1,0:T(8,128)(2,1)}, bf16[128,1536]{1,0:T(8,128)(2,1)}, u32[]{:S(2)}, u32[]{:S(2)}) collective-permute-start(bf16[128,1536]{1,0:T(8,128)(2,1)} %dynamic-slice_convert_fusion.4), channel_id=1, source_target_pairs={{0,64},{64,0},{1,65},{65,1},{2,66},{66,2},{3,67},{67,3},{4,68},{68... | collective-permute-start | bytes 1179656 | tf_op jit(solution)/shard_map/ppermute | solution.py:280
  749.6 69.4 %all-to-all-start.5 = ((bf16[64,24,1664]{2,1,0:T(8,128)(2,1)}), bf16[64,24,1664]{2,1,0:T(8,128)(2,1)}, u32[]{:S(2)}, u32[]{:S(2)}) async-start(bf16[64,24,1664]{2,1,0:T(8,128)(2,1)} %concatenate.141), calls=%async_computation.5 | async-start | bytes 10223616 | tf_op jit(solution)/shard_map/all_to_all | solution.py:550
  757.1 65.1 %collective-permute-start.8 = (bf16[128,1536]{1,0:T(8,128)(2,1)}, bf16[128,1536]{1,0:T(8,128)(2,1)}, u32[]{:S(2)}, u32[]{:S(2)}) collective-permute-start(bf16[128,1536]{1,0:T(8,128)(2,1)} %dynamic-slice_convert_fusion.3), channel_id=1, source_target_pairs={{0,64},{64,0},{1,65},{65,1},{2,66},{66,2},{3,67},{67,3},{4,68},{68... | collective-permute-start | bytes 1179656 | tf_op jit(solution)/shard_map/ppermute | solution.py:280
  771.3 12.0 %collective-permute-start.13 = (bf16[256,1536]{1,0:T(8,128)(2,1)S(1)}, bf16[256,1536]{1,0:T(8,128)(2,1)S(1)}, u32[]{:S(2)}, u32[]{:S(2)}) collective-permute-start(bf16[256,1536]{1,0:T(8,128)(2,1)S(1)} %dynamic-slice_convert_fusion.1), channel_id=1, source_target_pairs={{0,64},{64,0},{1,65},{65,1},{2,66},{66,2},{3,67},{67,3},{4,68},{68... | collective-permute-start | bytes 2359304 | tf_op jit(solution)/shard_map/ppermute | solution.py:280
  783.2 46.7 %collective-permute-start.12 = (bf16[768,1024]{1,0:T(8,128)(2,1)}, bf16[768,1024]{1,0:T(8,128)(2,1)}, u32[]{:S(2)}, u32[]{:S(2)}) collective-permute-start(bf16[768,1024]{1,0:T(8,128)(2,1)} %dynamic-slice_convert_fusion), channel_id=1, source_target_pairs={{0,64},{64,0},{1,65},{65,1},{2,66},{66,2},{3,67},{67,3},{4,68},{68... | collective-permute-start | bytes 4718600 | tf_op jit(solution)/shard_map/ppermute | solution.py:280
  829.2 5.2 collective-permute-start.9
  829.3 5.2 collective-permute-start.10
  999.9 15.3 %all-to-all-start.7 = ((f32[4,32,384]{2,1,0:T(8,128)}), f32[4,32,384]{2,1,0:T(8,128)S(1)}, u32[]{:S(2)}, u32[]{:S(2)}) async-start(f32[4,32,384]{2,1,0:T(8,128)} %pad_maximum_fusion.23), calls=%async_computation.7 | async-start | bytes 393216 | tf_op jit(solution)/shard_map/all_to_all | solution.py:685
  1015.1 15.2 %all-to-all-start.6 = ((f32[8,12,1152]{2,1,0:T(8,128)}), f32[8,12,1152]{2,1,0:T(8,128)S(1)}, u32[]{:S(2)}, u32[]{:S(2)}) async-start(f32[8,12,1152]{2,1,0:T(8,128)} %reshape.635), calls=%async_computation.6 | async-start | bytes 1179648 | tf_op jit(solution)/shard_map/all_to_all | solution.py:665
  1019.9 167.9 %all-reduce.18.cloned.1.call-start = ((), (), s32[]{:S(2)}) async-start(), calls=%async_computation.8 | async-start | bytes 188416 | tf_op jit(solution)/shard_map/psum | solution.py:653
  1020.7 29.3 %collective-permute-start.11 = (bf16[128,1536]{1,0:T(8,128)(2,1)}, bf16[128,1536]{1,0:T(8,128)(2,1)S(1)}, u32[]{:S(2)}, u32[]{:S(2)}) collective-permute-start(bf16[128,1536]{1,0:T(8,128)(2,1)} %dynamic-slice_convert_fusion.2), channel_id=1, source_target_pairs={{0,64},{64,0},{1,65},{65,1},{2,66},{66,2},{3,67},{67,3},{4,68},{68... | collective-permute-start | bytes 1179656 | tf_op jit(solution)/shard_map/ppermute | solution.py:280
  (177 other events, 854.4 us)
Sparse Core Ops, SparseCore 0:
  1051.2 136.4 all-reduce.17

commit v2 on v1

--- a/solution.py
+++ b/solution.py
@@ -276,6 +276,384 @@
     )(*arrays)
 
 
+def expert_kernel(rows_ref, grad_ref, gu_ref, down_ref, pick_ref, back_ref, act_ref, wact_ref, wgu_ref):
+    e_gu = dot(rows_ref[:, :1536], gu_ref[...])
+    eg, eu = e_gu[:, :512], e_gu[:, 512:]
+    sig = jax.nn.sigmoid(eg)
+    silu = eg * sig
+    act32 = silu * eu
+    act = act32.astype(bf16)
+    slot_gate = jnp.sum(rows_ref[:, 1536:].astype(f32) * pick_ref[...], axis=1, keepdims=True)
+    d_act = dot(grad_ref[...], down_ref[...], ((1,), (1,)))
+    d_gate = jnp.sum(act.astype(f32) * d_act, axis=1, keepdims=True)
+    d_eg = d_act * eu * (sig + silu * (1.0 - sig))
+    d_eu = d_act * silu
+    d_gu = jnp.concatenate([d_eg.astype(bf16), d_eu.astype(bf16)], axis=1)
+    back_ref[:, :1536] = dot(d_gu, gu_ref[...], ((1,), (1,))).astype(bf16)
+    hi = d_gate.astype(bf16).astype(f32)
+    lane = lax.broadcasted_iota(jnp.int32, (rows_ref.shape[0], 128), 1)
+    tail = jnp.where(lane == 0, hi, jnp.where(lane == 1, d_gate - hi, 0.0))
+    back_ref[:, 1536:] = tail.astype(bf16)
+    act_ref[...] = act
+    wact_ref[...] = (act32 * slot_gate).astype(bf16)
+    wgu_ref[:, :512] = (d_eg * slot_gate).astype(bf16)
+    wgu_ref[:, 512:] = (d_eu * slot_gate).astype(bf16)
+
+
+def expert_grads(rows, grad_rows, gate_up, down, pick):
+    n, block = rows.shape[0], 256
+    widths = (1664, 512, 512, 1024)
+
+    def blocked(w):
+        return pl.BlockSpec((block, w), lambda i: (i, 0))
+
+    def whole(v):
+        return pl.BlockSpec(v.shape, lambda i: (0, 0))
+
+    return pl.pallas_call(
+        expert_kernel,
+        grid=(n // block,),
+        out_shape=[jax.ShapeDtypeStruct((n, w), bf16) for w in widths],
+        in_specs=[blocked(1664), blocked(1536), whole(gate_up), whole(down), whole(pick)],
+        out_specs=[blocked(w) for w in widths],
+        compiler_params=pltpu.CompilerParams(vmem_limit_bytes=48 * 2**20),
+        cost_estimate=pl.CostEstimate(
+            flops=2 * n * 1536 * (1024 + 512 + 1024), bytes_accessed=26 * 2**20, transcendentals=0
+        ),
+        name="expert_grads",
+    )(rows, grad_rows, gate_up, down, pick)
+
+
+HEAD_AT = 80
+
+
+def split3(v):
+    hi = v.astype(bf16)
+    rest = v - hi.astype(f32)
+    mid = rest.astype(bf16)
+    return hi, mid, (rest - mid.astype(f32)).astype(bf16)
+
+
+def roll(v, by, axis):
+    return pltpu.roll(v, by, axis) if by else v
+
+
+def taps_pre(v, marks, w):
+    total = w[4:5] + w[3:4] * v
+    for d in (1, 2, 3):
+        total = total + w[3 - d : 4 - d] * (roll(v, d, 0) * marks[:, d : d + 1])
+    return total
+
+
+def taps_back(d_pre, v, marks, w):
+    d_v = w[3:4] * d_pre
+    d_w = [jnp.sum(d_pre * v, axis=0, keepdims=True)]
+    for d in (1, 2, 3):
+        masked = d_pre * marks[:, d : d + 1]
+        d_w.insert(0, jnp.sum(masked * roll(v, d, 0), axis=0, keepdims=True))
+        d_v = d_v + w[3 - d : 4 - d] * roll(masked, 256 - d, 0)
+    zero = jnp.zeros((3, v.shape[1]), f32)
+    return d_v, jnp.concatenate(d_w + [jnp.sum(d_pre, axis=0, keepdims=True), zero], axis=0)
+
+
+def lanes(shape):
+    return lax.broadcasted_iota(jnp.int32, shape, len(shape) - 1)
+
+
+def joined(first, second):
+    return jnp.where(lanes(first.shape) < 64, first, roll(second, 64, 1))
+
+
+def bc_raw(proj_ref, k):
+    return joined(
+        proj_ref[2 * k, :, 768:896].astype(f32), proj_ref[2 * k + 1, :, 768:896].astype(f32)
+    )
+
+
+def head_steps(proj_ref, hp_ref, j, tri):
+    raw = proj_ref[j, :, 768:896].astype(f32) + hp_ref[j, 1:2]
+    step = jnp.maximum(raw, 0.0) + jnp.log1p(jnp.exp(-jnp.abs(raw)))
+    rate = -step * hp_ref[j, 0:1]
+    cum = sum(dot(tri, part) for part in split3(rate))
+    return raw, step, rate, cum
+
+
+def triangle():
+    t = lax.broadcasted_iota(jnp.int32, (256, 256), 0)
+    return t >= lanes((256, 256))
+
+
+def pair_of(cols, p):
+    at = HEAD_AT + 2 * p
+    first = jnp.broadcast_to(cols[:, at : at + 1], (256, 128))
+    return jnp.where(lanes((256, 128)) < 64, first, cols[:, at + 1 : at + 2])
+
+
+def fade_of(cum, cum_rows, h, inside):
+    at = HEAD_AT + h
+    return jnp.exp(jnp.where(inside, cum[:, at : at + 1] - cum_rows[at : at + 1], -1e30))
+
+
+def forward_kernel(
+    x_ref, g_ref, w_in_ref, w_out_ref, cx_ref, cbc_ref, hp_ref, marks_ref, seg_ref,
+    normed_ref, proj_ref, y_ref, scaled_ref, part_ref, squares_ref, scores_ref,
+):
+    i = pl.program_id(0)
+
+    @pl.when(i == 0)
+    def _():
+        x = x_ref[...].astype(f32)
+        normed_ref[...] = (x * rms(x) * g_ref[0:1]).astype(bf16)
+
+    @pl.when(i < 4)
+    def _():
+        proj_ref[i] = dot(normed_ref[...], w_in_ref[0]).astype(bf16)
+
+    @pl.when(i == 4)
+    def _():
+        marks = marks_ref[...]
+        b_mat, c_mat = [jax.nn.silu(taps_pre(bc_raw(proj_ref, k), marks, cbc_ref[k])) for k in (0, 1)]
+        scores_ref[...] = dot(c_mat.astype(bf16), b_mat.astype(bf16), ((1,), (1,)))
+        part_ref[...] = jnp.zeros_like(part_ref)
+        squares_ref[...] = jnp.zeros_like(squares_ref)
+
+    @pl.when(i >= 4)
+    def _():
+        j = i - 4
+        marks, cx = marks_ref[...], cx_ref[j]
+        causal = triangle()
+        inside = causal & (marks[:, 4:5] == seg_ref[0:1])
+        _, step, _, cum = head_steps(proj_ref, hp_ref, j, causal.astype(bf16))
+        cum_rows = cum.T
+        x = jax.nn.silu(taps_pre(proj_ref[j, :, 384:768].astype(f32), marks, cx))
+        scores = scores_ref[...]
+        ys = []
+        for p in range(3):
+            xp = x[:, 128 * p : 128 * p + 128]
+            xs = (xp * pair_of(step, p)).astype(bf16)
+            y0, y1 = [
+                dot((fade_of(cum, cum_rows, 2 * p + k, inside) * scores).astype(bf16), xs)
+                for k in (0, 1)
+            ]
+            ys.append(jnp.where(lanes((256, 128)) < 64, y0, y1))
+        y = jnp.concatenate(ys, axis=1) + cx[5:6] * x
+        z = proj_ref[j, :, :384].astype(f32)
+        gated = y * jax.nn.silu(z)
+        scaled = (gated * cx[6:7]).astype(bf16)
+        y_ref[j] = y
+        scaled_ref[j] = scaled
+        squares_ref[...] += jnp.broadcast_to(
+            jnp.sum(gated * gated, axis=1, keepdims=True), squares_ref.shape
+        )
+        for c in range(4):
+            part_ref[:, c * 384 : c * 384 + 384] += dot(scaled, w_out_ref[c])
+
+
+def fixed(v):
+    return pl.BlockSpec(v.shape, lambda i: (0,) * len(v.shape))
+
+
+def mixer_forward(x, g, w_in, w_out, cx, cbc, hp, marks, seg):
+    outs = [
+        jax.ShapeDtypeStruct((256, 1536), bf16),
+        jax.ShapeDtypeStruct((4, 256, 896), bf16),
+        jax.ShapeDtypeStruct((4, 256, 384), f32),
+        jax.ShapeDtypeStruct((4, 256, 384), bf16),
+        jax.ShapeDtypeStruct((256, 1536), f32),
+        jax.ShapeDtypeStruct((256, 128), f32),
+    ]
+    return pl.pallas_call(
+        forward_kernel,
+        grid=(8,),
+        out_shape=outs,
+        in_specs=[
+            fixed(x),
+            fixed(g),
+            pl.BlockSpec((1, 1536, 896), lambda i: (jnp.minimum(i, 3), 0, 0)),
+            pl.BlockSpec((4, 384, 384), lambda i: (0, jnp.maximum(i - 4, 0), 0)),
+            *[fixed(v) for v in (cx, cbc, hp, marks, seg)],
+        ],
+        out_specs=[fixed(o) for o in outs],
+        scratch_shapes=[pltpu.VMEM((256, 256), f32)],
+        compiler_params=pltpu.CompilerParams(vmem_limit_bytes=48 * 2**20),
+        cost_estimate=pl.CostEstimate(
+            flops=2 * 256 * 1536 * (3584 + 1536), bytes_accessed=22 * 2**20, transcendentals=2**21
+        ),
+        name="mixer_forward",
+    )(x, g, w_in, w_out, cx, cbc, hp, marks, seg)
+
+
+def backward_kernel(
+    dm_ref, kappa_ref, w_out_ref, w_in_ref, normed_ref, ffn_ref, drout_ref, proj_ref, y_ref,
+    scaled_ref, cx_ref, cbc_ref, hp_ref, marks_ref, seg_ref,
+    gout_ref, gin_ref, dn_ref, gcx_ref, gcbc_ref, gheads_ref,
+    dproj_ref, scores_ref, dscores_ref, bc_ref,
+):
+    i = pl.program_id(0)
+
+    @pl.when(i == 0)
+    def _():
+        marks = marks_ref[...]
+        for k in (0, 1):
+            bc_ref[k] = jax.nn.silu(taps_pre(bc_raw(proj_ref, k), marks, cbc_ref[k])).astype(bf16)
+        scores_ref[...] = dot(bc_ref[1], bc_ref[0], ((1,), (1,)))
+        dscores_ref[...] = jnp.zeros_like(dscores_ref)
+
+    @pl.when(i < 4)
+    def _():
+        j = i
+        marks, cx = marks_ref[...], cx_ref[j]
+        scaled = scaled_ref[j]
+        d_scaled = jnp.zeros((256, 384), f32)
+        for c in range(4):
+            dm = dm_ref[:, c * 384 : c * 384 + 384]
+            d_scaled = d_scaled + dot(dm, w_out_ref[c], ((1,), (1,)))
+            gout_ref[c] = dot(scaled, dm, ((0,), (0,))).astype(bf16)
+        y = y_ref[j]
+        z = proj_ref[j, :, :384].astype(f32)
+        sig = jax.nn.sigmoid(z)
+        gate = z * sig
+        gated = y * gate
+        d_gated = d_scaled * cx[6:7] - kappa_ref[:, 0:1] * gated
+        dy = d_gated * gate
+        dproj_ref[j, :, :384] = (d_gated * y * (sig + gate * (1.0 - sig))).astype(bf16)
+        norm_grad = jnp.sum(d_scaled * gated, axis=0, keepdims=True)
+
+        causal = triangle()
+        inside = causal & (marks[:, 4:5] == seg_ref[0:1])
+        raw, step, rate, cum = head_steps(proj_ref, hp_ref, j, causal.astype(bf16))
+        cum_rows = cum.T
+        x_raw = proj_ref[j, :, 384:768].astype(f32)
+        x_pre = taps_pre(x_raw, marks, cx)
+        x_sig = jax.nn.sigmoid(x_pre)
+        x = x_pre * x_sig
+        scores = scores_ref[...]
+        d_scores = dscores_ref[...]
+        lane = lanes((256, 128))
+        low_half = lane < 64
+        row = lax.broadcasted_iota(jnp.int32, (128, 256), 0)
+        d_cum = jnp.zeros((256, 128), f32)
+        d_cum_rows = jnp.zeros((128, 256), f32)
+        d_step = jnp.zeros((256, 128), f32)
+        dxs = []
+        for p in range(3):
+            xp = x[:, 128 * p : 128 * p + 128]
+            dyp = dy[:, 128 * p : 128 * p + 128]
+            steps = pair_of(step, p)
+            xs = (xp * steps).astype(bf16)
+            dy_low = dyp.astype(bf16)
+            back = []
+            for k in (0, 1):
+                at = HEAD_AT + 2 * p + k
+                fade = fade_of(cum, cum_rows, 2 * p + k, inside)
+                mine = jnp.where(low_half if k == 0 else ~low_half, dyp, 0.0).astype(bf16)
+                pair = dot(mine, xs, ((1,), (1,)))
+                mixing = fade * scores
+                w = mixing * pair
+                d_scores = d_scores + fade * pair
+                d_cum = jnp.where(lane == at, jnp.sum(w, axis=1, keepdims=True), d_cum)
+                d_cum_rows = jnp.where(row == at, jnp.sum(w, axis=0, keepdims=True), d_cum_rows)
+                back.append(dot(mixing.astype(bf16), dy_low, ((0,), (0,))))
+            d_xs = jnp.where(low_half, back[0], back[1])
+            prod = xp * d_xs
+            first = jnp.sum(jnp.where(low_half, prod, 0.0), axis=1, keepdims=True)
+            second = jnp.sum(jnp.where(low_half, 0.0, prod), axis=1, keepdims=True)
+            at = HEAD_AT + 2 * p
+            d_step = jnp.where(lane == at, first, jnp.where(lane == at + 1, second, d_step))
+            dxs.append(d_xs * steps)
+        dscores_ref[...] = d_scores
+        dx = jnp.concatenate(dxs, axis=1) + cx[5:6] * dy
+        skip_grad = jnp.sum(x * dy, axis=0, keepdims=True)
+        d_x_pre = dx * (x_sig + x * (1.0 - x_sig))
+        d_x_raw, conv_grad = taps_back(d_x_pre, x_raw, marks, cx)
+        dproj_ref[j, :, 384:768] = d_x_raw.astype(bf16)
+        rowid = lax.broadcasted_iota(jnp.int32, (8, 384), 0)
+        gcx_ref[j] = jnp.where(rowid == 5, skip_grad, jnp.where(rowid == 6, norm_grad, conv_grad))
+        d_cum = d_cum - d_cum_rows.T
+        d_rate = sum(dot(causal.astype(bf16), part, ((0,), (0,))) for part in split3(d_cum))
+        d_raw = (d_step - d_rate * hp_ref[j, 0:1]) * jax.nn.sigmoid(raw)
+        dproj_ref[j, :, 768:896] = d_raw.astype(bf16)
+        rowid = lax.broadcasted_iota(jnp.int32, (8, 128), 0)
+        gheads_ref[j] = jnp.where(
+            rowid == 0,
+            jnp.sum(d_rate * rate, axis=0, keepdims=True),
+            jnp.where(rowid == 1, jnp.sum(d_raw, axis=0, keepdims=True), 0.0),
+        )
+
+    @pl.when(i == 4)
+    def _():
+        marks = marks_ref[...]
+        d_scores = dscores_ref[...].astype(bf16)
+        d_bc = (dot(d_scores, bc_ref[1], ((0,), (0,))), dot(d_scores, bc_ref[0]))
+        low_half = lanes((256, 128)) < 64
+        for k in (0, 1):
+            raw = bc_raw(proj_ref, k)
+            pre = taps_pre(raw, marks, cbc_ref[k])
+            sig = jax.nn.sigmoid(pre)
+            d_pre = d_bc[k] * (sig + pre * sig * (1.0 - sig))
+            d_raw, conv_grad = taps_back(d_pre, raw, marks, cbc_ref[k])
+            gcbc_ref[k] = conv_grad
+            for h, moved in enumerate((d_raw, roll(d_raw, 64, 1))):
+                steps = dproj_ref[2 * k + h, :, 768:896].astype(f32)
+                dproj_ref[2 * k + h, :, 768:896] = jnp.where(low_half, moved, steps).astype(bf16)
+        dn_ref[...] = jnp.zeros_like(dn_ref)
+
+    @pl.when(i >= 4)
+    def _():
+        j = i - 4
+        d_proj = dproj_ref[j]
+        dn_ref[...] += dot(d_proj, w_in_ref[0], ((1,), (1,)))
+        gin_ref[0, :, :768] = dot(normed_ref[...], d_proj[:, :768], ((0,), (0,))).astype(bf16)
+        last = dot(normed_ref[...], d_proj[:, 768:], ((0,), (0,)))
+        last = last + dot(ffn_ref[...], drout_ref[j], ((0,), (0,)))
+        gin_ref[0, :, 768:] = last.astype(bf16)
+
+
+def mixer_backward(dm, kappa, w_out, w_in, normed, ffn_in, drout, proj, y, scaled, cx, cbc, hp, marks, seg):
+    def late(i):
+        return jnp.maximum(i - 4, 0)
+
+    def early(i):
+        return jnp.minimum(i, 3)
+
+    small = [
+        jax.ShapeDtypeStruct((256, 1536), f32),
+        jax.ShapeDtypeStruct((4, 8, 384), f32),
+        jax.ShapeDtypeStruct((2, 8, 128), f32),
+        jax.ShapeDtypeStruct((4, 8, 128), f32),
+    ]
+    w_out_spec = pl.BlockSpec((4, 384, 384), lambda i: (0, early(i), 0))
+    w_in_spec = pl.BlockSpec((1, 1536, 896), lambda i: (late(i), 0, 0))
+    return pl.pallas_call(
+        backward_kernel,
+        grid=(8,),
+        out_shape=[
+            jax.ShapeDtypeStruct((4, 1536, 384), bf16),
+            jax.ShapeDtypeStruct((4, 1536, 896), bf16),
+            *small,
+        ],
+        in_specs=[
+            fixed(dm),
+            fixed(kappa),
+            w_out_spec,
+            w_in_spec,
+            *[fixed(v) for v in (normed, ffn_in, drout, proj, y, scaled, cx, cbc, hp, marks, seg)],
+        ],
+        out_specs=[w_out_spec, w_in_spec, *[fixed(o) for o in small]],
+        scratch_shapes=[
+            pltpu.VMEM((4, 256, 896), bf16),
+            pltpu.VMEM((256, 256), f32),
+            pltpu.VMEM((256, 256), f32),
+            pltpu.VMEM((2, 256, 128), bf16),
+        ],
+        compiler_params=pltpu.CompilerParams(vmem_limit_bytes=56 * 2**20),
+        cost_estimate=pl.CostEstimate(
+            flops=4 * 256 * 1536 * (3584 + 1536), bytes_accessed=40 * 2**20, transcendentals=2**21
+        ),
+        name="mixer_backward",
+    )(dm, kappa, w_out, w_in, normed, ffn_in, drout, proj, y, scaled, cx, cbc, hp, marks, seg)
+
+
 def swap(v):
     return lax.ppermute(v, "seq", [(0, 1), (1, 0)])
 
@@ -306,32 +684,6 @@
 def silu_grad(v):
     sig = jax.nn.sigmoid(v)
     return sig * (1.0 + v * (1.0 - sig))
-
-
-def shift_down(v, d):
-    return jnp.pad(v, [(0, 0)] * (v.ndim - 2) + [(d, 0), (0, 0)])[..., : v.shape[-2], :] if d else v
-
-
-def shift_up(v, d):
-    return jnp.pad(v, [(0, 0)] * (v.ndim - 2) + [(0, d), (0, 0)])[..., d:, :] if d else v
-
-
-def conv_pre(v, same, w, b):
-    total = b
-    for k in range(4):
-        d = 3 - k
-        total = total + w[k] * (shift_down(v, d) * same[d])
-    return total
-
-
-def conv_back(d_pre, v, same, w):
-    d_w = [jnp.sum(d_pre * (shift_down(v, 3 - k) * same[3 - k]), axis=-2) for k in range(4)]
-    d_b = jnp.sum(d_pre, axis=-2)
-    d_v = 0.0
-    for k in range(4):
-        d = 3 - k
-        d_v = d_v + w[k] * shift_up(d_pre * same[d], d)
-    return d_v, jnp.stack(d_w + [d_b], axis=0)
 
 
 def local(
@@ -400,7 +752,7 @@
             jnp.zeros((78,), bf16),
         ]
     )
-    vecs = lax.all_gather(vec[None], ALL, axis=0, tiled=True)
+    vecs = lax.all_to_all(jnp.broadcast_to(vec, (128, 256)), ALL, 0, 0, tiled=True)
     other_tokens = swap(tokens)
     other_grad = swap(out_grad)
     other_gate_up = swap(expert_gate_up[0])
@@ -422,13 +774,24 @@
     w_sdown = w_sdown.reshape(4, 512, 384)
 
     vecs = vecs.astype(f32)
-    g_in = vecs[:, :12].reshape(1536)
+    g_in = vecs[:, :12].reshape(1, 1536)
     g_ffn = vecs[:, 12:24].reshape(1536)
-    g_mix = lax.dynamic_slice_in_dim(vecs[:, 24:48].reshape(3072), s * 1536, 1536)
+    g_mix = lax.dynamic_slice_in_dim(vecs[:, 24:48].reshape(1, 3072), s * 1536, 1536, 1)
     conv = vecs[:, 48:178].reshape(128, 5, 26).transpose(1, 0, 2).reshape(5, 3328)
-    conv_x = lax.dynamic_slice_in_dim(conv[:, :3072], s * 1536, 1536, 1).reshape(5, 4, 1, 384)
-    conv_bc = conv[:, 3072:].reshape(5, 4, 1, 64)
     heads = lax.dynamic_slice_in_dim(head_params.astype(f32), s * 24, 24, 1)
+    cx = jnp.concatenate(
+        [
+            lax.dynamic_slice_in_dim(conv[:, :3072], s * 1536, 1536, 1),
+            jnp.broadcast_to(heads[2][:, None], (24, 64)).reshape(1, 1536),
+            g_mix,
+            jnp.zeros((1, 1536), f32),
+        ],
+        axis=0,
+    )
+    cx = cx.reshape(8, 4, 384).transpose(1, 0, 2)
+    cbc = jnp.pad(conv[:, 3072:], ((0, 3), (0, 0))).reshape(8, 2, 128).transpose(1, 0, 2)
+    hp = jnp.stack([jnp.exp(heads[0]), heads[1]]).reshape(2, 4, 6).transpose(1, 0, 2)
+    hp = jnp.pad(hp, ((0, 0), (0, 6), (HEAD_AT, 122 - HEAD_AT)))
     w_eg = both_halves(expert_gate_up[0], other_gate_up, s)
     w_ed = both_halves(expert_down[0], other_down, s)
 
@@ -446,52 +809,24 @@
     def to_slots(v):
         return dot(place, v, ((0,), (0,))).astype(bf16).reshape(experts, slots, v.shape[1])
 
-    grad_rows = lax.all_to_all(to_slots(out_grad), DP, 0, 0, tiled=True).reshape(n_slots, 1536)
+    grad_slots, w_in = lax.optimization_barrier((to_slots(out_grad), w_in))
+    grad_rows = lax.all_to_all(grad_slots, DP, 0, 0, tiled=True).reshape(n_slots, 1536)
 
     ends = jnp.cumsum(lengths[0])
     t256 = jnp.arange(256, dtype=jnp.int32)
     segment = jnp.sum((t256[:, None] >= ends[None, :]).astype(jnp.int32), axis=1)
+    seg = segment.astype(f32)
     same = [
-        (jnp.pad(segment, (d, 0), constant_values=-1)[:256] == segment).astype(f32)[:, None]
+        (jnp.pad(segment, (d, 0), constant_values=-1)[:256] == segment).astype(f32)
         for d in range(4)
     ]
-    inside = (segment[:, None] == segment[None, :]) & (t256[:, None] >= t256[None, :])
-    x_full = both_halves(tokens, other_tokens, s).astype(f32)
-    normed = (x_full * rms(x_full) * g_in).astype(bf16)
-    proj = jnp.stack([dot(normed, w_in[j]) for j in range(4)]).astype(bf16).astype(f32)
-    z, x_raw, bc_raw, dt = (
-        proj[..., :384],
-        proj[..., 384:768],
-        proj[..., 768:832],
-        proj[..., 848:854],
-    )
-    x_pre = conv_pre(x_raw, same, conv_x[:4], conv_x[4])
-    bc_pre = conv_pre(bc_raw, same, conv_bc[:4], conv_bc[4])
-    x = jax.nn.silu(x_pre)
-    bc = jax.nn.silu(bc_pre)
-    b_mat = jnp.concatenate([bc[0], bc[1]], axis=1)
-    c_mat = jnp.concatenate([bc[2], bc[3]], axis=1)
-    raw = dt.transpose(1, 0, 2).reshape(256, 24) + heads[1]
-    step = jax.nn.softplus(raw)
-    decay = jnp.exp(heads[0])
-    rate = -step * decay
-    tri = (t256[:, None] >= t256[None, :]).astype(f32)
-    cum = jnp.dot(tri, rate, precision=lax.Precision.HIGHEST, preferred_element_type=f32).T
-    scores = dot(c_mat.astype(bf16), b_mat.astype(bf16), ((1,), (1,)))
-    fade = jnp.where(inside, jnp.exp(jnp.where(inside, cum[:, :, None] - cum[:, None, :], 0.0)), 0.0)
-    mixing = fade * scores * step.T[:, None, :]
-    x_heads = x.reshape(4, 256, 6, 64).transpose(0, 2, 1, 3).reshape(24, 256, 64)
-    x_low = x_heads.astype(bf16)
-    y_heads = jnp.einsum("hts,hsp->htp", mixing.astype(bf16), x_low, preferred_element_type=f32)
-    y_heads = y_heads + heads[2][:, None, None] * x_heads
-    y = y_heads.reshape(4, 6, 256, 64).transpose(0, 2, 1, 3).reshape(4, 256, 384)
-    gate = jax.nn.silu(z)
-    gated = y * gate
-    g_mix = g_mix.reshape(4, 1, 384)
-    scaled = (gated * g_mix).astype(bf16)
-    squares = jnp.sum(gated * gated, axis=(0, 2))[:, None]
-    scaled_flat = scaled.transpose(1, 0, 2).reshape(256, 1536)
-    part = jnp.concatenate([dot(scaled_flat, w_out[j]) for j in range(4)], axis=1)
+    marks = jnp.pad(jnp.stack(same + [seg], axis=1), ((0, 0), (0, 123)))
+    seg = jnp.broadcast_to(seg, (8, 256))
+    x_full = both_halves(tokens, other_tokens, s)
+    normed, proj, y, scaled, part, squares = mixer_forward(
+        x_full, jnp.broadcast_to(g_in, (8, 1536)), w_in, w_out, cx, cbc, hp, marks, seg
+    )
+    squares = squares[:, :1]
     part_own, part_other = halves(part, s)
     sq_own, sq_other = halves(squares, s)
     part = part_own + swap(part_other)
@@ -508,6 +843,7 @@
     gating = weights / jnp.sum(weights, axis=1, keepdims=True)
     gate_hi, gate_lo = hi_lo(gating)
     sent = to_slots(jnp.concatenate([ffn_in, gate_hi, gate_lo], axis=1))
+    sent, grad_rows = lax.optimization_barrier((sent, grad_rows))
     arrived = lax.all_to_all(sent, DP, 0, 0, tiled=True).reshape(n_slots, 1664)
 
     ffn_full = both_halves(ffn_in, swap(ffn_in), s)
@@ -530,29 +866,17 @@
     df_own, df_other = halves(d_ffn, s)
     d_ffn = df_own + swap(df_other.astype(bf16)).astype(f32)
 
-    rows = arrived[:, :1536]
     lane = jnp.arange(128, dtype=jnp.int32) % 64
-    slot_gate = jnp.sum(
-        jnp.where(lane == dp, arrived[:, 1536:].astype(f32), 0.0), axis=1, keepdims=True
-    )
-    e_gu = dot(rows, w_eg)
-    eg, eu = e_gu[:, :512], e_gu[:, 512:]
-    e_act32 = jax.nn.silu(eg) * eu
-    e_act = e_act32.astype(bf16)
-    e_out = dot(e_act, w_ed).astype(bf16)
-    d_act = dot(grad_rows, w_ed, ((1,), (1,)))
-    d_gate = jnp.sum(e_act.astype(f32) * d_act, axis=1, keepdims=True)
-    d_gu32 = jnp.concatenate([d_act * eu * silu_grad(eg), d_act * jax.nn.silu(eg)], axis=1)
-    d_gu = d_gu32.astype(bf16)
-    d_rows = dot(d_gu, w_eg, ((1,), (1,))).astype(bf16)
-    dg_hi, dg_lo = hi_lo(d_gate)
-    d_rows = jnp.concatenate([d_rows, dg_hi, dg_lo, jnp.zeros((n_slots, 126), bf16)], axis=1)
+    pick = (lane == dp).astype(f32)[None, :]
+    d_rows, e_act, w_act, w_gu = expert_grads(arrived, grad_rows, w_eg, w_ed, pick)
     d_back = lax.all_to_all(d_rows.reshape(experts, slots, 1664), DP, 0, 0, tiled=True)
     d_back = d_back.reshape(n_slots, 1664)
+    e_out = dot(e_act, w_ed).astype(bf16)
+    e_out, d_back = lax.optimization_barrier((e_out, d_back))
     out_back = lax.all_to_all(e_out.reshape(experts, slots, 1536), DP, 0, 0, tiled=True)
     out_back = out_back.reshape(n_slots, 1536)
-    grad_ed = dot((e_act.astype(f32) * slot_gate).astype(bf16), grad_rows, ((0,), (0,)))
-    grad_eg = dot(rows, (d_gu32 * slot_gate).astype(bf16), ((0,), (0,)))
+    grad_ed = dot(w_act, grad_rows, ((0,), (0,)))
+    grad_eg = dot(arrived[:, :1536], w_gu, ((0,), (0,)))
     ge_own, ge_other = halves(grad_eg, s)
     grad_eg = ge_own + swap(ge_other.astype(bf16)).astype(f32)
     gd_own, gd_other = halves(grad_ed, s)
@@ -560,8 +884,6 @@
 
     wide_gate = dot(gate_hi, spread) + dot(gate_lo, spread)
     weighted = (place.astype(f32) * wide_gate).astype(bf16)
-    routed = dot(weighted, out_back)
-    block_out = (residual + s_out + routed).astype(bf16)
     d_route = dot(weighted, d_back[:, :1536])
     dg = d_back[:, 1536:1538].T
     d_gating = dot(place * dg[0:1], spread, ((1,), (1,))) + dot(
@@ -582,42 +904,16 @@
     kappa = q * q / 3072.0 * jnp.sum(d_mixed.astype(f32) * part, axis=1, keepdims=True)
     d_mixed_full = both_halves(d_mixed, swap(d_mixed), s)
     kappa = both_halves(kappa, swap(kappa), s)
-    dm_cols = d_mixed_full.reshape(256, 4, 384).transpose(1, 0, 2)
-    grad_out = jnp.stack([dot(scaled_flat, dm_cols[j], ((0,), (0,))) for j in range(4)])
-    grad_out = grad_out.astype(bf16)
-    d_scaled = sum(dot(dm_cols[j], w_out[j], ((1,), (1,))) for j in range(4))
-    d_scaled = d_scaled.reshape(256, 4, 384).transpose(1, 0, 2)
-    mixer_norm_grad = jnp.sum(d_scaled * gated, axis=1)
-    d_gated = d_scaled * g_mix - kappa * gated
-    d_y = d_gated * gate
-    d_z = d_gated * y * silu_grad(z)
-    dy_heads = d_y.reshape(4, 256, 6, 64).transpose(0, 2, 1, 3).reshape(24, 256, 64)
-    dy_low = dy_heads.astype(bf16)
-    d_skip = jnp.sum(x_heads * dy_heads, axis=(1, 2))
-    dx_heads = jnp.einsum("hts,htp->hsp", mixing.astype(bf16), dy_low, preferred_element_type=f32)
-    dx_heads = dx_heads + heads[2][:, None, None] * dy_heads
-    pair = jnp.einsum("htp,hsp->hts", dy_low, x_low, preferred_element_type=f32)
-    pair_fade = pair * fade
-    d_scores = jnp.sum(pair_fade * step.T[:, None, :], axis=0).astype(bf16)
-    q_pair = pair_fade * scores
-    d_step = jnp.sum(q_pair, axis=1).T
-    w_pair = q_pair * step.T[:, None, :]
-    d_cum = (jnp.sum(w_pair, axis=2) - jnp.sum(w_pair, axis=1)).T
-    d_rate = jnp.dot(tri.T, d_cum, precision=lax.Precision.HIGHEST, preferred_element_type=f32)
-    d_c = dot(d_scores, b_mat.astype(bf16))
-    d_b = dot(d_scores, c_mat.astype(bf16), ((0,), (0,)))
-    d_raw = (d_step - d_rate * decay) * jax.nn.sigmoid(raw)
-    head_grad = jnp.stack([jnp.sum(d_rate * rate, axis=0), jnp.sum(d_raw, axis=0), d_skip])
-    dx = dx_heads.reshape(4, 6, 256, 64).transpose(0, 2, 1, 3).reshape(4, 256, 384)
-    d_bc = jnp.stack([d_b[:, :64], d_b[:, 64:], d_c[:, :64], d_c[:, 64:]])
-    d_x_raw, conv_x_grad = conv_back(dx * silu_grad(x_pre), x_raw, same, conv_x[:4])
-    d_bc_raw, conv_bc_grad = conv_back(d_bc * silu_grad(bc_pre), bc_raw, same, conv_bc[:4])
-    d_dt = d_raw.reshape(256, 4, 6).transpose(1, 0, 2)
-    d_proj = jnp.concatenate(
-        [d_z, d_x_raw, d_bc_raw, jnp.zeros((4, 256, 16), f32), d_dt, jnp.zeros((4, 256, 42), f32)],
-        axis=2,
-    ).astype(bf16)
-    d_normed = sum(dot(d_proj[j], w_in[j], ((1,), (1,))) for j in range(4))
+    drout = jnp.pad(d_logits_low.reshape(128, 4, 16).transpose(1, 0, 2), ((0, 0), (0, 0), (64, 48)))
+    grad_out, grad_in, d_normed, g_cx, g_cbc, g_heads = mixer_backward(
+        d_mixed_full, kappa, w_out, w_in, normed, ffn_in, drout, proj, y, scaled, cx, cbc, hp, marks, seg
+    )
+    conv_x_grad = g_cx[:, :5].transpose(1, 0, 2).reshape(5, 1536)
+    conv_bc_grad = g_cbc[:, :5].transpose(1, 0, 2).reshape(5, 256)
+    mixer_norm_grad = g_cx[:, 6].reshape(1536)
+    head_grad = g_heads[:, :2, HEAD_AT : HEAD_AT + 6].transpose(1, 0, 2).reshape(2, 24)
+    d_skip = jnp.sum(g_cx[:, 5].reshape(24, 64), axis=1)
+    head_grad = jnp.concatenate([head_grad, d_skip[None]], axis=0)
     dn_own, dn_other = halves(d_normed, s)
     d_normed = dn_own + swap(dn_other.astype(bf16)).astype(f32)
     x_own = tokens.astype(f32)
@@ -628,29 +924,29 @@
         d_residual + p * v - p * p * p * x_own * jnp.mean(v * x_own, axis=1, keepdims=True)
     ).astype(bf16)
 
-    lhs = jnp.concatenate([normed, ffn_in], axis=0)
-    d_route_cols = jnp.pad(
-        d_logits_low.reshape(128, 4, 16).transpose(1, 0, 2), ((0, 0), (0, 0), (832, 48))
-    )
-    rhs = jnp.concatenate([d_proj, d_route_cols], axis=1)
-    grad_in = jnp.stack([dot(lhs, rhs[j], ((0,), (0,))) for j in range(4)]).astype(bf16)
+    conv_grad = lax.dynamic_update_slice(
+        jnp.zeros((5, 3328), f32), conv_x_grad, (0, s * 1536)
+    )
+    conv_grad = lax.dynamic_update_slice(conv_grad, conv_bc_grad, (0, 3072))
+    mixer_norm_grad = lax.dynamic_update_slice(
+        jnp.zeros((128, 24), f32), mixer_norm_grad.reshape(64, 24), (s * 64, 0)
+    )
+    head_grad = lax.dynamic_update_slice(jnp.zeros((3, 48), f32), head_grad, (0, s * 24))
     small = jnp.concatenate(
         [
-            in_norm_grad,
-            ffn_norm_grad,
-            lax.dynamic_update_slice(
-                jnp.zeros((3072,), f32), mixer_norm_grad.reshape(1536), (s * 1536,)
-            ),
-            lax.dynamic_update_slice(
-                jnp.zeros((5, 3328), f32), conv_x_grad.reshape(5, 1536), (0, s * 1536)
-            )
-            .at[:, 3072:]
-            .add(conv_bc_grad.reshape(5, 256))
-            .reshape(-1),
-            lax.dynamic_update_slice(jnp.zeros((3, 48), f32), head_grad, (0, s * 24)).reshape(-1),
-        ]
-    )
-    small = lax.psum(small, ALL)
+            in_norm_grad.reshape(128, 12),
+            ffn_norm_grad.reshape(128, 12),
+            mixer_norm_grad,
+            conv_grad.reshape(5, 128, 26).transpose(1, 0, 2).reshape(128, 130),
+            jnp.broadcast_to(head_grad.reshape(1, 144), (128, 144)),
+            jnp.zeros((128, 62), f32),
+        ],
+        axis=1,
+    )
+    weighted_late, small, grad_in = lax.optimization_barrier((weighted, small, grad_in))
+    small = jnp.sum(lax.all_to_all(small, ALL, 0, 0, tiled=True), axis=0)
+    routed = dot(weighted_late, out_back)
+    block_out = (residual + s_out + routed).astype(bf16)
     sum_in, sum_sgu, sum_out, sum_sdown = scatter(
         (
             grad_in.reshape(4, 2, 4, 4, 48, 896),
@@ -684,21 +980,18 @@
     )
     rows_out = lax.all_to_all(rows_out, "y", 0, 0, tiled=True).transpose(1, 0, 2).reshape(32, 1536)
 
-    def mine(at, width):
-        return lax.dynamic_slice_in_dim(small, at + device * width, width)
-
-    conv_grad = lax.dynamic_slice_in_dim(small[6144:22784].reshape(5, 3328), device * 26, 26, 1)
+    conv_grad = small[48:178].reshape(5, 26)
     return (
         block_out,
         token_grad,
-        mine(0, 12),
+        small[:12],
         in_proj_grad,
         conv_grad[:4].T,
         conv_grad[4],
-        small[22784:].reshape(3, 48),
-        mine(3072, 24),
+        small[178:322].reshape(3, 48),
+        small[24:48],
         rows_out[:24],
-        mine(1536, 12),
+        small[12:24],
         router_grad,
         sgu_grad,
         rows_out[24:],

time: 1210 us -> 658 us (0.54)
  blocking collectives: 304 us -> 0 us
  waiting for transfers between devices: 284 us -> 152 us
  matrix products: 137 us -> 57.3 us
  local copies, waits for them, and re-layouts: 141 us -> 82.9 us
  Pallas kernels: 190 us -> 246 us
  other arithmetic: 73.7 us -> 40.9 us
  between operations: 17.2 us -> 2.83 us
    all_gather x1 -> x0, blocking collectives: 304 us -> none  [local(): vecs = lax.all_gather(vec[None], ALL, axis=0, tiled=True)]
    psum x1 -> x0, waiting for transfers between devices: 136 us -> none  [local(): small = lax.psum(small, ALL)]
    pallas_call x0 -> x3, Pallas kernels: none -> 65.5 us  [the longest x1 30.8 us: mixer_backward(): pl.pallas_call(backward_kernel, grid=(8,), out_shape=[jax.ShapeDtypeStruc...]
    dot_general x69 -> x39, matrix products: 121 us -> 57.3 us  [dot(): return lax.dot_general(a, b, (dims, ((), ())), preferred_element_type=f32)]
    dot_general x5 -> x0, matrix products: 15.7 us -> none  [the longest x1 5.46 us: local(): pair = jnp.einsum('htp,hsp->hts', dy_low, x_low, preferred_element_type=f32)]
    all_to_all x1 -> x3, starting transfers between devices: 12.3 us -> 25.3 us  [the longest x1 10.2 us: local(): lax.all_to_all(jnp.broadcast_to(vec, (128, 256)), ALL, 0, 0, tiled=True)]
    all_to_all x1 -> x3, waiting for transfers between devices: 34.7 us -> 25.5 us  [the longest x1 17.5 us: local(): lax.all_to_all(grad_slots, DP, 0, 0, tiled=True).reshape(n_slots, 1536)]
    unnamed x390 -> x193, local copies, waits for them, and re-layouts: 27 us -> 19.5 us
  transfers between devices with their start and end apart: 23 -> 24, of which waited for: 7 -> 9; matrix products, arithmetic and copies ran while one was open for 16% -> 22% of each run, Pallas kernels for 8% -> 16%
where the time goes in v2:
time: 658 us; the launch traced here: 648 us
  Pallas kernels  246 us (37%)
  waiting for transfers between devices  152 us (23%)
  local copies, waits for them, and re-layouts  82.9 us (13%)
  starting transfers between devices  66.2 us (10%)
  matrix products  57.3 us (9%)
  other arithmetic  40.9 us (6%)
    pallas_call x1, Pallas kernels, scatter(): pl.pallas_call(functools.partial(scatter_kernel, specs), out_shape=outs,...  91.8 us
    pallas_call x1, Pallas kernels, gather(): pl.pallas_call(functools.partial(gather_kernel, specs), out_shape=outs, i...  88.7 us
    dot_general x39, matrix products, dot(): return lax.dot_general(a, b, (dims, ((), ())), preferred_element_type=f32)  57.3 us
    all_to_all x1, waiting for transfers between devices, local(): arrived = lax.all_to_all(sent, DP, 0, 0, tiled=True).reshape(n_slots, 1664)  42.6 us
    all_to_all x1, waiting for transfers between devices, local(): lax.all_to_all(e_out.reshape(experts, slots, 1536), DP, 0, 0, tiled=True)  33.1 us
    all_to_all x1, waiting for transfers between devices, local(): lax.all_to_all(d_rows.reshape(experts, slots, 1664), DP, 0, 0, tiled=True)  31.9 us
    pallas_call x1, Pallas kernels, mixer_backward(): pl.pallas_call(backward_kernel, grid=(8,), out_shape=[jax.ShapeDtypeStruc...  30.8 us
    unnamed x193, local copies, waits for them, and re-layouts  19.5 us
  transfers between devices with their start and end apart: 24, of which 9 were waited for; matrix products, arithmetic and copies ran while one was open for 22% of the time, Pallas kernels for 16%

profile of v2, /device:TPU:32, one launch (start us, length us, event | category | flops | bytes accessed | tf_op | source)
XLA Modules:
  0.0 648.3 jit_solution(2568831877036660035)
XLA Ops:
  6.5 10.2 %all-to-all-start = ((bf16[128,2,128]{2,1,0:T(2,128)(2,1)}), bf16[128,2,128]{2,1,0:T(2,128)(2,1)S(1)}, u32[]{:S(2)}, u32[]{:S(2)}) async-start(bf16[128,2,128]{2,1,0:T(2,128)(2,1)} %reshape.505), calls=%async_computation | async-start | bytes 131072 | tf_op jit(solution)/shard_map/all_to_all | solution.py:755
  26.5 3.7 convolution_convert_fusion.2
  36.7 4.4 all-to-all-start.2
  42.4 4.5 all-to-all-done.2
  46.9 3.4 all-to-all-start.1
  51.7 5.9 all-to-all-done.1
  58.9 88.7 %gather_weights.1 = (bf16[4,2,4,4,48,896]{5,4,3,2,1,0:T(8,128)(2,1)}, bf16[4,2,4,4,48,256]{5,4,3,2,1,0:T(8,128)(2,1)}, bf16[4,4,4,2,48,384]{5,4,3,2,1,0:T(8,128)(2,1)}, bf16[4,4,4,2,16,384]{5,4,3,2,1,0:T(8,128)(2,1)}) custom-call(bf16[2,48,896]{2,1,0:T(8,128)(2,1)} %slice.499.refs_0_, bf16[2,48,256]{2,1,0:T(8,128)(2,1)} %slice.500.refs_1_, ...), custom_call_target="tpu_custom_call" | custom-call | bytes 40894464 | tf_op jit(solution)/shard_map/gather_weights/pallas_call | solution.py:131
  150.6 8.3 %all-to-all-start.3 = ((bf16[64,24,1536]{2,1,0:T(8,128)(2,1)}), bf16[64,24,1536]{2,1,0:T(8,128)(2,1)}, u32[]{:S(2)}, u32[]{:S(2)}) async-start(bf16[64,24,1536]{2,1,0:T(8,128)(2,1)} %bitcast.281), calls=%async_computation.3 | async-start | bytes 9437184 | tf_op jit(solution)/shard_map/all_to_all | solution.py:813
  159.0 3.6 fusion.93
  163.8 16.3 %mixer_forward.1 = (bf16[256,1536]{1,0:T(8,128)(2,1)S(1)}, bf16[4,256,896]{2,1,0:T(8,128)(2,1)}, f32[4,256,384]{2,1,0:T(8,128)S(1)}, bf16[4,256,384]{2,1,0:T(8,1...) custom-call(bf16[256,1536]{1,0:T(8,128)(2,1)S(1)} %pad_maximum_fusion.6.x_ref, ...), custom_call_target="tpu_custom_call" | custom-call | flops 4026531840 | bytes 23068672 | tf_op jit(solution)/shard_map/mixer_forward/pallas_call | solution.py:465
  195.5 4.9 convolution_convert_fusion.1
  200.4 17.5 %all-to-all-done.3 = bf16[64,24,1536]{2,1,0:T(8,128)(2,1)} async-done(((bf16[64,24,1536]{2,1,0:T(8,128)(2,1)}), bf16[64,24,1536]{2,1,0:T(8,128)(2,1)}, u32[]{:S(2)}, u32[]{:S(2)}) %all-to-all-start.3) | async-done | bytes 4718624 | tf_op jit(solution)/shard_map/all_to_all | solution.py:813
  217.8 7.2 %all-to-all-start.4 = ((bf16[64,24,1664]{2,1,0:T(8,128)(2,1)}), bf16[64,24,1664]{2,1,0:T(8,128)(2,1)}, u32[]{:S(2)}, u32[]{:S(2)}) async-start(bf16[64,24,1664]{2,1,0:T(8,128)(2,1)} %bitcast.280), calls=%async_computation.4 | async-start | bytes 10223616 | tf_op jit(solution)/shard_map/all_to_all | solution.py:847
  245.8 42.6 %all-to-all-done.4 = bf16[64,24,1664]{2,1,0:T(8,128)(2,1)} async-done(((bf16[64,24,1664]{2,1,0:T(8,128)(2,1)}), bf16[64,24,1664]{2,1,0:T(8,128)(2,1)}, u32[]{:S(2)}, u32[]{:S(2)}) %all-to-all-start.4) | async-done | bytes 5111840 | tf_op jit(solution)/shard_map/all_to_all | solution.py:847
  288.4 18.4 %expert_grads.1 = (bf16[1536,1664]{1,0:T(8,128)(2,1)}, bf16[1536,512]{1,0:T(8,128)(2,1)S(1)}, bf16[1536,512]{1,0:T(8,128)(2,1)S(1)}, bf16[1536,1024]{1,0:T(8,128)(2,1)}) custom-call(bf16[1536,1664]{1,0:T(8,128)(2,1)} %bitcast.62.rows_ref, bf16[1536,1536]{1,0:T(8,128)(2,1)} %bitcast.61.grad_ref, bf16[1536,1024]{1,0:T(8,128)(2,1)} %pad_maximum_fusion.gu_ref, ...), custom_call_target="tpu_custom_call" | custom-call | flops 12079595520 | bytes 27262976 | tf_op jit(solution)/shard_map/expert_grads/pallas_call | solution.py:313
  309.1 8.1 %all-to-all-start.5 = ((bf16[64,24,1664]{2,1,0:T(8,128)(2,1)}), bf16[64,24,1664]{2,1,0:T(8,128)(2,1)}, u32[]{:S(2)}, u32[]{:S(2)}) async-start(bf16[64,24,1664]{2,1,0:T(8,128)(2,1)} %bitcast.312), calls=%async_computation.5 | async-start | bytes 10223616 | tf_op jit(solution)/shard_map/all_to_all | solution.py:872
  333.4 4.3 convolution_convert_fusion
  337.7 9.5 %fusion = f32[1536,1024]{1,0:T(8,128)} fusion(bf16[1536,1024]{1,0:T(8,128)(2,1)S(1)} %copy-done.90, bf16[1536,1664]{1,0:T(8,128)(2,1)} %bitcast.62.rows_ref), kind=kOutput, calls=%fused_computation.3 | convolution fusion | flops 4831838208 | bytes 14155776 | tf_op jit(solution)/shard_map/dot_general | solution.py:28
  347.2 31.9 %all-to-all-done.5 = bf16[64,24,1664]{2,1,0:T(8,128)(2,1)} async-done(((bf16[64,24,1664]{2,1,0:T(8,128)(2,1)}), bf16[64,24,1664]{2,1,0:T(8,128)(2,1)}, u32[]{:S(2)}, u32[]{:S(2)}) %all-to-all-start.5) | async-done | bytes 5111840 | tf_op jit(solution)/shard_map/all_to_all | solution.py:872
  382.4 4.2 multiply_reduce_fusion
  392.2 6.7 %fusion.108 = f32[512,1536]{1,0:T(8,128)} fusion(bf16[1536,512]{1,0:T(8,128)(2,1)S(1)} %copy-done.9, bf16[1536,1536]{1,0:T(8,128)(2,1)} %bitcast.61.grad_ref), kind=kOutput, calls=%fused_computation.257 | convolution fusion | flops 2415919104 | bytes 9437184 | tf_op jit(solution)/shard_map/dot_general | solution.py:28
  401.7 30.8 %mixer_backward.1 = (bf16[4,1536,384]{2,1,0:T(8,128)(2,1)}, bf16[4,1536,896]{2,1,0:T(8,128)(2,1)}, f32[256,1536]{1,0:T(8,128)}, f32[4,8,384]{2,1,0:T(8,128)}, f3...) custom-call(bf16[256,1536]{1,0:T(8,128)(2,1)} %pad_maximum_fusion.9.dm_ref, f32[256,1]{1,0:T(8,128)} %pad_maximum_fusion.14.kappa_ref, ...), custom_call_target="tpu_custom_call" | custom-call | flops 8053063680 | bytes 41943040 | tf_op jit(solution)/shard_map/mixer_backward/pallas_call | solution.py:627
  440.6 91.8 %scatter_grads.1 = (f32[2,48,896]{2,1,0:T(8,128)}, f32[2,48,256]{2,1,0:T(8,128)}, f32[2,48,384]{2,1,0:T(8,128)}, f32[2,16,384]{2,1,0:T(8,128)}) custom-call(bf16[4,2,4,4,48,896]{5,4,3,2,1,0:T(8,128)(2,1)} %bitcast.301, bf16[4,2,4,4,48,256]{5,4,3,2,1,0:T(8,128)(2,1)} %pad_maximum_fusion.1.refs_1_, bf16[4,4,4,2,48,384]{5,4,3,2,1,0:T(8,128)(2,1)} %bitcast.313, ...), custom_call_target="tpu_custom_call" | custom-call | bytes 40894464 | tf_op jit(solution)/shard_map/scatter_grads/pallas_call | solution.py:259
  534.0 3.4 all-to-all-start.9
  543.7 6.7 %all-to-all-start.7 = ((f32[128,1,384]{2,1,0:T(1,128)}), f32[128,1,384]{2,1,0:T(1,128)}, u32[]{:S(2)}, u32[]{:S(2)}) async-start(f32[128,1,384]{2,1,0:T(1,128)} %all_to_all.41), calls=%async_computation.7 | async-start | bytes 393216 | tf_op jit(solution)/shard_map/all_to_all | solution.py:947
  551.3 8.0 %all-to-all-done.7 = f32[128,1,384]{2,1,0:T(1,128)} async-done(((f32[128,1,384]{2,1,0:T(1,128)}), f32[128,1,384]{2,1,0:T(1,128)}, u32[]{:S(2)}, u32[]{:S(2)}) %all-to-all-start.7) | async-done | bytes 196640 | tf_op jit(solution)/shard_map/all_to_all | solution.py:947
  559.4 3.5 all-to-all-start.8
  566.8 6.5 %all-to-all-done.8 = f32[8,12,1152]{2,1,0:T(8,128)S(1)} async-done(((f32[8,12,1152]{2,1,0:T(8,128)}), f32[8,12,1152]{2,1,0:T(8,128)S(1)}, u32[]{:S(2)}, u32[]{:S(2)}) %all-to-all-start.8) | async-done | bytes 442400 | tf_op jit(solution)/shard_map/all_to_all | solution.py:961
  573.3 7.3 %all-to-all-start.6 = ((bf16[64,24,1536]{2,1,0:T(8,128)(2,1)}), bf16[64,24,1536]{2,1,0:T(8,128)(2,1)}, u32[]{:S(2)}, u32[]{:S(2)}) async-start(bf16[64,24,1536]{2,1,0:T(8,128)(2,1)} %bitcast.314), calls=%async_computation.6 | async-start | bytes 9437184 | tf_op jit(solution)/shard_map/all_to_all | solution.py:876
  586.2 4.9 add_bitcast_fusion
  610.6 33.1 %all-to-all-done.6 = bf16[64,24,1536]{2,1,0:T(8,128)(2,1)} async-done(((bf16[64,24,1536]{2,1,0:T(8,128)(2,1)}), bf16[64,24,1536]{2,1,0:T(8,128)(2,1)}, u32[]{:S(2)}, u32[]{:S(2)}) %all-to-all-start.6) | async-done | bytes 4718624 | tf_op jit(solution)/shard_map/all_to_all | solution.py:876
  643.7 4.1 add_convert_fusion
  (436 shorter events, 141.2 us)
Async XLA Ops:
  6.5 30.2 %all-to-all-start = ((bf16[128,2,128]{2,1,0:T(2,128)(2,1)}), bf16[128,2,128]{2,1,0:T(2,128)(2,1)S(1)}, u32[]{:S(2)}, u32[]{:S(2)}) async-start(bf16[128,2,128]{2,1,0:T(2,128)(2,1)} %reshape.505), calls=%async_computation | async-start | bytes 131072 | tf_op jit(solution)/shard_map/all_to_all | solution.py:755
  16.7 145.9 %collective-permute-start = (bf16[128,1536]{1,0:T(8,128)(2,1)}, bf16[128,1536]{1,0:T(8,128)(2,1)S(1)}, u32[]{:S(2)}, u32[]{:S(2)}) collective-permute-start(bf16[128,1536]{1,0:T(8,128)(2,1)} %param.17), channel_id=1, source_target_pairs={{0,64},{64,0},{1,65},{65,1},{2,66},{66,2},{3,67},{67,3},{4,68},{68... | collective-permute-start | bytes 1179656 | tf_op jit(solution)/shard_map/ppermute | solution.py:658
  16.9 145.7 %collective-permute-start.5 = (bf16[128,1536]{1,0:T(8,128)(2,1)}, bf16[128,1536]{1,0:T(8,128)(2,1)S(1)}, u32[]{:S(2)}, u32[]{:S(2)}) collective-permute-start(bf16[128,1536]{1,0:T(8,128)(2,1)} %param.18), channel_id=1, source_target_pairs={{0,64},{64,0},{1,65},{65,1},{2,66},{66,2},{3,67},{67,3},{4,68},{68... | collective-permute-start | bytes 1179656 | tf_op jit(solution)/shard_map/ppermute | solution.py:658
  17.3 212.8 %collective-permute-start.8 = (bf16[256,1536]{1,0:T(8,128)(2,1)}, bf16[256,1536]{1,0:T(8,128)(2,1)}, u32[]{:S(2)}, u32[]{:S(2)}) collective-permute-start(bf16[256,1536]{1,0:T(8,128)(2,1)} %bitcast.347), channel_id=1, source_target_pairs={{0,64},{64,0},{1,65},{65,1},{2,66},{66,2},{3,67},{67,3},{4,68},{68... | collective-permute-start | bytes 2359304 | tf_op jit(solution)/shard_map/ppermute | solution.py:658
  17.5 224.8 %collective-permute-start.7 = (bf16[768,1024]{1,0:T(8,128)(2,1)}, bf16[768,1024]{1,0:T(8,128)(2,1)}, u32[]{:S(2)}, u32[]{:S(2)}) collective-permute-start(bf16[768,1024]{1,0:T(8,128)(2,1)} %bitcast.343), channel_id=1, source_target_pairs={{0,64},{64,0},{1,65},{65,1},{2,66},{66,2},{3,67},{67,3},{4,68},{68... | collective-permute-start | bytes 4718600 | tf_op jit(solution)/shard_map/ppermute | solution.py:658
  30.9 132.8 %copy-start.2 = (f32[4,8,128]{2,1,0:T(8,128)}, f32[4,8,128]{2,1,0:T(8,128)S(1)}, u32[]{:S(2)}) copy-start(f32[4,8,128]{2,1,0:T(8,128)S(1)} %pad.29.hp_ref) | copy-start | bytes 49156
  31.0 132.8 %copy-start = (f32[256,128]{1,0:T(8,128)}, f32[256,128]{1,0:T(8,128)S(1)}, u32[]{:S(2)}) copy-start(f32[256,128]{1,0:T(8,128)S(1)} %pad.33.marks_ref) | copy-start | bytes 393220
  36.7 10.2 %all-to-all-start.2 = ((bf16[4,32,384]{2,1,0:T(8,128)(2,1)}), bf16[4,32,384]{2,1,0:T(8,128)(2,1)S(1)}, u32[]{:S(2)}, u32[]{:S(2)}) async-start(bf16[4,32,384]{2,1,0:T(8,128)(2,1)} %maximum_bitcast_fusion), calls=%async_computation.2 | async-start | bytes 196608 | tf_op jit(solution)/shard_map/all_to_all | solution.py:744
  42.2 121.5 %copy-start.72 = (f32[1536]{0:T(1024)}, f32[1536]{0:T(1024)S(1)}, u32[]{:S(2)}) copy-start(f32[1536]{0:T(1024)S(1)} %broadcast_in_dim.85) | copy-start | bytes 18436
  42.3 121.4 %copy-start.3 = (f32[2,8,128]{2,1,0:T(8,128)}, f32[2,8,128]{2,1,0:T(8,128)S(1)}, u32[]{:S(2)}) copy-start(f32[2,8,128]{2,1,0:T(8,128)S(1)} %pad_bitcast_fusion.cbc_ref) | copy-start | bytes 24580
  46.9 10.6 %all-to-all-start.1 = ((bf16[8,12,1152]{2,1,0:T(8,128)(2,1)}), bf16[8,12,1152]{2,1,0:T(8,128)(2,1)S(1)}, u32[]{:S(2)}, u32[]{:S(2)}) async-start(bf16[8,12,1152]{2,1,0:T(8,128)(2,1)} %bitcast_dynamic-update-slice_fusion), calls=%async_computation.1 | async-start | bytes 589824 | tf_op jit(solution)/shard_map/all_to_all | solution.py:740
  50.4 113.3 %copy-start.1 = (f32[4,8,384]{2,1,0:T(8,128)}, f32[4,8,384]{2,1,0:T(8,128)S(1)}, u32[]{:S(2)}) copy-start(f32[4,8,384]{2,1,0:T(8,128)S(1)} %maximum_bitcast_fusion.1.cx_ref) | copy-start | bytes 147460
  150.6 67.2 %all-to-all-start.3 = ((bf16[64,24,1536]{2,1,0:T(8,128)(2,1)}), bf16[64,24,1536]{2,1,0:T(8,128)(2,1)}, u32[]{:S(2)}, u32[]{:S(2)}) async-start(bf16[64,24,1536]{2,1,0:T(8,128)(2,1)} %bitcast.281), calls=%async_computation.3 | async-start | bytes 9437184 | tf_op jit(solution)/shard_map/all_to_all | solution.py:813
  183.1 7.2 %collective-permute-start.2 = (f32[128,1536]{1,0:T(8,128)}, f32[128,1536]{1,0:T(8,128)}, u32[]{:S(2)}, u32[]{:S(2)}) collective-permute-start(f32[128,1536]{1,0:T(8,128)} %constant_dynamic-slice_fusion), channel_id=1, source_target_pairs={{0,64},{64,0},{1,65},{65,1},{2,66},{66,2},{3,67},{67,3},{4,68},{68... | collective-permute-start | bytes 2359304 | tf_op jit(solution)/shard_map/ppermute | solution.py:658
  185.2 41.8 %copy-start.28 = (bf16[1,4,4,2,16,384]{5,4,3,2,1,0:T(8,128)(2,1)}, bf16[1,4,4,2,16,384]{5,4,3,2,1,0:T(8,128)(2,1)S(1)}, u32[]{:S(2)}) copy-start(bf16[1,4,4,2,16,384]{5,4,3,2,1,0:T(8,128)(2,1)S(1)} %get-tuple-element.113) | copy-start | bytes 1179652
  186.9 2.6 collective-permute-start.1
  188.4 38.6 %copy-start.20 = (bf16[32,4,8,384]{3,2,0,1:T(8,128)(2,1)}, bf16[32,4,8,384]{3,2,0,1:T(8,128)(2,1)S(1)}, u32[]{:S(2)}) copy-start(bf16[32,4,8,384]{3,2,0,1:T(8,128)(2,1)S(1)} %copy.227) | copy-start | bytes 2359300
  217.8 70.6 %all-to-all-start.4 = ((bf16[64,24,1664]{2,1,0:T(8,128)(2,1)}), bf16[64,24,1664]{2,1,0:T(8,128)(2,1)}, u32[]{:S(2)}, u32[]{:S(2)}) async-start(bf16[64,24,1664]{2,1,0:T(8,128)(2,1)} %bitcast.280), calls=%async_computation.4 | async-start | bytes 10223616 | tf_op jit(solution)/shard_map/all_to_all | solution.py:847
  232.9 2.2 collective-permute-start.3
  309.1 70.0 %all-to-all-start.5 = ((bf16[64,24,1664]{2,1,0:T(8,128)(2,1)}), bf16[64,24,1664]{2,1,0:T(8,128)(2,1)}, u32[]{:S(2)}, u32[]{:S(2)}) async-start(bf16[64,24,1664]{2,1,0:T(8,128)(2,1)} %bitcast.312), calls=%async_computation.5 | async-start | bytes 10223616 | tf_op jit(solution)/shard_map/all_to_all | solution.py:872
  323.3 59.0 %collective-permute-start.6 = (bf16[128,1536]{1,0:T(8,128)(2,1)}, bf16[128,1536]{1,0:T(8,128)(2,1)}, u32[]{:S(2)}, u32[]{:S(2)}) collective-permute-start(bf16[128,1536]{1,0:T(8,128)(2,1)} %dynamic-slice_convert_fusion.3), channel_id=1, source_target_pairs={{0,64},{64,0},{1,65},{65,1},{2,66},{66,2},{3,67},{67,3},{4,68},{68... | collective-permute-start | bytes 1179656 | tf_op jit(solution)/shard_map/ppermute | solution.py:658
  391.4 8.6 %collective-permute-start.10 = (f32[128,1]{1,0:T(8,128)S(1)}, f32[128,1]{1,0:T(8,128)S(1)}, u32[]{:S(2)}, u32[]{:S(2)}) collective-permute-start(f32[128,1]{1,0:T(8,128)S(1)} %multiply_multiply_fusion), channel_id=1, source_target_pairs={{0,64},{64,0},{1,65},{65,1},{2,66},{66,2},{3,67},{67,3},{4,68},{68... | collective-permute-start | bytes 1544 | tf_op jit(solution)/shard_map/ppermute | solution.py:658
  391.5 9.2 %collective-permute-start.9 = (bf16[128,1536]{1,0:T(8,128)(2,1)}, bf16[128,1536]{1,0:T(8,128)(2,1)S(1)}, u32[]{:S(2)}, u32[]{:S(2)}) collective-permute-start(bf16[128,1536]{1,0:T(8,128)(2,1)} %get-tuple-element.93), channel_id=1, source_target_pairs={{0,64},{64,0},{1,65},{65,1},{2,66},{66,2},{3,67},{67,3},{4,68},{68... | collective-permute-start | bytes 1179656 | tf_op jit(solution)/shard_map/ppermute | solution.py:658
  435.8 3.0 collective-permute-start.11
  438.8 93.6 %copy-start.59 = (bf16[128,1536]{1,0:T(8,128)(2,1)}, bf16[128,1536]{1,0:T(8,128)(2,1)S(1)}, u32[]{:S(2)}) copy-start(bf16[128,1536]{1,0:T(8,128)(2,1)S(1)} %collective-permute-done.11) | copy-start | bytes 1179652
  534.0 9.7 %all-to-all-start.9 = ((f32[4,32,384]{2,1,0:T(8,128)}), f32[4,32,384]{2,1,0:T(8,128)S(1)}, u32[]{:S(2)}, u32[]{:S(2)}) async-start(f32[4,32,384]{2,1,0:T(8,128)} %pad_maximum_fusion.12), calls=%async_computation.9 | async-start | bytes 393216 | tf_op jit(solution)/shard_map/all_to_all | solution.py:981
  540.7 45.5 %collective-permute-start.12 = (bf16[768,1024]{1,0:T(8,128)(2,1)}, bf16[768,1024]{1,0:T(8,128)(2,1)}, u32[]{:S(2)}, u32[]{:S(2)}) collective-permute-start(bf16[768,1024]{1,0:T(8,128)(2,1)} %dynamic-slice_convert_fusion), channel_id=1, source_target_pairs={{0,64},{64,0},{1,65},{65,1},{2,66},{66,2},{3,67},{67,3},{4,68},{68... | collective-permute-start | bytes 4718600 | tf_op jit(solution)/shard_map/ppermute | solution.py:658
  543.7 15.7 %all-to-all-start.7 = ((f32[128,1,384]{2,1,0:T(1,128)}), f32[128,1,384]{2,1,0:T(1,128)}, u32[]{:S(2)}, u32[]{:S(2)}) async-start(f32[128,1,384]{2,1,0:T(1,128)} %all_to_all.41), calls=%async_computation.7 | async-start | bytes 393216 | tf_op jit(solution)/shard_map/all_to_all | solution.py:947
  559.4 13.9 %all-to-all-start.8 = ((f32[8,12,1152]{2,1,0:T(8,128)}), f32[8,12,1152]{2,1,0:T(8,128)S(1)}, u32[]{:S(2)}, u32[]{:S(2)}) async-start(f32[8,12,1152]{2,1,0:T(8,128)} %reshape.458), calls=%async_computation.8 | async-start | bytes 1179648 | tf_op jit(solution)/shard_map/all_to_all | solution.py:961
  565.3 18.4 %collective-permute-start.13 = (bf16[256,1536]{1,0:T(8,128)(2,1)}, bf16[256,1536]{1,0:T(8,128)(2,1)}, u32[]{:S(2)}, u32[]{:S(2)}) collective-permute-start(bf16[256,1536]{1,0:T(8,128)(2,1)} %dynamic-slice_convert_fusion.1), channel_id=1, source_target_pairs={{0,64},{64,0},{1,65},{65,1},{2,66},{66,2},{3,67},{67,3},{4,68},{68... | collective-permute-start | bytes 2359304 | tf_op jit(solution)/shard_map/ppermute | solution.py:658
  573.3 70.4 %all-to-all-start.6 = ((bf16[64,24,1536]{2,1,0:T(8,128)(2,1)}), bf16[64,24,1536]{2,1,0:T(8,128)(2,1)}, u32[]{:S(2)}, u32[]{:S(2)}) async-start(bf16[64,24,1536]{2,1,0:T(8,128)(2,1)} %bitcast.314), calls=%async_computation.6 | async-start | bytes 9437184 | tf_op jit(solution)/shard_map/all_to_all | solution.py:876
  583.4 27.2 %collective-permute-start.4 = (bf16[128,1536]{1,0:T(8,128)(2,1)}, bf16[128,1536]{1,0:T(8,128)(2,1)}, u32[]{:S(2)}, u32[]{:S(2)}) collective-permute-start(bf16[128,1536]{1,0:T(8,128)(2,1)} %dynamic-slice_convert_fusion.4), channel_id=1, source_target_pairs={{0,64},{64,0},{1,65},{65,1},{2,66},{66,2},{3,67},{67,3},{4,68},{68... | collective-permute-start | bytes 1179656 | tf_op jit(solution)/shard_map/ppermute | solution.py:658
  (85 other events, 500.7 us)

commit v3 on v2

--- a/solution.py
+++ b/solution.py
@@ -21,7 +21,10 @@
 
 ROWS_FIRST = (("y", "s", "z", "x"), "rows")
 CHANNELS = (("y", "z", "x", "s"), "cols")
-SPECS = (ROWS_FIRST, ROWS_FIRST, CHANNELS, CHANNELS)
+VECTORS = (("s", "z", "x", "y"), "one")
+SPECS = (ROWS_FIRST, ROWS_FIRST, CHANNELS, CHANNELS, VECTORS)
+HEAD_AT = 80
+SIZES = {"y": 4, "z": 4, "x": 4, "s": 2}
 
 
 def dot(a, b, dims=((1,), (0,))):
@@ -36,16 +39,33 @@
     return pos, right, left, opp
 
 
+def chip_row():
+    core, y = lax.axis_index("seq"), lax.axis_index("y")
+    return [(lax.rem(core + c, 2), lax.rem(y + d, 4)) for c in range(2) for d in range(4)]
+
+
 def greet(right, left):
     barrier = pltpu.get_barrier_semaphore()
-    for a in DP:
-        for n in (right[a], left[a]):
-            pl.semaphore_signal(barrier, inc=1, device_id={a: n}, device_id_type=MESH_ID)
-    pl.semaphore_wait(barrier, 6)
+
+    def signal(device_id):
+        pl.semaphore_signal(barrier, inc=1, device_id=device_id, device_id_type=MESH_ID)
+
+    for a in ("z", "x"):
+        signal({a: right[a]})
+        signal({a: left[a]})
+    for core, y in chip_row()[1:]:
+        signal({"seq": core, "y": y})
+    pl.semaphore_wait(barrier, 11)
+
+
+def cuts(spec):
+    return range(1 if spec[1] == "one" else 3)
 
 
 def third(shape, split, a):
     rows, cols = shape[-2:]
+    if split == "one":
+        return (slice(None), slice(None))
     if split == "rows":
         return (pl.ds(rows // 3 * a, rows // 3), slice(None))
     return (slice(None), pl.ds(cols // 3 * a, cols // 3))
@@ -53,7 +73,7 @@
 
 def third_shape(shape, split):
     rows, cols = shape[-2:]
-    return (rows // 3, cols) if split == "rows" else (rows, cols // 3)
+    return {"one": (rows, cols), "rows": (rows // 3, cols), "cols": (rows, cols // 3)}[split]
 
 
 def region(ref, spec, free, fixed, a, s=None):
@@ -67,18 +87,87 @@
     return ref.at[tuple(ix) + third(ref.shape, split, a)]
 
 
-def gather_kernel(specs, *refs):
-    n = len(specs)
-    ins, outs, (send, recv, loc) = refs[:n], refs[n : 2 * n], refs[2 * n :]
+def roll(v, by, axis):
+    by = by % v.shape[axis]
+    return pltpu.roll(v, by, axis) if by else v
+
+
+def lanes(shape):
+    return lax.broadcasted_iota(jnp.int32, shape, len(shape) - 1)
+
+
+def moved(v, at, to, width):
+    lane = lanes(v.shape)
+    return jnp.where((lane >= to) & (lane < to + width), roll(v, to - at, 1), 0.0)
+
+
+def gather_kernel(in_ref, gu_ref, router_ref, rows_ref, vec_ref, *refs):
+    specs, n = SPECS, len(SPECS)
+    outs, blocks = refs[:n], refs[n : 2 * n]
+    pin, pout, bin_, bout, send0, recv0, send, recv, loc = refs[2 * n :]
     pos, right, left, opp = neighbours()
+    row = chip_row()
+    (core, y) = row[0]
+    bc = [in_ref[:, 6144 + 128 * k : 6272 + 128 * k].astype(f32) for k in range(2)]
+    router, steps = router_ref[...].astype(f32), in_ref[:, 6400:6528].astype(f32)
+    for c in range(2):
+        for j in range(4):
+            k, at = 4 * c + j, c * 1536 + j * 384
+            misc = (
+                moved(bc[j // 2], 64 * (j % 2), 0, 64)
+                + moved(router, 16 * j, 64, 16)
+                + moved(steps, 24 * c + 6 * j, HEAD_AT, 6)
+            )
+            pin[k, :, :384] = in_ref[:, at : at + 384]
+            pin[k, :, 384:768] = in_ref[:, 3072 + at : 3456 + at]
+            pin[k, :, 768:896] = misc.astype(bf16)
+            pin[k, :, 896:1024] = gu_ref[:, 128 * k : 128 * k + 128]
+            pin[k, :, 1024:] = gu_ref[:, 1024 + 128 * k : 1152 + 128 * k]
+    for j in range(4):
+        pout[j] = rows_ref[:, 384 * j : 384 * j + 384]
+    greet(right, left)
+    sends, first = [], []
+
+    def push(src, dst, k, device_id):
+        c = pltpu.make_async_remote_copy(
+            src_ref=src,
+            dst_ref=dst,
+            send_sem=send0.at[k],
+            recv_sem=recv0.at[k],
+            device_id=device_id,
+            device_id_type=MESH_ID,
+        )
+        c.start()
+        sends.append(c)
+        first.append(c)
+
+    for k, (c, d) in enumerate(row):
+        if k:
+            push(pin.at[4 * c + d], bin_.at[4 * core + y], k, {"seq": c, "y": d})
+    for k, (_, d) in enumerate(row[:4]):
+        if k:
+            push(pout.at[d], bout.at[y], 8 + k, {"y": d})
+    push(vec_ref, blocks[4].at[core], 0, {"seq": 1 - core})
+    blocks[4][core] = vec_ref[...]
+    bin_[4 * core + y] = pin[4 * core + y]
+    bout[y] = pout[y]
+    for c in first:
+        c.wait_recv()
+    for c in range(2):
+        v = jnp.concatenate([bin_[4 * c + d].astype(f32)[:12] for d in range(4)], axis=0)
+        blocks[0][c] = v[:, :896].astype(bf16)
+        blocks[1][c] = v[:, 896:].astype(bf16)
+    v = [bout[d].astype(f32) for d in range(4)]
+    for h in range(2):
+        blocks[2][h] = jnp.concatenate([v[2 * h][:24], v[2 * h + 1][:24]], axis=0).astype(bf16)
+        blocks[3][h] = jnp.concatenate([v[2 * h][24:], v[2 * h + 1][24:]], axis=0).astype(bf16)
+
     own = []
     for i in range(n):
         ix = tuple(slice(None) if d == "s" else pos[d] for d in specs[i][0])
-        c = pltpu.make_async_copy(ins[i], outs[i].at[ix], loc.at[i])
+        c = pltpu.make_async_copy(blocks[i], outs[i].at[ix], loc.at[i])
         c.start()
         own.append(c)
-    greet(right, left)
-    sends = []
 
     def remote(i, st, a, k, src, dst, ax, to):
         c = pltpu.make_async_remote_copy(
@@ -93,24 +182,23 @@
         sends.append(c)
         return c
 
+    every = [(i, a) for i in range(n) for a in cuts(specs[i])]
     for st in range(3):
         first, later = {}, []
-        for i in range(n):
-            for a in range(3):
-                ax, free = ORDER[a][st], ORDER[a][:st]
-                dst = region(outs[i], specs[i], free, pos, a)
-                src = dst
-                if st == 0:
-                    src = ins[i].at[(slice(None),) + third(ins[i].shape, specs[i][1], a)]
-                for d, to in enumerate((right[ax], left[ax])):
-                    first[i, a, d] = remote(i, st, a, d, src, dst, ax, to)
-        for i in range(n):
-            for a in range(3):
-                ax, free = ORDER[a][st], ORDER[a][:st]
-                for d, (to, frm) in enumerate(((right[ax], left[ax]), (left[ax], right[ax]))):
-                    first[i, a, d].wait_recv()
-                    r = region(outs[i], specs[i], free, {**pos, ax: frm}, a, s=d)
-                    later.append(remote(i, st, a, 2 + d, r, r, ax, to))
+        for i, a in every:
+            ax, free = ORDER[a][st], ORDER[a][:st]
+            dst = region(outs[i], specs[i], free, pos, a)
+            src = dst
+            if st == 0:
+                src = blocks[i].at[(slice(None),) + third(blocks[i].shape, specs[i][1], a)]
+            for d, to in enumerate((right[ax], left[ax])):
+                first[i, a, d] = remote(i, st, a, d, src, dst, ax, to)
+        for i, a in every:
+            ax, free = ORDER[a][st], ORDER[a][:st]
+            for d, (to, frm) in enumerate(((right[ax], left[ax]), (left[ax], right[ax]))):
+                first[i, a, d].wait_recv()
+                r = region(outs[i], specs[i], free, {**pos, ax: frm}, a, s=d)
+                later.append(remote(i, st, a, 2 + d, r, r, ax, to))
         for c in later:
             c.wait_recv()
         if st == 0:
@@ -120,28 +208,37 @@
         c.wait_send()
 
 
-def gather(arrays, specs, collective_id):
-    n = len(arrays)
-    sizes = {"y": 4, "z": 4, "x": 4, "s": 2}
+def gather(in_rows, gu_rows, router_rows, rows, vec):
+    n = len(SPECS)
+    blocks = [(2, 48, 896), (2, 48, 256), (2, 48, 384), (2, 16, 384), (2, 16, 128)]
     outs = [
-        jax.ShapeDtypeStruct(tuple(sizes[d] for d in spec[0]) + v.shape[1:], v.dtype)
-        for v, spec in zip(arrays, specs)
+        jax.ShapeDtypeStruct(tuple(SIZES[d] for d in spec[0]) + v[1:], bf16)
+        for v, spec in zip(blocks, SPECS)
     ]
-    moved = sum(int(np.prod(o.shape)) for o in outs) * 2
+    total = sum(int(np.prod(o.shape)) for o in outs) * 2
     return pl.pallas_call(
-        functools.partial(gather_kernel, specs),
+        gather_kernel,
         out_shape=outs,
-        in_specs=[pl.BlockSpec(memory_space=pl.ANY)] * n,
+        in_specs=[pl.BlockSpec(memory_space=pltpu.VMEM)] * 5,
         out_specs=[pl.BlockSpec(memory_space=pl.ANY)] * n,
-        scratch_shapes=[
+        scratch_shapes=[pltpu.VMEM(v, bf16) for v in blocks]
+        + [
+            pltpu.VMEM((8, 16, 1152), bf16),
+            pltpu.VMEM((4, 32, 384), bf16),
+            pltpu.VMEM((8, 16, 1152), bf16),
+            pltpu.VMEM((4, 32, 384), bf16),
+            pltpu.SemaphoreType.DMA((12,)),
+            pltpu.SemaphoreType.DMA((12,)),
             pltpu.SemaphoreType.DMA((n, 3, 3, 4)),
             pltpu.SemaphoreType.DMA((n, 3, 3, 4)),
             pltpu.SemaphoreType.DMA((n,)),
         ],
-        compiler_params=pltpu.CompilerParams(collective_id=collective_id, has_side_effects=True),
-        cost_estimate=pl.CostEstimate(flops=0, bytes_accessed=2 * moved, transcendentals=0),
+        compiler_params=pltpu.CompilerParams(
+            collective_id=1, has_side_effects=True, vmem_limit_bytes=60 * 2**20
+        ),
+        cost_estimate=pl.CostEstimate(flops=0, bytes_accessed=2 * total, transcendentals=0),
         name="gather_weights",
-    )(*arrays)
+    )(in_rows, gu_rows, router_rows, rows, vec)
 
 
 def each(lead, fn):
@@ -158,12 +255,15 @@
         fn(tuple(reversed(ix)))
 
 
-def scatter_kernel(specs, *refs):
-    n = len(specs)
-    gs, outs = refs[:n], refs[n : 2 * n]
-    held, got = refs[2 * n : 3 * n], [refs[3 * n + 3 * i : 3 * n + 3 * i + 3] for i in range(n)]
-    send, recv, loc = refs[6 * n :]
+def scatter_kernel(*refs):
+    specs, n = SPECS, len(SPECS)
+    gs, (in_out, router_out, gu_out, out_out, down_out, small_out) = refs[:n], refs[n : n + 6]
+    outs, refs = refs[n + 6 : 2 * n + 6], refs[2 * n + 6 :]
+    held, got = refs[:n], [refs[n + 3 * i : n + 3 * i + 3] for i in range(n)]
+    pin, pout, bin_, bout, other, send0, recv0, send, recv, loc = refs[4 * n :]
     pos, right, left, opp = neighbours()
+    row = chip_row()
+    (core, y) = row[0]
 
     def source(i, st, a, idx, s):
         ax = ORDER[a][2 - st]
@@ -177,7 +277,7 @@
 
     local = {}
     for i in range(n):
-        for a in range(3):
+        for a in cuts(specs[i]):
             ax = ORDER[a][2]
             for k, (idx, s) in enumerate(((right[ax], 0), (left[ax], 1), (pos[ax], 0), (pos[ax], 1))):
                 c = pltpu.make_async_copy(source(i, 0, a, idx, s), held[i].at[a, k], loc.at[i, a, k])
@@ -199,7 +299,7 @@
         sends.append(c)
         return c
 
-    every = [(i, a) for i in range(n) for a in range(3)]
+    every = [(i, a) for i in range(n) for a in cuts(specs[i])]
     for st in range(3):
         lead = ((4, 4), (4,), ())[st]
         cp = {}
@@ -247,31 +347,99 @@
                         acc[ix] = total.astype(acc.dtype)
 
                     each(lead, finish)
+
+    for k in range(8):
+        c, d = divmod(k, 4)
+        pin[k, :12, :896] = outs[0][c, 12 * d : 12 * d + 12, :]
+        pin[k, :12, 896:] = outs[1][c, 12 * d : 12 * d + 12, :]
+    for d in range(4):
+        h, at = divmod(d, 2)
+        pout[d, :24] = outs[2][h, 24 * at : 24 * at + 24, :]
+        pout[d, 24:] = outs[3][h, 8 * at : 8 * at + 8, :]
+    last = []
+
+    def push(src, dst, k, device_id):
+        c = pltpu.make_async_remote_copy(
+            src_ref=src,
+            dst_ref=dst,
+            send_sem=send0.at[k],
+            recv_sem=recv0.at[k],
+            device_id=device_id,
+            device_id_type=MESH_ID,
+        )
+        c.start()
+        sends.append(c)
+        last.append(c)
+
+    for k, (c, d) in enumerate(row):
+        if k:
+            push(pin.at[4 * c + d], bin_.at[4 * core + y], k, {"seq": c, "y": d})
+    for k, (_, d) in enumerate(row[:4]):
+        if k:
+            push(pout.at[d], bout.at[y], 8 + k, {"y": d})
+    push(outs[4].at[1 - core], other, 0, {"seq": 1 - core})
+    bin_[4 * core + y] = pin[4 * core + y]
+    bout[y] = pout[y]
+    for c in last:
+        c.wait_recv()
+    small_out[...] = outs[4][core] + other[...]
+    misc = []
+    for k in range(8):
+        got_k = bin_[k]
+        in_out[:, 384 * k : 384 * k + 384] = got_k[:12, :384]
+        in_out[:, 3072 + 384 * k : 3456 + 384 * k] = got_k[:12, 384:768]
+        gu_out[:, 128 * k : 128 * k + 128] = got_k[:12, 896:1024]
+        gu_out[:, 1024 + 128 * k : 1152 + 128 * k] = got_k[:12, 1024:]
+        misc.append(got_k[:, 768:896])
+    both = [misc[j] + misc[4 + j] for j in range(4)]
+    for h in range(2):
+        pair = moved(both[2 * h], 0, 0, 64) + moved(both[2 * h + 1], 0, 64, 64)
+        in_out[:, 6144 + 128 * h : 6272 + 128 * h] = pair[:12]
+    steps = sum(moved(misc[k], HEAD_AT, 6 * k, 6) for k in range(8))
+    in_out[:, 6400:] = steps[:12, :48]
+    router = sum(moved(both[j], 64, 16 * j, 16) for j in range(4))
+    router_out[...] = router[:12, :64]
+    for j in range(4):
+        out_out[:, 384 * j : 384 * j + 384] = bout[j, :24]
+        down_out[:, 384 * j : 384 * j + 384] = bout[j, 24:]
     for c in sends:
         c.wait_send()
 
 
-def scatter(arrays, specs, collective_id):
+def scatter(arrays):
     n = len(arrays)
-    outs = [jax.ShapeDtypeStruct((2,) + v.shape[4:], f32) for v in arrays]
-    pieces = [third_shape(v.shape, spec[1]) for v, spec in zip(arrays, specs)]
-    moved = sum(int(np.prod(v.shape)) for v in arrays) * 2
+    results = [(12, 6448), (12, 64), (12, 2048), (24, 1536), (8, 1536), (8, 128)]
+    pieces = [(third_shape(v.shape, spec[1]), v.dtype) for v, spec in zip(arrays, SPECS)]
+    cut = [len(cuts(spec)) for spec in SPECS]
+    total = sum(int(np.prod(v.shape)) for v in arrays) * 2
     return pl.pallas_call(
-        functools.partial(scatter_kernel, specs),
-        out_shape=outs,
+        scatter_kernel,
+        out_shape=[jax.ShapeDtypeStruct(v, f32) for v in results],
         in_specs=[pl.BlockSpec(memory_space=pl.ANY)] * n,
-        out_specs=[pl.BlockSpec(memory_space=pltpu.VMEM)] * n,
-        scratch_shapes=[pltpu.VMEM((3, 4, 4, 4) + p, bf16) for p in pieces]
-        + [pltpu.VMEM((3, 6) + lead + p, bf16) for p in pieces for lead in ((4, 4), (4,), ())]
+        out_specs=[pl.BlockSpec(memory_space=pltpu.VMEM)] * len(results),
+        scratch_shapes=[pltpu.VMEM((2,) + v.shape[4:], f32) for v in arrays]
+        + [pltpu.VMEM((k, 4, 4, 4) + p, t) for k, (p, t) in zip(cut, pieces)]
         + [
+            pltpu.VMEM((k, 6) + lead + p, t)
+            for k, (p, t) in zip(cut, pieces)
+            for lead in ((4, 4), (4,), ())
+        ]
+        + [
+            pltpu.VMEM((8, 16, 1152), f32),
+            pltpu.VMEM((4, 32, 384), f32),
+            pltpu.VMEM((8, 16, 1152), f32),
+            pltpu.VMEM((4, 32, 384), f32),
+            pltpu.VMEM((8, 128), f32),
+            pltpu.SemaphoreType.DMA((12,)),
+            pltpu.SemaphoreType.DMA((12,)),
             pltpu.SemaphoreType.DMA((n, 3, 3, 6)),
             pltpu.SemaphoreType.DMA((n, 3, 3, 6)),
             pltpu.SemaphoreType.DMA((n, 3, 4)),
         ],
         compiler_params=pltpu.CompilerParams(
-            collective_id=collective_id, has_side_effects=True, vmem_limit_bytes=56 * 2**20
+            collective_id=2, has_side_effects=True, vmem_limit_bytes=56 * 2**20
         ),
-        cost_estimate=pl.CostEstimate(flops=0, bytes_accessed=2 * moved, transcendentals=0),
+        cost_estimate=pl.CostEstimate(flops=0, bytes_accessed=2 * total, transcendentals=0),
         name="scatter_grads",
     )(*arrays)
 
@@ -324,18 +492,11 @@
     )(rows, grad_rows, gate_up, down, pick)
 
 
-HEAD_AT = 80
-
-
 def split3(v):
     hi = v.astype(bf16)
     rest = v - hi.astype(f32)
     mid = rest.astype(bf16)
     return hi, mid, (rest - mid.astype(f32)).astype(bf16)
-
-
-def roll(v, by, axis):
-    return pltpu.roll(v, by, axis) if by else v
 
 
 def taps_pre(v, marks, w):
@@ -354,10 +515,6 @@
         d_v = d_v + w[3 - d : 4 - d] * roll(masked, 256 - d, 0)
     zero = jnp.zeros((3, v.shape[1]), f32)
     return d_v, jnp.concatenate(d_w + [jnp.sum(d_pre, axis=0, keepdims=True), zero], axis=0)
-
-
-def lanes(shape):
-    return lax.broadcasted_iota(jnp.int32, shape, len(shape) - 1)
 
 
 def joined(first, second):
@@ -707,77 +864,32 @@
 ):
     s = lax.axis_index("seq")
     dp = lax.axis_index(DP)
-    device = s * 64 + dp
     experts, slots = 64, 24
     n_slots = experts * slots
 
-    pieces = []
-    for c in range(2):
-        for j in range(4):
-            at = c * 1536 + j * 384
-            misc = jnp.concatenate(
-                [
-                    in_proj[:, 6144 + j * 64 : 6208 + j * 64],
-                    router[:, j * 16 : j * 16 + 16],
-                    in_proj[:, 6400 + c * 24 + j * 6 : 6406 + c * 24 + j * 6],
-                    jnp.zeros((12, 42), bf16),
-                ],
-                axis=1,
-            )
-            up = 1024 + c * 512 + j * 128
-            pieces.append(
-                jnp.concatenate(
-                    [
-                        in_proj[:, at : at + 384],
-                        in_proj[:, 3072 + at : 3456 + at],
-                        misc,
-                        shared_gate_up[:, up - 1024 : up - 896],
-                        shared_gate_up[:, up : up + 128],
-                    ],
-                    axis=1,
-                )
-            )
-    rows_in = lax.all_to_all(jnp.stack(pieces), ("seq", "y"), 0, 0, tiled=True).reshape(2, 48, 1152)
-    out_rows = jnp.concatenate(
-        [out_proj.reshape(24, 4, 384), shared_down.reshape(8, 4, 384)], axis=0
-    ).transpose(1, 0, 2)
-    out_rows = lax.all_to_all(out_rows, "y", 0, 0, tiled=True)
-    vec = jnp.concatenate(
-        [
-            in_norm,
-            ffn_norm,
-            mixer_norm,
-            conv_weight.T.reshape(-1),
-            conv_bias,
-            jnp.zeros((78,), bf16),
-        ]
-    )
-    vecs = lax.all_to_all(jnp.broadcast_to(vec, (128, 256)), ALL, 0, 0, tiled=True)
+    vec = [in_norm[None], ffn_norm[None], mixer_norm[None], conv_weight.T, conv_bias[None]]
+    vec = jnp.concatenate([jnp.pad(v, ((0, 0), (0, 128 - v.shape[1]))) for v in vec], axis=0)
     other_tokens = swap(tokens)
     other_grad = swap(out_grad)
     other_gate_up = swap(expert_gate_up[0])
     other_down = swap(expert_down[0])
-
-    w_in, w_sgu, w_out, w_sdown = gather(
-        (
-            rows_in[:, :, :896],
-            rows_in[:, :, 896:],
-            out_rows[:, :24].reshape(2, 48, 384),
-            out_rows[:, 24:].reshape(2, 16, 384),
-        ),
-        SPECS,
-        1,
+    w_in, w_sgu, w_out, w_sdown, vecs = gather(
+        jnp.pad(in_proj, ((0, 4), (0, 80))),
+        jnp.pad(shared_gate_up, ((0, 4), (0, 0))),
+        jnp.pad(router, ((0, 4), (0, 64))),
+        jnp.concatenate([out_proj, shared_down], axis=0),
+        jnp.pad(vec, ((0, 8), (0, 0))),
     )
     w_in = w_in.reshape(4, 1536, 896)
     w_sgu = w_sgu.reshape(4, 1536, 256)
     w_out = w_out.reshape(4, 1536, 384)
     w_sdown = w_sdown.reshape(4, 512, 384)
 
-    vecs = vecs.astype(f32)
-    g_in = vecs[:, :12].reshape(1, 1536)
-    g_ffn = vecs[:, 12:24].reshape(1536)
-    g_mix = lax.dynamic_slice_in_dim(vecs[:, 24:48].reshape(1, 3072), s * 1536, 1536, 1)
-    conv = vecs[:, 48:178].reshape(128, 5, 26).transpose(1, 0, 2).reshape(5, 3328)
+    vecs = vecs.reshape(128, 16, 128).astype(f32)
+    g_in = vecs[:, 0, :12].reshape(1, 1536)
+    g_ffn = vecs[:, 1, :12].reshape(1536)
+    g_mix = lax.dynamic_slice_in_dim(vecs[:, 2, :24].reshape(1, 3072), s * 1536, 1536, 1)
+    conv = vecs[:, 3:8, :26].transpose(1, 0, 2).reshape(5, 3328)
     heads = lax.dynamic_slice_in_dim(head_params.astype(f32), s * 24, 24, 1)
     cx = jnp.concatenate(
         [
@@ -870,17 +982,19 @@
     pick = (lane == dp).astype(f32)[None, :]
     d_rows, e_act, w_act, w_gu = expert_grads(arrived, grad_rows, w_eg, w_ed, pick)
     d_back = lax.all_to_all(d_rows.reshape(experts, slots, 1664), DP, 0, 0, tiled=True)
-    d_back = d_back.reshape(n_slots, 1664)
     e_out = dot(e_act, w_ed).astype(bf16)
-    e_out, d_back = lax.optimization_barrier((e_out, d_back))
-    out_back = lax.all_to_all(e_out.reshape(experts, slots, 1536), DP, 0, 0, tiled=True)
-    out_back = out_back.reshape(n_slots, 1536)
     grad_ed = dot(w_act, grad_rows, ((0,), (0,)))
     grad_eg = dot(arrived[:, :1536], w_gu, ((0,), (0,)))
     ge_own, ge_other = halves(grad_eg, s)
     grad_eg = ge_own + swap(ge_other.astype(bf16)).astype(f32)
     gd_own, gd_other = halves(grad_ed, s)
     grad_ed = gd_own + swap(gd_other.astype(bf16)).astype(f32)
+    e_out, d_back, grad_eg, grad_ed, d_ffn = lax.optimization_barrier(
+        (e_out, d_back, grad_eg, grad_ed, d_ffn)
+    )
+    d_back = d_back.reshape(n_slots, 1664)
+    out_back = lax.all_to_all(e_out.reshape(experts, slots, 1536), DP, 0, 0, tiled=True)
+    out_back = out_back.reshape(n_slots, 1536)
 
     wide_gate = dot(gate_hi, spread) + dot(gate_lo, spread)
     weighted = (place.astype(f32) * wide_gate).astype(bf16)
@@ -932,69 +1046,48 @@
         jnp.zeros((128, 24), f32), mixer_norm_grad.reshape(64, 24), (s * 64, 0)
     )
     head_grad = lax.dynamic_update_slice(jnp.zeros((3, 48), f32), head_grad, (0, s * 24))
+    def rows_of(v, width):
+        return jnp.pad(v.reshape(128, 1, width), ((0, 0), (0, 0), (0, 64 - width)))
+
+    conv_grad = conv_grad.reshape(5, 128, 26).transpose(1, 0, 2)
     small = jnp.concatenate(
         [
-            in_norm_grad.reshape(128, 12),
-            ffn_norm_grad.reshape(128, 12),
-            mixer_norm_grad,
-            conv_grad.reshape(5, 128, 26).transpose(1, 0, 2).reshape(128, 130),
-            jnp.broadcast_to(head_grad.reshape(1, 144), (128, 144)),
-            jnp.zeros((128, 62), f32),
+            rows_of(in_norm_grad, 12),
+            rows_of(ffn_norm_grad, 12),
+            rows_of(mixer_norm_grad, 24),
+            jnp.pad(conv_grad, ((0, 0), (0, 0), (0, 38))),
         ],
         axis=1,
     )
-    weighted_late, small, grad_in = lax.optimization_barrier((weighted, small, grad_in))
-    small = jnp.sum(lax.all_to_all(small, ALL, 0, 0, tiled=True), axis=0)
+    head_rows = jnp.broadcast_to(jnp.pad(head_grad, ((0, 5), (0, 16)))[None], (128, 8, 64))
+    small = jnp.concatenate([small, head_rows], axis=2).reshape(2, 4, 4, 4, 8, 128)
+    weighted_late, grad_in = lax.optimization_barrier((weighted, grad_in))
     routed = dot(weighted_late, out_back)
     block_out = (residual + s_out + routed).astype(bf16)
-    sum_in, sum_sgu, sum_out, sum_sdown = scatter(
+    block_out, small = lax.optimization_barrier((block_out, small))
+    in_proj_grad, router_grad, sgu_grad, out_proj_grad, sdown_grad, small = scatter(
         (
             grad_in.reshape(4, 2, 4, 4, 48, 896),
             grad_sgu.reshape(4, 2, 4, 4, 48, 256),
             grad_out.reshape(4, 4, 4, 2, 48, 384),
             grad_sdown.reshape(4, 4, 4, 2, 16, 384),
-        ),
-        SPECS,
-        2,
-    )
-    back = jnp.concatenate([sum_in, sum_sgu], axis=2).reshape(8, 12, 1152)
-    back = lax.all_to_all(back, ("seq", "y"), 0, 0, tiled=True).reshape(2, 4, 12, 1152)
-    back = back.transpose(2, 0, 1, 3)
-    bc_dt = back[..., 768:896]
-    both_cores = bc_dt[:, 0] + bc_dt[:, 1]
-    in_proj_grad = jnp.concatenate(
-        [
-            back[..., :384].reshape(12, 3072),
-            back[..., 384:768].reshape(12, 3072),
-            both_cores[..., :64].reshape(12, 256),
-            bc_dt[..., 80:86].reshape(12, 48),
-        ],
-        axis=1,
-    )
-    router_grad = both_cores[..., 64:80].reshape(12, 64)
-    sgu_grad = jnp.concatenate(
-        [back[..., 896:1024].reshape(12, 1024), back[..., 1024:].reshape(12, 1024)], axis=1
-    )
-    rows_out = jnp.concatenate(
-        [sum_out.reshape(4, 24, 384), sum_sdown.reshape(4, 8, 384)], axis=1
-    )
-    rows_out = lax.all_to_all(rows_out, "y", 0, 0, tiled=True).transpose(1, 0, 2).reshape(32, 1536)
-
-    conv_grad = small[48:178].reshape(5, 26)
+            small,
+        )
+    )
     return (
         block_out,
         token_grad,
-        small[:12],
+        small[0, :12],
         in_proj_grad,
-        conv_grad[:4].T,
-        conv_grad[4],
-        small[178:322].reshape(3, 48),
-        small[24:48],
-        rows_out[:24],
-        small[12:24],
+        small[3:7, :26].T,
+        small[7, :26],
+        small[:3, 64:112],
+        small[2, :24],
+        out_proj_grad,
+        small[1, :12],
         router_grad,
         sgu_grad,
-        rows_out[24:],
+        sdown_grad,
         grad_eg[None],
         grad_ed[None],
     )

time: 658 us -> 558 us (0.85)
  waiting for transfers between devices: 152 us -> 83.7 us
  starting transfers between devices: 66.2 us -> 38.3 us
  Pallas kernels: 246 us -> 273 us
  local copies, waits for them, and re-layouts: 82.9 us -> 63.5 us
    all_to_all x6 -> x0, starting transfers between devices: 31.6 us -> none  [the longest x1 10.2 us: local(): lax.all_to_all(jnp.broadcast_to(vec, (128, 256)), ALL, 0, 0, tiled=True)]
    pallas_call x2, Pallas kernels: 180 us -> 208 us  [the longest x1 107 us: scatter(): pl.pallas_call(scatter_kernel, out_shape=[jax.ShapeDtypeStruct(v, f32) fo...]
    all_to_all x1, waiting for transfers between devices: 33.1 us -> 5.89 us  [local(): lax.all_to_all(e_out.reshape(experts, slots, 1536), DP, 0, 0, tiled=True)]
    all_to_all x6 -> x0, waiting for transfers between devices: 27 us -> none  [the longest x1 8.03 us: local(): small = jnp.sum(lax.all_to_all(small, ALL, 0, 0, tiled=True), axis=0)]
    all_to_all x1, waiting for transfers between devices: 17.5 us -> 0.01 us  [local(): lax.all_to_all(grad_slots, DP, 0, 0, tiled=True).reshape(n_slots, 1536)]
    slice x28 -> x4, local copies, waits for them, and re-layouts: 15.6 us -> 1.52 us  [the longest x1 1.33 us: local(): small[:3, 64:112]]
    broadcast_in_dim x3 -> x0, other arithmetic: 8.41 us -> none  [the longest x1 4.9 us: local(): grad_eg[None]]
    pad x0 -> x10, local copies, waits for them, and re-layouts: none -> 8.38 us  [the longest x5 3.38 us: local(): jnp.pad(v, ((0, 0), (0, 128 - v.shape[1])))]
  transfers between devices with their start and end apart: 24 -> 18, of which waited for: 9 -> 3; matrix products, arithmetic and copies ran while one was open for 22% -> 22% of each run, Pallas kernels for 16% -> 30%
where the time goes in v3:
time: 558 us; the launch traced here: 550 us
  Pallas kernels  273 us (49%)
  waiting for transfers between devices  83.7 us (15%)
  local copies, waits for them, and re-layouts  63.5 us (11%)
  matrix products  52.4 us (9%)
  starting transfers between devices  38.3 us (7%)
  other arithmetic  36.8 us (7%)
    pallas_call x1, Pallas kernels, scatter(): pl.pallas_call(scatter_kernel, out_shape=[jax.ShapeDtypeStruct(v, f32) fo...  107 us
    pallas_call x1, Pallas kernels, gather(): pl.pallas_call(gather_kernel, out_shape=outs, in_specs=[pl.BlockSpec(memo...  101 us
    dot_general x39, matrix products, dot(): return lax.dot_general(a, b, (dims, ((), ())), preferred_element_type=f32)  52.4 us
    all_to_all x1, waiting for transfers between devices, local(): arrived = lax.all_to_all(sent, DP, 0, 0, tiled=True).reshape(n_slots, 1664)  42.5 us
    all_to_all x1, waiting for transfers between devices, local(): lax.all_to_all(d_rows.reshape(experts, slots, 1664), DP, 0, 0, tiled=True)  35.3 us
    pallas_call x1, Pallas kernels, mixer_backward(): pl.pallas_call(backward_kernel, grid=(8,), out_shape=[jax.ShapeDtypeStruc...  30.8 us
    unnamed x176, local copies, waits for them, and re-layouts  18.4 us
    pallas_call x1, Pallas kernels, expert_grads(): pl.pallas_call(expert_kernel, grid=(n // block,), out_shape=[jax.ShapeDty...  18.4 us
  transfers between devices with their start and end apart: 18, of which 3 were waited for; matrix products, arithmetic and copies ran while one was open for 22% of the time, Pallas kernels for 30%

profile of v3, /device:TPU:32, one launch (start us, length us, event | category | flops | bytes accessed | tf_op | source)
XLA Modules:
  0.0 550.3 jit_solution(18277353649207205428)
XLA Ops:
  11.3 3.6 convolution_convert_fusion.2
  15.5 100.8 %gather_weights.1 = (bf16[4,2,4,4,48,896]{5,4,3,2,1,0:T(8,128)(2,1)}, bf16[4,2,4,4,48,256]{5,4,3,2,1,0:T(8,128)(2,1)}, bf16[4,4,4,2,48,384]{5,4,3,2,1,0:T(8,128)...) custom-call(bf16[16,6528]{1,0:T(8,128)(2,1)} %pad.82.in_ref, bf16[16,2048]{1,0:T(8,128)(2,1)} %pad.83.gu_ref, ...), custom_call_target="tpu_custom_call" | custom-call | bytes 41943040 | tf_op jit(solution)/shard_map/gather_weights/pallas_call | solution.py:219
  116.3 7.2 %all-to-all-start = ((bf16[64,24,1536]{2,1,0:T(8,128)(2,1)}), bf16[64,24,1536]{2,1,0:T(8,128)(2,1)}, u32[]{:S(2)}, u32[]{:S(2)}) async-start(bf16[64,24,1536]{2,1,0:T(8,128)(2,1)} %bitcast.256), calls=%async_computation | async-start | bytes 9437184 | tf_op jit(solution)/shard_map/all_to_all | solution.py:925
  126.9 2.3 fusion.98
  129.2 2.3 slice_bitcast_fusion
  132.9 3.6 fusion.97
  138.0 16.3 %mixer_forward.1 = (bf16[256,1536]{1,0:T(8,128)(2,1)S(1)}, bf16[4,256,896]{2,1,0:T(8,128)(2,1)}, f32[4,256,384]{2,1,0:T(8,128)S(1)}, bf16[4,256,384]{2,1,0:T(8,1...) custom-call(bf16[256,1536]{1,0:T(8,128)(2,1)S(1)} %pad_maximum_fusion.6.x_ref, ...), custom_call_target="tpu_custom_call" | custom-call | flops 4026531840 | bytes 23068672 | tf_op jit(solution)/shard_map/mixer_forward/pallas_call | solution.py:622
  173.5 5.0 convolution_convert_fusion.1
  182.4 10.5 %all-to-all-start.1 = ((bf16[64,24,1664]{2,1,0:T(8,128)(2,1)}), bf16[64,24,1664]{2,1,0:T(8,128)(2,1)}, u32[]{:S(2)}, u32[]{:S(2)}) async-start(bf16[64,24,1664]{2,1,0:T(8,128)(2,1)} %bitcast.255), calls=%async_computation.1 | async-start | bytes 10223616 | tf_op jit(solution)/shard_map/all_to_all | solution.py:959
  192.9 1.9 convolution_bitcast_fusion.1
  205.4 2.3 copy.156
  207.9 2.0 fusion.13
  209.9 2.0 fusion.14
  214.7 2.1 broadcast_select_fusion.1
  216.8 2.0 pad_maximum_fusion.gu_ref
  218.7 42.5 %all-to-all-done.1 = bf16[64,24,1664]{2,1,0:T(8,128)(2,1)} async-done(((bf16[64,24,1664]{2,1,0:T(8,128)(2,1)}), bf16[64,24,1664]{2,1,0:T(8,128)(2,1)}, u32[]{:S(2)}, u32[]{:S(2)}) %all-to-all-start.1) | async-done | bytes 5111840 | tf_op jit(solution)/shard_map/all_to_all | solution.py:959
  261.2 18.4 %expert_grads.1 = (bf16[1536,1664]{1,0:T(8,128)(2,1)}, bf16[1536,512]{1,0:T(8,128)(2,1)S(1)}, bf16[1536,512]{1,0:T(8,128)(2,1)S(1)}, bf16[1536,1024]{1,0:T(8,128)(2,1)}) custom-call(bf16[1536,1664]{1,0:T(8,128)(2,1)} %bitcast.44.rows_ref, bf16[1536,1536]{1,0:T(8,128)(2,1)} %bitcast.43.grad_ref, bf16[1536,1024]{1,0:T(8,128)(2,1)} %pad_maximum_fusion.gu_ref, ...), custom_call_target="tpu_custom_call" | custom-call | flops 12079595520 | bytes 27262976 | tf_op jit(solution)/shard_map/expert_grads/pallas_call | solution.py:481
  281.9 7.5 %all-to-all-start.2 = ((bf16[64,24,1664]{2,1,0:T(8,128)(2,1)}), bf16[64,24,1664]{2,1,0:T(8,128)(2,1)}, u32[]{:S(2)}, u32[]{:S(2)}) async-start(bf16[64,24,1664]{2,1,0:T(8,128)(2,1)} %bitcast.281), calls=%async_computation.2 | async-start | bytes 10223616 | tf_op jit(solution)/shard_map/all_to_all | solution.py:984
  289.4 2.0 dynamic-slice_convert_fusion.4
  295.0 4.7 fusion.105
  299.7 7.1 %fusion.2 = f32[1536,1024]{1,0:T(8,128)S(1)} fusion(bf16[1536,1024]{1,0:T(8,128)(2,1)S(1)} %copy-done.84, bf16[1536,1664]{1,0:T(8,128)(2,1)} %bitcast.44.rows_ref), kind=kOutput, calls=%fused_computation.5 | convolution fusion | flops 4831838208 | bytes 14155776 | tf_op jit(solution)/shard_map/dot_general | solution.py:31
  309.3 4.4 convolution_convert_fusion
  315.1 2.2 convert_add_fusion
  317.2 35.3 %all-to-all-done.2 = bf16[64,24,1664]{2,1,0:T(8,128)(2,1)} async-done(((bf16[64,24,1664]{2,1,0:T(8,128)(2,1)}), bf16[64,24,1664]{2,1,0:T(8,128)(2,1)}, u32[]{:S(2)}, u32[]{:S(2)}) %all-to-all-start.2) | async-done | bytes 5111840 | tf_op jit(solution)/shard_map/all_to_all | solution.py:984
  355.1 3.2 fusion
  359.4 8.3 %all-to-all-start.3 = ((bf16[64,24,1536]{2,1,0:T(8,128)(2,1)}), bf16[64,24,1536]{2,1,0:T(8,128)(2,1)}, u32[]{:S(2)}, u32[]{:S(2)}) async-start(bf16[64,24,1536]{2,1,0:T(8,128)(2,1)} %bitcast.283), calls=%async_computation.3 | async-start | bytes 9437184 | tf_op jit(solution)/shard_map/all_to_all | solution.py:996
  367.7 2.8 multiply_reduce_fusion.1
  372.6 2.6 pad_maximum_fusion.4.refs_3_
  378.0 30.8 %mixer_backward.1 = (bf16[4,1536,384]{2,1,0:T(8,128)(2,1)}, bf16[4,1536,896]{2,1,0:T(8,128)(2,1)}, f32[256,1536]{1,0:T(8,128)}, f32[4,8,384]{2,1,0:T(8,128)}, f3...) custom-call(bf16[256,1536]{1,0:T(8,128)(2,1)} %pad_maximum_fusion.9.dm_ref, f32[256,1]{1,0:T(8,128)} %pad_maximum_fusion.11.kappa_ref, ...), custom_call_target="tpu_custom_call" | custom-call | flops 8053063680 | bytes 41943040 | tf_op jit(solution)/shard_map/mixer_backward/pallas_call | solution.py:784
  419.0 5.9 %all-to-all-done.3 = bf16[64,24,1536]{2,1,0:T(8,128)(2,1)} async-done(((bf16[64,24,1536]{2,1,0:T(8,128)(2,1)}), bf16[64,24,1536]{2,1,0:T(8,128)(2,1)}, u32[]{:S(2)}, u32[]{:S(2)}) %all-to-all-start.3) | async-done | bytes 4718624 | tf_op jit(solution)/shard_map/all_to_all | solution.py:996
  424.9 4.2 add_convert_fusion
  429.1 107.1 %scatter_grads.1 = (f32[12,6448]{1,0:T(8,128)}, f32[12,64]{1,0:T(8,128)}, f32[12,2048]{1,0:T(8,128)}, f32[24,1536]{1,0:T(8,128)}, f32[8,1536]{1,0:T(8,128)}, /*index=5*/f32[8,128]{1,0:T(8,128)}) custom-call(bf16[4,2,4,4,48,896]{5,4,3,2,1,0:T(8,128)(2,1)} %bitcast.272, bf16[4,2,4,4,48,256]{5,4,3,2,1,0:T(8,128)(2,1)} %pad_maximum_fusion.1.refs_1_, ...), custom_call_target="tpu_custom_call" | custom-call | bytes 41418752 | tf_op jit(solution)/shard_map/scatter_grads/pallas_call | solution.py:415
  (359 shorter events, 95.5 us)
Async XLA Ops:
  0.6 135.9 %collective-permute-start = (bf16[128,1536]{1,0:T(8,128)(2,1)}, bf16[128,1536]{1,0:T(8,128)(2,1)}, u32[]{:S(2)}, u32[]{:S(2)}) collective-permute-start(bf16[128,1536]{1,0:T(8,128)(2,1)} %param.17), channel_id=1, source_target_pairs={{0,64},{64,0},{1,65},{65,1},{2,66},{66,2},{3,67},{67,3},{4,68},{68... | collective-permute-start | bytes 1179656 | tf_op jit(solution)/shard_map/ppermute | solution.py:815
  0.7 135.8 %collective-permute-start.9 = (bf16[128,1536]{1,0:T(8,128)(2,1)}, bf16[128,1536]{1,0:T(8,128)(2,1)}, u32[]{:S(2)}, u32[]{:S(2)}) collective-permute-start(bf16[128,1536]{1,0:T(8,128)(2,1)} %param.18), channel_id=1, source_target_pairs={{0,64},{64,0},{1,65},{65,1},{2,66},{66,2},{3,67},{67,3},{4,68},{68... | collective-permute-start | bytes 1179656 | tf_op jit(solution)/shard_map/ppermute | solution.py:815
  1.2 10.0 %copy-start.72 = (s32[1536]{0:T(1024)}, s32[1536]{0:T(1024)S(1)}, u32[]{:S(2)}) copy-start(s32[1536]{0:T(1024)S(1)} %get-tuple-element.156) | copy-start | bytes 18436
  116.3 66.1 %all-to-all-start = ((bf16[64,24,1536]{2,1,0:T(8,128)(2,1)}), bf16[64,24,1536]{2,1,0:T(8,128)(2,1)}, u32[]{:S(2)}, u32[]{:S(2)}) async-start(bf16[64,24,1536]{2,1,0:T(8,128)(2,1)} %bitcast.256), calls=%async_computation | async-start | bytes 9437184 | tf_op jit(solution)/shard_map/all_to_all | solution.py:925
  123.4 37.3 %collective-permute-start.6 = (bf16[256,1536]{1,0:T(8,128)(2,1)}, bf16[256,1536]{1,0:T(8,128)(2,1)}, u32[]{:S(2)}, u32[]{:S(2)}) collective-permute-start(bf16[256,1536]{1,0:T(8,128)(2,1)} %bitcast.46), channel_id=1, source_target_pairs={{0,64},{64,0},{1,65},{65,1},{2,66},{66,2},{3,67},{67,3},{4,68},{68... | collective-permute-start | bytes 2359304 | tf_op jit(solution)/shard_map/ppermute | solution.py:815
  123.5 91.1 %collective-permute-start.5 = (bf16[768,1024]{1,0:T(8,128)(2,1)}, bf16[768,1024]{1,0:T(8,128)(2,1)}, u32[]{:S(2)}, u32[]{:S(2)}) collective-permute-start(bf16[768,1024]{1,0:T(8,128)(2,1)} %bitcast.45), channel_id=1, source_target_pairs={{0,64},{64,0},{1,65},{65,1},{2,66},{66,2},{3,67},{67,3},{4,68},{68... | collective-permute-start | bytes 4718600 | tf_op jit(solution)/shard_map/ppermute | solution.py:815
  126.6 11.3 %copy-start.2 = (f32[4,8,128]{2,1,0:T(8,128)}, f32[4,8,128]{2,1,0:T(8,128)S(1)}, u32[]{:S(2)}) copy-start(f32[4,8,128]{2,1,0:T(8,128)S(1)} %pad.92.hp_ref) | copy-start | bytes 49156
  126.7 11.3 %copy-start = (f32[256,128]{1,0:T(8,128)}, f32[256,128]{1,0:T(8,128)S(1)}, u32[]{:S(2)}) copy-start(f32[256,128]{1,0:T(8,128)S(1)} %pad.96.marks_ref) | copy-start | bytes 393220
  126.8 11.1 %copy-start.70 = (f32[1536]{0:T(1024)}, f32[1536]{0:T(1024)S(1)}, u32[]{:S(2)}) copy-start(f32[1536]{0:T(1024)S(1)} %broadcast_in_dim.89) | copy-start | bytes 18436
  126.8 11.1 %copy-start.3 = (f32[2,8,128]{2,1,0:T(8,128)}, f32[2,8,128]{2,1,0:T(8,128)S(1)}, u32[]{:S(2)}) copy-start(f32[2,8,128]{2,1,0:T(8,128)S(1)} %pad_bitcast_fusion.cbc_ref) | copy-start | bytes 24580
  129.2 28.6 %copy-start.33 = (bf16[1,4,4,2,16,384]{5,4,3,2,1,0:T(8,128)(2,1)}, bf16[1,4,4,2,16,384]{5,4,3,2,1,0:T(8,128)(2,1)S(1)}, u32[]{:S(2)}) copy-start(bf16[1,4,4,2,16,384]{5,4,3,2,1,0:T(8,128)(2,1)S(1)} %get-tuple-element.125) | copy-start | bytes 1179652
  129.2 28.9 %copy-start.31 = (bf16[1,4,4,2,16,384]{5,4,3,2,1,0:T(8,128)(2,1)}, bf16[1,4,4,2,16,384]{5,4,3,2,1,0:T(8,128)(2,1)S(1)}, u32[]{:S(2)}) copy-start(bf16[1,4,4,2,16,384]{5,4,3,2,1,0:T(8,128)(2,1)S(1)} %get-tuple-element.124) | copy-start | bytes 1179652
  129.2 29.3 %copy-start.29 = (bf16[1,4,4,2,16,384]{5,4,3,2,1,0:T(8,128)(2,1)}, bf16[1,4,4,2,16,384]{5,4,3,2,1,0:T(8,128)(2,1)S(1)}, u32[]{:S(2)}) copy-start(bf16[1,4,4,2,16,384]{5,4,3,2,1,0:T(8,128)(2,1)S(1)} %get-tuple-element.123) | copy-start | bytes 1179652
  138.0 16.3 %copy-start.4 = (f32[8,256]{1,0:T(8,128)}, f32[8,256]{1,0:T(8,128)S(1)}, u32[]{:S(2)}) copy-start(f32[8,256]{1,0:T(8,128)S(1)} %broadcast_in_dim.95.seg_ref) | copy-start | bytes 24580
  155.0 4.8 collective-permute-start.1
  156.2 7.3 %collective-permute-start.2 = (f32[128,1536]{1,0:T(8,128)}, f32[128,1536]{1,0:T(8,128)}, u32[]{:S(2)}, u32[]{:S(2)}) collective-permute-start(f32[128,1536]{1,0:T(8,128)} %constant_dynamic-slice_fusion), channel_id=1, source_target_pairs={{0,64},{64,0},{1,65},{65,1},{2,66},{66,2},{3,67},{67,3},{4,68},{68... | collective-permute-start | bytes 2359304 | tf_op jit(solution)/shard_map/ppermute | solution.py:815
  166.5 12.0 %collective-permute-start.3 = (bf16[128,1536]{1,0:T(8,128)(2,1)}, bf16[128,1536]{1,0:T(8,128)(2,1)}, u32[]{:S(2)}, u32[]{:S(2)}) collective-permute-start(bf16[128,1536]{1,0:T(8,128)(2,1)} %multiply_convert_fusion.1.ffn_ref), channel_id=1, source_target_pairs={{0,64},{64,0},{1,65},{65,1},{2,66},{66,2},{3,67},{67,3},{4,68},{68... | collective-permute-start | bytes 1179656 | tf_op jit(solution)/shard_map/ppermute | solution.py:815
  182.4 78.8 %all-to-all-start.1 = ((bf16[64,24,1664]{2,1,0:T(8,128)(2,1)}), bf16[64,24,1664]{2,1,0:T(8,128)(2,1)}, u32[]{:S(2)}, u32[]{:S(2)}) async-start(bf16[64,24,1664]{2,1,0:T(8,128)(2,1)} %bitcast.255), calls=%async_computation.1 | async-start | bytes 10223616 | tf_op jit(solution)/shard_map/all_to_all | solution.py:959
  207.7 100.5 %collective-permute-start.10 = (bf16[128,1536]{1,0:T(8,128)(2,1)}, bf16[128,1536]{1,0:T(8,128)(2,1)}, u32[]{:S(2)}, u32[]{:S(2)}) collective-permute-start(bf16[128,1536]{1,0:T(8,128)(2,1)} %dynamic-slice_convert_fusion.3), channel_id=1, source_target_pairs={{0,64},{64,0},{1,65},{65,1},{2,66},{66,2},{3,67},{67,3},{4,68},{68... | collective-permute-start | bytes 1179656 | tf_op jit(solution)/shard_map/ppermute | solution.py:815
  281.9 9.5 %copy-start.15 = (bf16[1536,256]{1,0:T(8,128)(2,1)S(1)}, bf16[1536,256]{1,0:T(8,128)(2,1)}, u32[]{:S(2)}) copy-start(bf16[1536,256]{1,0:T(8,128)(2,1)} %copy.156) | copy-start | bytes 2359300
  281.9 9.5 %copy-start.64 = (bf16[1,256,256]{1,2,0:T(8,128)(2,1)S(1)}, bf16[1,256,256]{1,2,0:T(8,128)(2,1)}, u32[]{:S(2)}) copy-start(bf16[1,256,256]{1,2,0:T(8,128)(2,1)} %copy-done.63) | copy-start | bytes 393220
  281.9 70.6 %all-to-all-start.2 = ((bf16[64,24,1664]{2,1,0:T(8,128)(2,1)}), bf16[64,24,1664]{2,1,0:T(8,128)(2,1)}, u32[]{:S(2)}, u32[]{:S(2)}) async-start(bf16[64,24,1664]{2,1,0:T(8,128)(2,1)} %bitcast.281), calls=%async_computation.2 | async-start | bytes 10223616 | tf_op jit(solution)/shard_map/all_to_all | solution.py:984
  291.3 127.7 %collective-permute-start.4 = (bf16[128,1536]{1,0:T(8,128)(2,1)}, bf16[128,1536]{1,0:T(8,128)(2,1)}, u32[]{:S(2)}, u32[]{:S(2)}) collective-permute-start(bf16[128,1536]{1,0:T(8,128)(2,1)} %dynamic-slice_convert_fusion.4), channel_id=1, source_target_pairs={{0,64},{64,0},{1,65},{65,1},{2,66},{66,2},{3,67},{67,3},{4,68},{68... | collective-permute-start | bytes 1179656 | tf_op jit(solution)/shard_map/ppermute | solution.py:815
  307.1 8.0 %collective-permute-start.7 = (bf16[768,1024]{1,0:T(8,128)(2,1)S(1)}, bf16[768,1024]{1,0:T(8,128)(2,1)S(1)}, u32[]{:S(2)}, u32[]{:S(2)}) collective-permute-start(bf16[768,1024]{1,0:T(8,128)(2,1)S(1)} %dynamic-slice_convert_fusion), channel_id=1, source_target_pairs={{0,64},{64,0},{1,65},{65,1},{2,66},{66,2},{3,67},{67,3},{4,68},{68... | collective-permute-start | bytes 4718600 | tf_op jit(solution)/shard_map/ppermute | solution.py:815
  307.7 6.0 %collective-permute-start.8 = (bf16[256,1536]{1,0:T(8,128)(2,1)S(1)}, bf16[256,1536]{1,0:T(8,128)(2,1)S(1)}, u32[]{:S(2)}, u32[]{:S(2)}) collective-permute-start(bf16[256,1536]{1,0:T(8,128)(2,1)S(1)} %dynamic-slice_convert_fusion.1), channel_id=1, source_target_pairs={{0,64},{64,0},{1,65},{65,1},{2,66},{66,2},{3,67},{67,3},{4,68},{68... | collective-permute-start | bytes 2359304 | tf_op jit(solution)/shard_map/ppermute | solution.py:815
  317.2 36.8 %copy-start.54 = (pred[128,1536]{1,0:T(32,128)(4,1)S(1)}, pred[128,1536]{1,0:T(32,128)(4,1)}, u32[]{:S(2)}) copy-start(pred[128,1536]{1,0:T(32,128)(4,1)} %copy-done.52) | copy-start | bytes 589828
  317.2 36.8 %copy-start.74 = (s32[1536]{0:T(1024)S(1)}, s32[1536]{0:T(1024)}, u32[]{:S(2)}) copy-start(s32[1536]{0:T(1024)} %copy-done.72) | copy-start | bytes 18436
  317.2 37.1 %copy-start.68 = (f32[128,64]{1,0:T(8,128)S(1)}, f32[128,64]{1,0:T(8,128)}, u32[]{:S(2)}) copy-start(f32[128,64]{1,0:T(8,128)} %get-tuple-element.112) | copy-start | bytes 98308
  359.4 65.5 %all-to-all-start.3 = ((bf16[64,24,1536]{2,1,0:T(8,128)(2,1)}), bf16[64,24,1536]{2,1,0:T(8,128)(2,1)}, u32[]{:S(2)}, u32[]{:S(2)}) async-start(bf16[64,24,1536]{2,1,0:T(8,128)(2,1)} %bitcast.283), calls=%async_computation.3 | async-start | bytes 9437184 | tf_op jit(solution)/shard_map/all_to_all | solution.py:996
  371.5 4.8 collective-permute-start.12
  371.6 5.4 collective-permute-start.11
  412.0 2.5 collective-permute-start.13
  (71 other events, 212.1 us)

commit v4 on v3

--- a/solution.py
+++ b/solution.py
@@ -55,7 +55,10 @@
         signal({a: left[a]})
     for core, y in chip_row()[1:]:
         signal({"seq": core, "y": y})
-    pl.semaphore_wait(barrier, 11)
+
+
+def met(count):
+    pl.semaphore_wait(pltpu.get_barrier_semaphore(), count)
 
 
 def cuts(spec):
@@ -101,15 +104,24 @@
     return jnp.where((lane >= to) & (lane < to + width), roll(v, to - at, 1), 0.0)
 
 
-def gather_kernel(in_ref, gu_ref, router_ref, rows_ref, vec_ref, *refs):
+def gather_kernel(in_ref, gu_ref, router_ref, rows_ref, *refs):
     specs, n = SPECS, len(SPECS)
-    outs, blocks = refs[:n], refs[n : 2 * n]
-    pin, pout, bin_, bout, send0, recv0, send, recv, loc = refs[2 * n :]
+    vec_refs, outs, blocks = refs[:5], refs[5 : 5 + n], refs[5 + n : 5 + 2 * n]
+    pin, pout, bin_, bout, wide, vec, send0, recv0, send, recv, loc = refs[5 + 2 * n :]
     pos, right, left, opp = neighbours()
     row = chip_row()
     (core, y) = row[0]
+    greet(right, left)
+    wide[...] = jnp.zeros_like(wide)
+    wide[0, :12, :48] = in_ref[:, 6400:].astype(f32)
+    wide[1, :12, :64] = router_ref[...].astype(f32)
+    at = 0
+    for v in vec_refs:
+        wide[2, at : at + v.shape[0], : v.shape[1]] = v[...].astype(f32)
+        at += v.shape[0]
+    vec[...] = wide[2].astype(bf16)
     bc = [in_ref[:, 6144 + 128 * k : 6272 + 128 * k].astype(f32) for k in range(2)]
-    router, steps = router_ref[...].astype(f32), in_ref[:, 6400:6528].astype(f32)
+    steps, router = wide[0, :12], wide[1, :12]
     for c in range(2):
         for j in range(4):
             k, at = 4 * c + j, c * 1536 + j * 384
@@ -118,14 +130,14 @@
                 + moved(router, 16 * j, 64, 16)
                 + moved(steps, 24 * c + 6 * j, HEAD_AT, 6)
             )
-            pin[k, :, :384] = in_ref[:, at : at + 384]
-            pin[k, :, 384:768] = in_ref[:, 3072 + at : 3456 + at]
-            pin[k, :, 768:896] = misc.astype(bf16)
-            pin[k, :, 896:1024] = gu_ref[:, 128 * k : 128 * k + 128]
-            pin[k, :, 1024:] = gu_ref[:, 1024 + 128 * k : 1152 + 128 * k]
+            pin[k, :12, :384] = in_ref[:, at : at + 384]
+            pin[k, :12, 384:768] = in_ref[:, 3072 + at : 3456 + at]
+            pin[k, :12, 768:896] = misc.astype(bf16)
+            pin[k, :12, 896:1024] = gu_ref[:, 128 * k : 128 * k + 128]
+            pin[k, :12, 1024:] = gu_ref[:, 1024 + 128 * k : 1152 + 128 * k]
     for j in range(4):
         pout[j] = rows_ref[:, 384 * j : 384 * j + 384]
-    greet(right, left)
+    met(11)
     sends, first = [], []
 
     def push(src, dst, k, device_id):
@@ -147,8 +159,8 @@
     for k, (_, d) in enumerate(row[:4]):
         if k:
             push(pout.at[d], bout.at[y], 8 + k, {"y": d})
-    push(vec_ref, blocks[4].at[core], 0, {"seq": 1 - core})
-    blocks[4][core] = vec_ref[...]
+    push(vec, blocks[4].at[core], 0, {"seq": 1 - core})
+    blocks[4][core] = vec[...]
     bin_[4 * core + y] = pin[4 * core + y]
     bout[y] = pout[y]
     for c in first:
@@ -183,32 +195,38 @@
         return c
 
     every = [(i, a) for i in range(n) for a in cuts(specs[i])]
+    first, later = {}, {}
+
+    def begin(i, a, st):
+        ax, free = ORDER[a][st], ORDER[a][:st]
+        dst = region(outs[i], specs[i], free, pos, a)
+        src = dst
+        if st == 0:
+            src = blocks[i].at[(slice(None),) + third(blocks[i].shape, specs[i][1], a)]
+        for d, to in enumerate((right[ax], left[ax])):
+            first[i, a, d] = remote(i, st, a, d, src, dst, ax, to)
+
+    for i, a in every:
+        begin(i, a, 0)
+    for c in own:
+        c.wait()
     for st in range(3):
-        first, later = {}, []
-        for i, a in every:
-            ax, free = ORDER[a][st], ORDER[a][:st]
-            dst = region(outs[i], specs[i], free, pos, a)
-            src = dst
-            if st == 0:
-                src = blocks[i].at[(slice(None),) + third(blocks[i].shape, specs[i][1], a)]
-            for d, to in enumerate((right[ax], left[ax])):
-                first[i, a, d] = remote(i, st, a, d, src, dst, ax, to)
         for i, a in every:
             ax, free = ORDER[a][st], ORDER[a][:st]
             for d, (to, frm) in enumerate(((right[ax], left[ax]), (left[ax], right[ax]))):
                 first[i, a, d].wait_recv()
                 r = region(outs[i], specs[i], free, {**pos, ax: frm}, a, s=d)
-                later.append(remote(i, st, a, 2 + d, r, r, ax, to))
-        for c in later:
-            c.wait_recv()
-        if st == 0:
-            for c in own:
-                c.wait()
+                later[i, a, d] = remote(i, st, a, 2 + d, r, r, ax, to)
+        for i, a in every:
+            for d in range(2):
+                later[i, a, d].wait_recv()
+            if st < 2:
+                begin(i, a, st + 1)
     for c in sends:
         c.wait_send()
 
 
-def gather(in_rows, gu_rows, router_rows, rows, vec):
+def gather(in_proj, gate_up, router, rows, vectors):
     n = len(SPECS)
     blocks = [(2, 48, 896), (2, 48, 256), (2, 48, 384), (2, 16, 384), (2, 16, 128)]
     outs = [
@@ -219,7 +237,7 @@
     return pl.pallas_call(
         gather_kernel,
         out_shape=outs,
-        in_specs=[pl.BlockSpec(memory_space=pltpu.VMEM)] * 5,
+        in_specs=[pl.BlockSpec(memory_space=pltpu.VMEM)] * 9,
         out_specs=[pl.BlockSpec(memory_space=pl.ANY)] * n,
         scratch_shapes=[pltpu.VMEM(v, bf16) for v in blocks]
         + [
@@ -227,6 +245,8 @@
             pltpu.VMEM((4, 32, 384), bf16),
             pltpu.VMEM((8, 16, 1152), bf16),
             pltpu.VMEM((4, 32, 384), bf16),
+            pltpu.VMEM((3, 16, 128), f32),
+            pltpu.VMEM((16, 128), bf16),
             pltpu.SemaphoreType.DMA((12,)),
             pltpu.SemaphoreType.DMA((12,)),
             pltpu.SemaphoreType.DMA((n, 3, 3, 4)),
@@ -238,7 +258,7 @@
         ),
         cost_estimate=pl.CostEstimate(flops=0, bytes_accessed=2 * total, transcendentals=0),
         name="gather_weights",
-    )(in_rows, gu_rows, router_rows, rows, vec)
+    )(in_proj, gate_up, router, rows, *vectors)
 
 
 def each(lead, fn):
@@ -257,10 +277,10 @@
 
 def scatter_kernel(*refs):
     specs, n = SPECS, len(SPECS)
-    gs, (in_out, router_out, gu_out, out_out, down_out, small_out) = refs[:n], refs[n : n + 6]
-    outs, refs = refs[n + 6 : 2 * n + 6], refs[2 * n + 6 :]
+    gs, (bin_, bout, small_out) = refs[:n], refs[n : n + 3]
+    outs, refs = refs[n + 3 : 2 * n + 3], refs[2 * n + 3 :]
     held, got = refs[:n], [refs[n + 3 * i : n + 3 * i + 3] for i in range(n)]
-    pin, pout, bin_, bout, other, send0, recv0, send, recv, loc = refs[4 * n :]
+    pin, pout, other, send0, recv0, send, recv, loc = refs[4 * n :]
     pos, right, left, opp = neighbours()
     row = chip_row()
     (core, y) = row[0]
@@ -284,6 +304,7 @@
                 c.start()
                 local[i, a, k] = c
     greet(right, left)
+    met(11)
     sends = []
 
     def remote(i, st, a, k, src, ax, to):
@@ -300,17 +321,19 @@
         return c
 
     every = [(i, a) for i in range(n) for a in cuts(specs[i])]
+    cp = {}
+
+    def begin(i, a, st):
+        ax = ORDER[a][2 - st]
+        cp[i, a, 0] = remote(i, st, a, 0, source(i, st, a, opp[ax], 0), ax, right[ax])
+        cp[i, a, 1] = remote(i, st, a, 1, source(i, st, a, opp[ax], 1), ax, left[ax])
+        cp[i, a, 2] = remote(i, st, a, 2, source(i, st, a, right[ax], 1), ax, right[ax])
+        cp[i, a, 3] = remote(i, st, a, 3, source(i, st, a, left[ax], 0), ax, left[ax])
+
+    for i, a in every:
+        begin(i, a, 0)
     for st in range(3):
         lead = ((4, 4), (4,), ())[st]
-        cp = {}
-        for i, a in every:
-            ax = ORDER[a][2 - st]
-            cp[i, a, 0] = remote(i, st, a, 0, source(i, st, a, opp[ax], 0), ax, right[ax])
-            cp[i, a, 1] = remote(i, st, a, 1, source(i, st, a, opp[ax], 1), ax, left[ax])
-        for i, a in every:
-            ax = ORDER[a][2 - st]
-            cp[i, a, 2] = remote(i, st, a, 2, source(i, st, a, right[ax], 1), ax, right[ax])
-            cp[i, a, 3] = remote(i, st, a, 3, source(i, st, a, left[ax], 0), ax, left[ax])
         for i, a in every:
             ax = ORDER[a][2 - st]
             for d, to in enumerate((right[ax], left[ax])):
@@ -342,11 +365,13 @@
                     outs[i][ix] = acc[...].astype(f32) + one[...].astype(f32) + two[...].astype(f32)
                 else:
 
-                    def finish(ix, acc=acc, one=one, two=two):
+                    def close(ix, acc=acc, one=one, two=two):
                         total = acc[ix].astype(f32) + one[ix].astype(f32) + two[ix].astype(f32)
                         acc[ix] = total.astype(acc.dtype)
 
-                    each(lead, finish)
+                    each(lead, close)
+            if st < 2:
+                begin(i, a, st + 1)
 
     for k in range(8):
         c, d = divmod(k, 4)
@@ -383,6 +408,11 @@
     for c in last:
         c.wait_recv()
     small_out[...] = outs[4][core] + other[...]
+    for c in sends:
+        c.wait_send()
+
+
+def finish_kernel(bin_, bout, small, in_out, router_out, gu_out, out_out, down_out, heads_out, taps_out, *vecs):
     misc = []
     for k in range(8):
         got_k = bin_[k]
@@ -402,13 +432,27 @@
     for j in range(4):
         out_out[:, 384 * j : 384 * j + 384] = bout[j, :24]
         down_out[:, 384 * j : 384 * j + 384] = bout[j, 24:]
-    for c in sends:
-        c.wait_send()
+    heads_out[...] = moved(small[...], 64, 0, 48)[:3, :48]
+    taps_out[...] = jnp.concatenate([small[...]] * 16, axis=0).T[:26, 3:7]
+    for v, at in zip(vecs, (0, 1, 2, 7)):
+        v[...] = small[at : at + 1, : v.shape[1]]
+
+
+def finish(bin_, bout, small):
+    results = [(12, 6448), (12, 64), (12, 2048), (24, 1536), (8, 1536), (3, 48), (26, 4)]
+    results += [(1, 12), (1, 12), (1, 24), (1, 26)]
+    return pl.pallas_call(
+        finish_kernel,
+        out_shape=[jax.ShapeDtypeStruct(v, f32) for v in results],
+        in_specs=[pl.BlockSpec(memory_space=pltpu.VMEM)] * 3,
+        out_specs=[pl.BlockSpec(memory_space=pltpu.VMEM)] * len(results),
+        name="finish_grads",
+    )(bin_, bout, small)
 
 
 def scatter(arrays):
     n = len(arrays)
-    results = [(12, 6448), (12, 64), (12, 2048), (24, 1536), (8, 1536), (8, 128)]
+    results = [(8, 16, 1152), (4, 32, 384), (8, 128)]
     pieces = [(third_shape(v.shape, spec[1]), v.dtype) for v, spec in zip(arrays, SPECS)]
     cut = [len(cuts(spec)) for spec in SPECS]
     total = sum(int(np.prod(v.shape)) for v in arrays) * 2
@@ -425,8 +469,6 @@
             for lead in ((4, 4), (4,), ())
         ]
         + [
-            pltpu.VMEM((8, 16, 1152), f32),
-            pltpu.VMEM((4, 32, 384), f32),
             pltpu.VMEM((8, 16, 1152), f32),
             pltpu.VMEM((4, 32, 384), f32),
             pltpu.VMEM((8, 128), f32),
@@ -469,7 +511,7 @@
 
 
 def expert_grads(rows, grad_rows, gate_up, down, pick):
-    n, block = rows.shape[0], 256
+    n, block = rows.shape[0], 512
     widths = (1664, 512, 512, 1024)
 
     def blocked(w):
@@ -867,18 +909,16 @@
     experts, slots = 64, 24
     n_slots = experts * slots
 
-    vec = [in_norm[None], ffn_norm[None], mixer_norm[None], conv_weight.T, conv_bias[None]]
-    vec = jnp.concatenate([jnp.pad(v, ((0, 0), (0, 128 - v.shape[1]))) for v in vec], axis=0)
     other_tokens = swap(tokens)
     other_grad = swap(out_grad)
     other_gate_up = swap(expert_gate_up[0])
     other_down = swap(expert_down[0])
     w_in, w_sgu, w_out, w_sdown, vecs = gather(
-        jnp.pad(in_proj, ((0, 4), (0, 80))),
-        jnp.pad(shared_gate_up, ((0, 4), (0, 0))),
-        jnp.pad(router, ((0, 4), (0, 64))),
+        in_proj,
+        shared_gate_up,
+        router,
         jnp.concatenate([out_proj, shared_down], axis=0),
-        jnp.pad(vec, ((0, 8), (0, 0))),
+        (in_norm[None], ffn_norm[None], mixer_norm[None], conv_weight.T, conv_bias[None]),
     )
     w_in = w_in.reshape(4, 1536, 896)
     w_sgu = w_sgu.reshape(4, 1536, 256)
@@ -1065,7 +1105,7 @@
     routed = dot(weighted_late, out_back)
     block_out = (residual + s_out + routed).astype(bf16)
     block_out, small = lax.optimization_barrier((block_out, small))
-    in_proj_grad, router_grad, sgu_grad, out_proj_grad, sdown_grad, small = scatter(
+    sums = scatter(
         (
             grad_in.reshape(4, 2, 4, 4, 48, 896),
             grad_sgu.reshape(4, 2, 4, 4, 48, 256),
@@ -1074,17 +1114,21 @@
             small,
         )
     )
+    (
+        in_proj_grad, router_grad, sgu_grad, out_proj_grad, sdown_grad, head_grad, conv_grad,
+        in_norm_grad, ffn_norm_grad, mixer_norm_grad, conv_bias_grad,
+    ) = finish(*sums)
     return (
         block_out,
         token_grad,
-        small[0, :12],
+        in_norm_grad[0],
         in_proj_grad,
-        small[3:7, :26].T,
-        small[7, :26],
-        small[:3, 64:112],
-        small[2, :24],
+        conv_grad,
+        conv_bias_grad[0],
+        head_grad,
+        mixer_norm_grad[0],
         out_proj_grad,
-        small[1, :12],
+        ffn_norm_grad[0],
         router_grad,
         sgu_grad,
         sdown_grad,

time: 558 us -> 533 us (0.955)
  local copies, waits for them, and re-layouts: 63.5 us -> 42.6 us
    pad x9 -> x0, local copies, waits for them, and re-layouts: 8.38 us -> none  [the longest x5 3.38 us: local(): jnp.pad(v, ((0, 0), (0, 128 - v.shape[1])))]
    unnamed x176 -> x172, local copies, waits for them, and re-layouts: 18.4 us -> 12.2 us
  transfers between devices with their start and end apart: 18 -> 18, of which waited for: 3 -> 3; matrix products, arithmetic and copies ran while one was open for 22% -> 22% of each run, Pallas kernels for 30% -> 31%
where the time goes in v4:
time: 533 us; the launch traced here: 525 us
  Pallas kernels  268 us (50%)
  waiting for transfers between devices  83.8 us (16%)
  matrix products  52.4 us (10%)
  local copies, waits for them, and re-layouts  42.6 us (8%)
  starting transfers between devices  38.6 us (7%)
  other arithmetic  36.8 us (7%)
    pallas_call x1, Pallas kernels, scatter(): pl.pallas_call(scatter_kernel, out_shape=[jax.ShapeDtypeStruct(v, f32) fo...  102 us
    pallas_call x1, Pallas kernels, gather(): pl.pallas_call(gather_kernel, out_shape=outs, in_specs=[pl.BlockSpec(memo...  97.9 us
    dot_general x39, matrix products, dot(): return lax.dot_general(a, b, (dims, ((), ())), preferred_element_type=f32)  52.4 us
    all_to_all x1, waiting for transfers between devices, local(): arrived = lax.all_to_all(sent, DP, 0, 0, tiled=True).reshape(n_slots, 1664)  42.4 us
    all_to_all x1, waiting for transfers between devices, local(): lax.all_to_all(d_rows.reshape(experts, slots, 1664), DP, 0, 0, tiled=True)  35.3 us
    pallas_call x1, Pallas kernels, mixer_backward(): pl.pallas_call(backward_kernel, grid=(8,), out_shape=[jax.ShapeDtypeStruc...  30.8 us
    pallas_call x1, Pallas kernels, expert_grads(): pl.pallas_call(expert_kernel, grid=(n // block,), out_shape=[jax.ShapeDty...  18.7 us
    pallas_call x1, Pallas kernels, mixer_forward(): pl.pallas_call(forward_kernel, grid=(8,), out_shape=outs, in_specs=[fixed...  16.3 us
  transfers between devices with their start and end apart: 18, of which 3 were waited for; matrix products, arithmetic and copies ran while one was open for 22% of the time, Pallas kernels for 31%

profile of v4, /device:TPU:32, one launch (start us, length us, event | category | flops | bytes accessed | tf_op | source)
XLA Modules:
  0.0 524.9 jit_solution(15830159602302930522)
XLA Ops:
  2.8 3.6 convolution_convert_fusion.2
  7.1 97.9 %gather_weights.1 = (bf16[4,2,4,4,48,896]{5,4,3,2,1,0:T(8,128)(2,1)}, bf16[4,2,4,4,48,256]{5,4,3,2,1,0:T(8,128)(2,1)}, bf16[4,4,4,2,48,384]{5,4,3,2,1,0:T(8,128)...) custom-call(bf16[12,6448]{1,0:T(8,128)(2,1)} %in_ref.1, bf16[12,2048]{1,0:T(8,128)(2,1)} %gu_ref.1, ...), custom_call_target="tpu_custom_call" | custom-call | bytes 41943040 | tf_op jit(solution)/shard_map/gather_weights/pallas_call | solution.py:237
  105.0 7.8 %all-to-all-start = ((bf16[64,24,1536]{2,1,0:T(8,128)(2,1)}), bf16[64,24,1536]{2,1,0:T(8,128)(2,1)}, u32[]{:S(2)}, u32[]{:S(2)}) async-start(bf16[64,24,1536]{2,1,0:T(8,128)(2,1)} %bitcast.250), calls=%async_computation | async-start | bytes 9437184 | tf_op jit(solution)/shard_map/all_to_all | solution.py:965
  116.0 2.3 fusion.98
  118.2 2.3 slice_bitcast_fusion
  122.0 3.6 fusion.97
  127.0 16.3 %mixer_forward.1 = (bf16[256,1536]{1,0:T(8,128)(2,1)S(1)}, bf16[4,256,896]{2,1,0:T(8,128)(2,1)}, f32[4,256,384]{2,1,0:T(8,128)S(1)}, bf16[4,256,384]{2,1,0:T(8,1...) custom-call(bf16[256,1536]{1,0:T(8,128)(2,1)S(1)} %pad_maximum_fusion.6.x_ref, ...), custom_call_target="tpu_custom_call" | custom-call | flops 4026531840 | bytes 23068672 | tf_op jit(solution)/shard_map/mixer_forward/pallas_call | solution.py:664
  162.8 5.0 convolution_convert_fusion.1
  171.7 10.5 %all-to-all-start.1 = ((bf16[64,24,1664]{2,1,0:T(8,128)(2,1)}), bf16[64,24,1664]{2,1,0:T(8,128)(2,1)}, u32[]{:S(2)}, u32[]{:S(2)}) async-start(bf16[64,24,1664]{2,1,0:T(8,128)(2,1)} %bitcast.249), calls=%async_computation.1 | async-start | bytes 10223616 | tf_op jit(solution)/shard_map/all_to_all | solution.py:999
  194.7 2.3 copy.160
  197.1 2.1 fusion.13
  199.2 2.0 fusion.14
  203.9 2.1 broadcast_select_fusion.1
  206.0 2.0 pad_maximum_fusion.gu_ref
  208.0 42.4 %all-to-all-done.1 = bf16[64,24,1664]{2,1,0:T(8,128)(2,1)} async-done(((bf16[64,24,1664]{2,1,0:T(8,128)(2,1)}), bf16[64,24,1664]{2,1,0:T(8,128)(2,1)}, u32[]{:S(2)}, u32[]{:S(2)}) %all-to-all-start.1) | async-done | bytes 5111840 | tf_op jit(solution)/shard_map/all_to_all | solution.py:999
  250.4 18.7 %expert_grads.1 = (bf16[1536,1664]{1,0:T(8,128)(2,1)}, bf16[1536,512]{1,0:T(8,128)(2,1)S(1)}, bf16[1536,512]{1,0:T(8,128)(2,1)S(1)}, bf16[1536,1024]{1,0:T(8,128)(2,1)}) custom-call(bf16[1536,1664]{1,0:T(8,128)(2,1)} %bitcast.44.rows_ref, bf16[1536,1536]{1,0:T(8,128)(2,1)} %bitcast.43.grad_ref, bf16[1536,1024]{1,0:T(8,128)(2,1)} %pad_maximum_fusion.gu_ref, ...), custom_call_target="tpu_custom_call" | custom-call | flops 12079595520 | bytes 27262976 | tf_op jit(solution)/shard_map/expert_grads/pallas_call | solution.py:523
  271.4 7.4 %all-to-all-start.2 = ((bf16[64,24,1664]{2,1,0:T(8,128)(2,1)}), bf16[64,24,1664]{2,1,0:T(8,128)(2,1)}, u32[]{:S(2)}, u32[]{:S(2)}) async-start(bf16[64,24,1664]{2,1,0:T(8,128)(2,1)} %bitcast.275), calls=%async_computation.2 | async-start | bytes 10223616 | tf_op jit(solution)/shard_map/all_to_all | solution.py:1024
  278.9 2.0 dynamic-slice_convert_fusion.4
  284.5 4.7 fusion.105
  289.3 7.1 %fusion.2 = f32[1536,1024]{1,0:T(8,128)S(1)} fusion(bf16[1536,1024]{1,0:T(8,128)(2,1)S(1)} %copy-done.84, bf16[1536,1664]{1,0:T(8,128)(2,1)} %bitcast.44.rows_ref), kind=kOutput, calls=%fused_computation.5 | convolution fusion | flops 4831838208 | bytes 14155776 | tf_op jit(solution)/shard_map/dot_general | solution.py:31
  298.9 4.4 convolution_convert_fusion
  304.6 2.2 convert_add_fusion
  306.8 35.3 %all-to-all-done.2 = bf16[64,24,1664]{2,1,0:T(8,128)(2,1)} async-done(((bf16[64,24,1664]{2,1,0:T(8,128)(2,1)}), bf16[64,24,1664]{2,1,0:T(8,128)(2,1)}, u32[]{:S(2)}, u32[]{:S(2)}) %all-to-all-start.2) | async-done | bytes 5111840 | tf_op jit(solution)/shard_map/all_to_all | solution.py:1024
  344.7 3.2 fusion
  349.0 8.2 %all-to-all-start.3 = ((bf16[64,24,1536]{2,1,0:T(8,128)(2,1)}), bf16[64,24,1536]{2,1,0:T(8,128)(2,1)}, u32[]{:S(2)}, u32[]{:S(2)}) async-start(bf16[64,24,1536]{2,1,0:T(8,128)(2,1)} %bitcast.277), calls=%async_computation.3 | async-start | bytes 9437184 | tf_op jit(solution)/shard_map/all_to_all | solution.py:1036
  357.3 2.8 multiply_reduce_fusion.1
  361.9 2.6 pad_maximum_fusion.4.refs_3_
  367.3 30.8 %mixer_backward.1 = (bf16[4,1536,384]{2,1,0:T(8,128)(2,1)}, bf16[4,1536,896]{2,1,0:T(8,128)(2,1)}, f32[256,1536]{1,0:T(8,128)}, f32[4,8,384]{2,1,0:T(8,128)}, f3...) custom-call(bf16[256,1536]{1,0:T(8,128)(2,1)} %pad_maximum_fusion.9.dm_ref, f32[256,1]{1,0:T(8,128)} %pad_maximum_fusion.11.kappa_ref, ...), custom_call_target="tpu_custom_call" | custom-call | flops 8053063680 | bytes 41943040 | tf_op jit(solution)/shard_map/mixer_backward/pallas_call | solution.py:826
  408.5 6.0 %all-to-all-done.3 = bf16[64,24,1536]{2,1,0:T(8,128)(2,1)} async-done(((bf16[64,24,1536]{2,1,0:T(8,128)(2,1)}), bf16[64,24,1536]{2,1,0:T(8,128)(2,1)}, u32[]{:S(2)}, u32[]{:S(2)}) %all-to-all-start.3) | async-done | bytes 4718624 | tf_op jit(solution)/shard_map/all_to_all | solution.py:1036
  414.5 4.2 add_convert_fusion
  418.7 102.1 %scatter_grads.1 = (f32[8,16,1152]{2,1,0:T(8,128)}, f32[4,32,384]{2,1,0:T(8,128)}, f32[8,128]{1,0:T(8,128)}) custom-call(bf16[4,2,4,4,48,896]{5,4,3,2,1,0:T(8,128)(2,1)} %bitcast.266, bf16[4,2,4,4,48,256]{5,4,3,2,1,0:T(8,128)(2,1)} %pad_maximum_fusion.1.refs_1_, bf16[4,4,4,2,48,384]{5,4,3,2,1,0:T(8,128)(2,1)} %bitcast.276, ...), custom_call_target="tpu_custom_call" | custom-call | bytes 41418752 | tf_op jit(solution)/shard_map/scatter_grads/pallas_call | solution.py:459
  520.8 2.1 finish_grads.1
  (341 shorter events, 76.2 us)
Async XLA Ops:
  0.7 124.9 %collective-permute-start = (bf16[128,1536]{1,0:T(8,128)(2,1)}, bf16[128,1536]{1,0:T(8,128)(2,1)}, u32[]{:S(2)}, u32[]{:S(2)}) collective-permute-start(bf16[128,1536]{1,0:T(8,128)(2,1)} %param.17), channel_id=1, source_target_pairs={{0,64},{64,0},{1,65},{65,1},{2,66},{66,2},{3,67},{67,3},{4,68},{68... | collective-permute-start | bytes 1179656 | tf_op jit(solution)/shard_map/ppermute | solution.py:857
  0.8 124.8 %collective-permute-start.9 = (bf16[128,1536]{1,0:T(8,128)(2,1)}, bf16[128,1536]{1,0:T(8,128)(2,1)}, u32[]{:S(2)}, u32[]{:S(2)}) collective-permute-start(bf16[128,1536]{1,0:T(8,128)(2,1)} %param.18), channel_id=1, source_target_pairs={{0,64},{64,0},{1,65},{65,1},{2,66},{66,2},{3,67},{67,3},{4,68},{68... | collective-permute-start | bytes 1179656 | tf_op jit(solution)/shard_map/ppermute | solution.py:857
  105.0 8.6 %copy-start.65 = (bf16[2,4,4,4,16,128]{5,4,3,2,1,0:T(8,128)(2,1)S(1)}, bf16[2,4,4,4,16,128]{5,4,3,2,1,0:T(8,128)(2,1)}, u32[]{:S(2)}) copy-start(bf16[2,4,4,4,16,128]{5,4,3,2,1,0:T(8,128)(2,1)} %get-tuple-element.63) | copy-start | bytes 1572868
  105.0 66.7 %all-to-all-start = ((bf16[64,24,1536]{2,1,0:T(8,128)(2,1)}), bf16[64,24,1536]{2,1,0:T(8,128)(2,1)}, u32[]{:S(2)}, u32[]{:S(2)}) async-start(bf16[64,24,1536]{2,1,0:T(8,128)(2,1)} %bitcast.250), calls=%async_computation | async-start | bytes 9437184 | tf_op jit(solution)/shard_map/all_to_all | solution.py:965
  112.8 37.0 %collective-permute-start.6 = (bf16[256,1536]{1,0:T(8,128)(2,1)}, bf16[256,1536]{1,0:T(8,128)(2,1)}, u32[]{:S(2)}, u32[]{:S(2)}) collective-permute-start(bf16[256,1536]{1,0:T(8,128)(2,1)} %bitcast.46), channel_id=1, source_target_pairs={{0,64},{64,0},{1,65},{65,1},{2,66},{66,2},{3,67},{67,3},{4,68},{68... | collective-permute-start | bytes 2359304 | tf_op jit(solution)/shard_map/ppermute | solution.py:857
  112.9 91.0 %collective-permute-start.5 = (bf16[768,1024]{1,0:T(8,128)(2,1)}, bf16[768,1024]{1,0:T(8,128)(2,1)}, u32[]{:S(2)}, u32[]{:S(2)}) collective-permute-start(bf16[768,1024]{1,0:T(8,128)(2,1)} %bitcast.45), channel_id=1, source_target_pairs={{0,64},{64,0},{1,65},{65,1},{2,66},{66,2},{3,67},{67,3},{4,68},{68... | collective-permute-start | bytes 4718600 | tf_op jit(solution)/shard_map/ppermute | solution.py:857
  115.7 11.3 %copy-start.2 = (f32[4,8,128]{2,1,0:T(8,128)}, f32[4,8,128]{2,1,0:T(8,128)S(1)}, u32[]{:S(2)}) copy-start(f32[4,8,128]{2,1,0:T(8,128)S(1)} %pad.48.hp_ref) | copy-start | bytes 49156
  115.7 11.3 %copy-start = (f32[256,128]{1,0:T(8,128)}, f32[256,128]{1,0:T(8,128)S(1)}, u32[]{:S(2)}) copy-start(f32[256,128]{1,0:T(8,128)S(1)} %pad.52.marks_ref) | copy-start | bytes 393220
  115.8 11.1 %copy-start.70 = (f32[1536]{0:T(1024)}, f32[1536]{0:T(1024)S(1)}, u32[]{:S(2)}) copy-start(f32[1536]{0:T(1024)S(1)} %broadcast_in_dim.89) | copy-start | bytes 18436
  115.8 11.1 %copy-start.3 = (f32[2,8,128]{2,1,0:T(8,128)}, f32[2,8,128]{2,1,0:T(8,128)S(1)}, u32[]{:S(2)}) copy-start(f32[2,8,128]{2,1,0:T(8,128)S(1)} %pad_bitcast_fusion.cbc_ref) | copy-start | bytes 24580
  118.2 28.6 %copy-start.33 = (bf16[1,4,4,2,16,384]{5,4,3,2,1,0:T(8,128)(2,1)}, bf16[1,4,4,2,16,384]{5,4,3,2,1,0:T(8,128)(2,1)S(1)}, u32[]{:S(2)}) copy-start(bf16[1,4,4,2,16,384]{5,4,3,2,1,0:T(8,128)(2,1)S(1)} %get-tuple-element.216) | copy-start | bytes 1179652
  118.2 28.9 %copy-start.31 = (bf16[1,4,4,2,16,384]{5,4,3,2,1,0:T(8,128)(2,1)}, bf16[1,4,4,2,16,384]{5,4,3,2,1,0:T(8,128)(2,1)S(1)}, u32[]{:S(2)}) copy-start(bf16[1,4,4,2,16,384]{5,4,3,2,1,0:T(8,128)(2,1)S(1)} %get-tuple-element.215) | copy-start | bytes 1179652
  118.2 29.3 %copy-start.29 = (bf16[1,4,4,2,16,384]{5,4,3,2,1,0:T(8,128)(2,1)}, bf16[1,4,4,2,16,384]{5,4,3,2,1,0:T(8,128)(2,1)S(1)}, u32[]{:S(2)}) copy-start(bf16[1,4,4,2,16,384]{5,4,3,2,1,0:T(8,128)(2,1)S(1)} %get-tuple-element.214) | copy-start | bytes 1179652
  127.0 16.3 %copy-start.4 = (f32[8,256]{1,0:T(8,128)}, f32[8,256]{1,0:T(8,128)S(1)}, u32[]{:S(2)}) copy-start(f32[8,256]{1,0:T(8,128)S(1)} %broadcast_in_dim.95.seg_ref) | copy-start | bytes 24580
  144.0 4.8 collective-permute-start.1
  145.2 7.3 %collective-permute-start.2 = (f32[128,1536]{1,0:T(8,128)}, f32[128,1536]{1,0:T(8,128)}, u32[]{:S(2)}, u32[]{:S(2)}) collective-permute-start(f32[128,1536]{1,0:T(8,128)} %constant_dynamic-slice_fusion), channel_id=1, source_target_pairs={{0,64},{64,0},{1,65},{65,1},{2,66},{66,2},{3,67},{67,3},{4,68},{68... | collective-permute-start | bytes 2359304 | tf_op jit(solution)/shard_map/ppermute | solution.py:857
  155.5 12.3 %collective-permute-start.3 = (bf16[128,1536]{1,0:T(8,128)(2,1)}, bf16[128,1536]{1,0:T(8,128)(2,1)}, u32[]{:S(2)}, u32[]{:S(2)}) collective-permute-start(bf16[128,1536]{1,0:T(8,128)(2,1)} %multiply_convert_fusion.1.ffn_ref), channel_id=1, source_target_pairs={{0,64},{64,0},{1,65},{65,1},{2,66},{66,2},{3,67},{67,3},{4,68},{68... | collective-permute-start | bytes 1179656 | tf_op jit(solution)/shard_map/ppermute | solution.py:857
  171.7 78.7 %all-to-all-start.1 = ((bf16[64,24,1664]{2,1,0:T(8,128)(2,1)}), bf16[64,24,1664]{2,1,0:T(8,128)(2,1)}, u32[]{:S(2)}, u32[]{:S(2)}) async-start(bf16[64,24,1664]{2,1,0:T(8,128)(2,1)} %bitcast.249), calls=%async_computation.1 | async-start | bytes 10223616 | tf_op jit(solution)/shard_map/all_to_all | solution.py:999
  196.9 100.7 %collective-permute-start.10 = (bf16[128,1536]{1,0:T(8,128)(2,1)}, bf16[128,1536]{1,0:T(8,128)(2,1)}, u32[]{:S(2)}, u32[]{:S(2)}) collective-permute-start(bf16[128,1536]{1,0:T(8,128)(2,1)} %dynamic-slice_convert_fusion.3), channel_id=1, source_target_pairs={{0,64},{64,0},{1,65},{65,1},{2,66},{66,2},{3,67},{67,3},{4,68},{68... | collective-permute-start | bytes 1179656 | tf_op jit(solution)/shard_map/ppermute | solution.py:857
  271.4 9.5 %copy-start.15 = (bf16[1536,256]{1,0:T(8,128)(2,1)S(1)}, bf16[1536,256]{1,0:T(8,128)(2,1)}, u32[]{:S(2)}) copy-start(bf16[1536,256]{1,0:T(8,128)(2,1)} %copy.160) | copy-start | bytes 2359300
  271.4 9.5 %copy-start.64 = (bf16[1,256,256]{1,2,0:T(8,128)(2,1)S(1)}, bf16[1,256,256]{1,2,0:T(8,128)(2,1)}, u32[]{:S(2)}) copy-start(bf16[1,256,256]{1,2,0:T(8,128)(2,1)} %copy-done.63) | copy-start | bytes 393220
  271.4 70.6 %all-to-all-start.2 = ((bf16[64,24,1664]{2,1,0:T(8,128)(2,1)}), bf16[64,24,1664]{2,1,0:T(8,128)(2,1)}, u32[]{:S(2)}, u32[]{:S(2)}) async-start(bf16[64,24,1664]{2,1,0:T(8,128)(2,1)} %bitcast.275), calls=%async_computation.2 | async-start | bytes 10223616 | tf_op jit(solution)/shard_map/all_to_all | solution.py:1024
  280.9 127.6 %collective-permute-start.4 = (bf16[128,1536]{1,0:T(8,128)(2,1)}, bf16[128,1536]{1,0:T(8,128)(2,1)}, u32[]{:S(2)}, u32[]{:S(2)}) collective-permute-start(bf16[128,1536]{1,0:T(8,128)(2,1)} %dynamic-slice_convert_fusion.4), channel_id=1, source_target_pairs={{0,64},{64,0},{1,65},{65,1},{2,66},{66,2},{3,67},{67,3},{4,68},{68... | collective-permute-start | bytes 1179656 | tf_op jit(solution)/shard_map/ppermute | solution.py:857
  296.6 8.0 %collective-permute-start.7 = (bf16[768,1024]{1,0:T(8,128)(2,1)S(1)}, bf16[768,1024]{1,0:T(8,128)(2,1)S(1)}, u32[]{:S(2)}, u32[]{:S(2)}) collective-permute-start(bf16[768,1024]{1,0:T(8,128)(2,1)S(1)} %dynamic-slice_convert_fusion), channel_id=1, source_target_pairs={{0,64},{64,0},{1,65},{65,1},{2,66},{66,2},{3,67},{67,3},{4,68},{68... | collective-permute-start | bytes 4718600 | tf_op jit(solution)/shard_map/ppermute | solution.py:857
  297.3 6.0 %collective-permute-start.8 = (bf16[256,1536]{1,0:T(8,128)(2,1)S(1)}, bf16[256,1536]{1,0:T(8,128)(2,1)S(1)}, u32[]{:S(2)}, u32[]{:S(2)}) collective-permute-start(bf16[256,1536]{1,0:T(8,128)(2,1)S(1)} %dynamic-slice_convert_fusion.1), channel_id=1, source_target_pairs={{0,64},{64,0},{1,65},{65,1},{2,66},{66,2},{3,67},{67,3},{4,68},{68... | collective-permute-start | bytes 2359304 | tf_op jit(solution)/shard_map/ppermute | solution.py:857
  306.8 36.8 %copy-start.54 = (pred[128,1536]{1,0:T(32,128)(4,1)S(1)}, pred[128,1536]{1,0:T(32,128)(4,1)}, u32[]{:S(2)}) copy-start(pred[128,1536]{1,0:T(32,128)(4,1)} %copy-done.52) | copy-start | bytes 589828
  306.8 36.8 %copy-start.74 = (s32[1536]{0:T(1024)S(1)}, s32[1536]{0:T(1024)}, u32[]{:S(2)}) copy-start(s32[1536]{0:T(1024)} %copy-done.72) | copy-start | bytes 18436
  306.8 37.1 %copy-start.68 = (f32[128,64]{1,0:T(8,128)S(1)}, f32[128,64]{1,0:T(8,128)}, u32[]{:S(2)}) copy-start(f32[128,64]{1,0:T(8,128)} %get-tuple-element.203) | copy-start | bytes 98308
  349.0 65.5 %all-to-all-start.3 = ((bf16[64,24,1536]{2,1,0:T(8,128)(2,1)}), bf16[64,24,1536]{2,1,0:T(8,128)(2,1)}, u32[]{:S(2)}, u32[]{:S(2)}) async-start(bf16[64,24,1536]{2,1,0:T(8,128)(2,1)} %bitcast.277), calls=%async_computation.3 | async-start | bytes 9437184 | tf_op jit(solution)/shard_map/all_to_all | solution.py:1036
  361.1 4.6 collective-permute-start.12
  361.2 5.1 collective-permute-start.11
  401.4 2.7 collective-permute-start.13
  (71 other events, 204.9 us)

commit v5 on v4

--- a/solution.py
+++ b/solution.py
@@ -44,7 +44,7 @@
     return [(lax.rem(core + c, 2), lax.rem(y + d, 4)) for c in range(2) for d in range(4)]
 
 
-def greet(right, left):
+def greet(right, left, opp):
     barrier = pltpu.get_barrier_semaphore()
 
     def signal(device_id):
@@ -53,6 +53,7 @@
     for a in ("z", "x"):
         signal({a: right[a]})
         signal({a: left[a]})
+        signal({a: opp[a]})
     for core, y in chip_row()[1:]:
         signal({"seq": core, "y": y})
 
@@ -111,7 +112,7 @@
     pos, right, left, opp = neighbours()
     row = chip_row()
     (core, y) = row[0]
-    greet(right, left)
+    greet(right, left, opp)
     wide[...] = jnp.zeros_like(wide)
     wide[0, :12, :48] = in_ref[:, 6400:].astype(f32)
     wide[1, :12, :64] = router_ref[...].astype(f32)
@@ -137,7 +138,7 @@
             pin[k, :12, 1024:] = gu_ref[:, 1024 + 128 * k : 1152 + 128 * k]
     for j in range(4):
         pout[j] = rows_ref[:, 384 * j : 384 * j + 384]
-    met(11)
+    met(13)
     sends, first = [], []
 
     def push(src, dst, k, device_id):
@@ -205,6 +206,8 @@
             src = blocks[i].at[(slice(None),) + third(blocks[i].shape, specs[i][1], a)]
         for d, to in enumerate((right[ax], left[ax])):
             first[i, a, d] = remote(i, st, a, d, src, dst, ax, to)
+        if st == 0:
+            later[i, a, 0] = remote(i, st, a, 2, src, dst, ax, opp[ax])
 
     for i, a in every:
         begin(i, a, 0)
@@ -215,10 +218,11 @@
             ax, free = ORDER[a][st], ORDER[a][:st]
             for d, (to, frm) in enumerate(((right[ax], left[ax]), (left[ax], right[ax]))):
                 first[i, a, d].wait_recv()
-                r = region(outs[i], specs[i], free, {**pos, ax: frm}, a, s=d)
-                later[i, a, d] = remote(i, st, a, 2 + d, r, r, ax, to)
+                if st:
+                    r = region(outs[i], specs[i], free, {**pos, ax: frm}, a, s=d)
+                    later[i, a, d] = remote(i, st, a, 2 + d, r, r, ax, to)
         for i, a in every:
-            for d in range(2):
+            for d in range(2 if st else 1):
                 later[i, a, d].wait_recv()
             if st < 2:
                 begin(i, a, st + 1)
@@ -262,10 +266,6 @@
 
 
 def each(lead, fn):
-    if not lead:
-        fn((Ellipsis,))
-        return
-
     @pl.loop(0, int(np.prod(lead)))
     def _(i):
         ix = []
@@ -303,8 +303,8 @@
                 c = pltpu.make_async_copy(source(i, 0, a, idx, s), held[i].at[a, k], loc.at[i, a, k])
                 c.start()
                 local[i, a, k] = c
-    greet(right, left)
-    met(11)
+    greet(right, left, opp)
+    met(13)
     sends = []
 
     def remote(i, st, a, k, src, ax, to):
@@ -325,6 +325,11 @@
 
     def begin(i, a, st):
         ax = ORDER[a][2 - st]
+        if st == 2:
+            for k, to in enumerate((opp[ax], right[ax], left[ax])):
+                for s in range(2):
+                    cp[i, a, 2 * k + s] = remote(i, st, a, 2 * k + s, source(i, st, a, to, s), ax, to)
+            return
         cp[i, a, 0] = remote(i, st, a, 0, source(i, st, a, opp[ax], 0), ax, right[ax])
         cp[i, a, 1] = remote(i, st, a, 1, source(i, st, a, opp[ax], 1), ax, left[ax])
         cp[i, a, 2] = remote(i, st, a, 2, source(i, st, a, right[ax], 1), ax, right[ax])
@@ -332,8 +337,8 @@
 
     for i, a in every:
         begin(i, a, 0)
-    for st in range(3):
-        lead = ((4, 4), (4,), ())[st]
+    for st in range(2):
+        lead = ((4, 4), (4,))[st]
         for i, a in every:
             ax = ORDER[a][2 - st]
             for d, to in enumerate((right[ax], left[ax])):
@@ -360,18 +365,21 @@
                 cp[i, a, q].wait_recv()
                 acc = held[i].at[a, 2 + s] if st == 0 else source(i, st, a, pos[ax], s)
                 one, two = got[i][st].at[a, p], got[i][st].at[a, q]
-                if st == 2:
-                    ix = (s,) + third(outs[i].shape, specs[i][1], a)
-                    outs[i][ix] = acc[...].astype(f32) + one[...].astype(f32) + two[...].astype(f32)
-                else:
-
-                    def close(ix, acc=acc, one=one, two=two):
-                        total = acc[ix].astype(f32) + one[ix].astype(f32) + two[ix].astype(f32)
-                        acc[ix] = total.astype(acc.dtype)
-
-                    each(lead, close)
-            if st < 2:
-                begin(i, a, st + 1)
+
+                def close(ix, acc=acc, one=one, two=two):
+                    total = acc[ix].astype(f32) + one[ix].astype(f32) + two[ix].astype(f32)
+                    acc[ix] = total.astype(acc.dtype)
+
+                each(lead, close)
+            begin(i, a, st + 1)
+    for i, a in every:
+        ax = ORDER[a][0]
+        for s in range(2):
+            total = source(i, 2, a, pos[ax], s)[...].astype(f32)
+            for k in range(3):
+                cp[i, a, 2 * k + s].wait_recv()
+                total = total + got[i][2][a, 2 * k + s].astype(f32)
+            outs[i][(s,) + third(outs[i].shape, specs[i][1], a)] = total
 
     for k in range(8):
         c, d = divmod(k, 4)
@@ -455,7 +463,6 @@
     results = [(8, 16, 1152), (4, 32, 384), (8, 128)]
     pieces = [(third_shape(v.shape, spec[1]), v.dtype) for v, spec in zip(arrays, SPECS)]
     cut = [len(cuts(spec)) for spec in SPECS]
-    total = sum(int(np.prod(v.shape)) for v in arrays) * 2
     return pl.pallas_call(
         scatter_kernel,
         out_shape=[jax.ShapeDtypeStruct(v, f32) for v in results],
@@ -481,33 +488,35 @@
         compiler_params=pltpu.CompilerParams(
             collective_id=2, has_side_effects=True, vmem_limit_bytes=56 * 2**20
         ),
-        cost_estimate=pl.CostEstimate(flops=0, bytes_accessed=2 * total, transcendentals=0),
+        cost_estimate=pl.CostEstimate(flops=0, bytes_accessed=0, transcendentals=0),
         name="scatter_grads",
     )(*arrays)
 
 
 def expert_kernel(rows_ref, grad_ref, gu_ref, down_ref, pick_ref, back_ref, act_ref, wact_ref, wgu_ref):
-    e_gu = dot(rows_ref[:, :1536], gu_ref[...])
-    eg, eu = e_gu[:, :512], e_gu[:, 512:]
-    sig = jax.nn.sigmoid(eg)
-    silu = eg * sig
-    act32 = silu * eu
-    act = act32.astype(bf16)
-    slot_gate = jnp.sum(rows_ref[:, 1536:].astype(f32) * pick_ref[...], axis=1, keepdims=True)
-    d_act = dot(grad_ref[...], down_ref[...], ((1,), (1,)))
-    d_gate = jnp.sum(act.astype(f32) * d_act, axis=1, keepdims=True)
-    d_eg = d_act * eu * (sig + silu * (1.0 - sig))
-    d_eu = d_act * silu
-    d_gu = jnp.concatenate([d_eg.astype(bf16), d_eu.astype(bf16)], axis=1)
-    back_ref[:, :1536] = dot(d_gu, gu_ref[...], ((1,), (1,))).astype(bf16)
-    hi = d_gate.astype(bf16).astype(f32)
-    lane = lax.broadcasted_iota(jnp.int32, (rows_ref.shape[0], 128), 1)
-    tail = jnp.where(lane == 0, hi, jnp.where(lane == 1, d_gate - hi, 0.0))
-    back_ref[:, 1536:] = tail.astype(bf16)
-    act_ref[...] = act
-    wact_ref[...] = (act32 * slot_gate).astype(bf16)
-    wgu_ref[:, :512] = (d_eg * slot_gate).astype(bf16)
-    wgu_ref[:, 512:] = (d_eu * slot_gate).astype(bf16)
+    for at in range(0, rows_ref.shape[0], 256):
+        part = pl.ds(at, 256)
+        e_gu = dot(rows_ref[part, :1536], gu_ref[...])
+        d_act = dot(grad_ref[part, :], down_ref[...], ((1,), (1,)))
+        eg, eu = e_gu[:, :512], e_gu[:, 512:]
+        sig = jax.nn.sigmoid(eg)
+        silu = eg * sig
+        act32 = silu * eu
+        act = act32.astype(bf16)
+        slot_gate = jnp.sum(rows_ref[part, 1536:].astype(f32) * pick_ref[...], axis=1, keepdims=True)
+        d_gate = jnp.sum(act.astype(f32) * d_act, axis=1, keepdims=True)
+        d_eg = d_act * eu * (sig + silu * (1.0 - sig))
+        d_eu = d_act * silu
+        d_gu = jnp.concatenate([d_eg.astype(bf16), d_eu.astype(bf16)], axis=1)
+        back_ref[part, :1536] = dot(d_gu, gu_ref[...], ((1,), (1,))).astype(bf16)
+        hi = d_gate.astype(bf16).astype(f32)
+        lane = lanes((256, 128))
+        tail = jnp.where(lane == 0, hi, jnp.where(lane == 1, d_gate - hi, 0.0))
+        back_ref[part, 1536:] = tail.astype(bf16)
+        act_ref[part, :] = act
+        wact_ref[part, :] = (act32 * slot_gate).astype(bf16)
+        wgu_ref[part, :512] = (d_eg * slot_gate).astype(bf16)
+        wgu_ref[part, 512:] = (d_eu * slot_gate).astype(bf16)
 
 
 def expert_grads(rows, grad_rows, gate_up, down, pick):
@@ -684,8 +693,8 @@
 
 def backward_kernel(
     dm_ref, kappa_ref, w_out_ref, w_in_ref, normed_ref, ffn_ref, drout_ref, proj_ref, y_ref,
-    scaled_ref, cx_ref, cbc_ref, hp_ref, marks_ref, seg_ref,
-    gout_ref, gin_ref, dn_ref, gcx_ref, gcbc_ref, gheads_ref,
+    scaled_ref, cx_ref, cbc_ref, hp_ref, marks_ref, seg_ref, x_ref,
+    gout_ref, gin_ref, dn_ref, gcx_ref, gcbc_ref, gheads_ref, gnorm_ref,
     dproj_ref, scores_ref, dscores_ref, bc_ref,
 ):
     i = pl.program_id(0)
@@ -807,8 +816,14 @@
         last = last + dot(ffn_ref[...], drout_ref[j], ((0,), (0,)))
         gin_ref[0, :, 768:] = last.astype(bf16)
 
-
-def mixer_backward(dm, kappa, w_out, w_in, normed, ffn_in, drout, proj, y, scaled, cx, cbc, hp, marks, seg):
+    @pl.when(i == 7)
+    def _():
+        x = x_ref[...].astype(f32)
+        total = jnp.sum(dn_ref[...] * x * rms(x), axis=0, keepdims=True)
+        gnorm_ref[...] = jnp.broadcast_to(total, gnorm_ref.shape)
+
+
+def mixer_backward(dm, kappa, w_out, w_in, *rest):
     def late(i):
         return jnp.maximum(i - 4, 0)
 
@@ -820,6 +835,7 @@
         jax.ShapeDtypeStruct((4, 8, 384), f32),
         jax.ShapeDtypeStruct((2, 8, 128), f32),
         jax.ShapeDtypeStruct((4, 8, 128), f32),
+        jax.ShapeDtypeStruct((8, 1536), f32),
     ]
     w_out_spec = pl.BlockSpec((4, 384, 384), lambda i: (0, early(i), 0))
     w_in_spec = pl.BlockSpec((1, 1536, 896), lambda i: (late(i), 0, 0))
@@ -836,7 +852,7 @@
             fixed(kappa),
             w_out_spec,
             w_in_spec,
-            *[fixed(v) for v in (normed, ffn_in, drout, proj, y, scaled, cx, cbc, hp, marks, seg)],
+            *[fixed(v) for v in rest],
         ],
         out_specs=[w_out_spec, w_in_spec, *[fixed(o) for o in small]],
         scratch_shapes=[
@@ -847,10 +863,10 @@
         ],
         compiler_params=pltpu.CompilerParams(vmem_limit_bytes=56 * 2**20),
         cost_estimate=pl.CostEstimate(
-            flops=4 * 256 * 1536 * (3584 + 1536), bytes_accessed=40 * 2**20, transcendentals=2**21
+            flops=0, bytes_accessed=0, transcendentals=0
         ),
         name="mixer_backward",
-    )(dm, kappa, w_out, w_in, normed, ffn_in, drout, proj, y, scaled, cx, cbc, hp, marks, seg)
+    )(dm, kappa, w_out, w_in, *rest)
 
 
 def swap(v):
@@ -1029,8 +1045,8 @@
     grad_eg = ge_own + swap(ge_other.astype(bf16)).astype(f32)
     gd_own, gd_other = halves(grad_ed, s)
     grad_ed = gd_own + swap(gd_other.astype(bf16)).astype(f32)
-    e_out, d_back, grad_eg, grad_ed, d_ffn = lax.optimization_barrier(
-        (e_out, d_back, grad_eg, grad_ed, d_ffn)
+    e_out, d_back, grad_eg, grad_ed, d_ffn, grad_sgu, grad_sdown = lax.optimization_barrier(
+        (e_out, d_back, grad_eg, grad_ed, d_ffn, grad_sgu, grad_sdown)
     )
     d_back = d_back.reshape(n_slots, 1664)
     out_back = lax.all_to_all(e_out.reshape(experts, slots, 1536), DP, 0, 0, tiled=True)
@@ -1059,8 +1075,8 @@
     d_mixed_full = both_halves(d_mixed, swap(d_mixed), s)
     kappa = both_halves(kappa, swap(kappa), s)
     drout = jnp.pad(d_logits_low.reshape(128, 4, 16).transpose(1, 0, 2), ((0, 0), (0, 0), (64, 48)))
-    grad_out, grad_in, d_normed, g_cx, g_cbc, g_heads = mixer_backward(
-        d_mixed_full, kappa, w_out, w_in, normed, ffn_in, drout, proj, y, scaled, cx, cbc, hp, marks, seg
+    grad_out, grad_in, d_normed, g_cx, g_cbc, g_heads, in_norm_grad = mixer_backward(
+        d_mixed_full, kappa, w_out, w_in, normed, ffn_in, drout, proj, y, scaled, cx, cbc, hp, marks, seg, x_full
     )
     conv_x_grad = g_cx[:, :5].transpose(1, 0, 2).reshape(5, 1536)
     conv_bc_grad = g_cbc[:, :5].transpose(1, 0, 2).reshape(5, 256)
@@ -1069,14 +1085,7 @@
     d_skip = jnp.sum(g_cx[:, 5].reshape(24, 64), axis=1)
     head_grad = jnp.concatenate([head_grad, d_skip[None]], axis=0)
     dn_own, dn_other = halves(d_normed, s)
-    d_normed = dn_own + swap(dn_other.astype(bf16)).astype(f32)
-    x_own = tokens.astype(f32)
-    p = rms(x_own)
-    in_norm_grad = jnp.sum(d_normed * x_own * p, axis=0)
-    v = d_normed * g_in
-    token_grad = (
-        d_residual + p * v - p * p * p * x_own * jnp.mean(v * x_own, axis=1, keepdims=True)
-    ).astype(bf16)
+    dn_other = swap(dn_other.astype(bf16))
 
     conv_grad = lax.dynamic_update_slice(
         jnp.zeros((5, 3328), f32), conv_x_grad, (0, s * 1536)
@@ -1092,7 +1101,7 @@
     conv_grad = conv_grad.reshape(5, 128, 26).transpose(1, 0, 2)
     small = jnp.concatenate(
         [
-            rows_of(in_norm_grad, 12),
+            rows_of(in_norm_grad[0], 12),
             rows_of(ffn_norm_grad, 12),
             rows_of(mixer_norm_grad, 24),
             jnp.pad(conv_grad, ((0, 0), (0, 0), (0, 38))),
@@ -1101,10 +1110,6 @@
     )
     head_rows = jnp.broadcast_to(jnp.pad(head_grad, ((0, 5), (0, 16)))[None], (128, 8, 64))
     small = jnp.concatenate([small, head_rows], axis=2).reshape(2, 4, 4, 4, 8, 128)
-    weighted_late, grad_in = lax.optimization_barrier((weighted, grad_in))
-    routed = dot(weighted_late, out_back)
-    block_out = (residual + s_out + routed).astype(bf16)
-    block_out, small = lax.optimization_barrier((block_out, small))
     sums = scatter(
         (
             grad_in.reshape(4, 2, 4, 4, 48, 896),
@@ -1114,6 +1119,16 @@
             small,
         )
     )
+    weighted_late, dn_own, sums = lax.optimization_barrier((weighted, dn_own, tuple(sums)))
+    routed = dot(weighted_late, out_back)
+    block_out = (residual + s_out + routed).astype(bf16)
+    d_normed = dn_own + dn_other.astype(f32)
+    x_own = tokens.astype(f32)
+    p = rms(x_own)
+    v = d_normed * g_in
+    token_grad = (
+        d_residual + p * v - p * p * p * x_own * jnp.mean(v * x_own, axis=1, keepdims=True)
+    ).astype(bf16)
     (
         in_proj_grad, router_grad, sgu_grad, out_proj_grad, sdown_grad, head_grad, conv_grad,
         in_norm_grad, ffn_norm_grad, mixer_norm_grad, conv_bias_grad,

time: 533 us -> 516 us (0.968)
  local copies, waits for them, and re-layouts: 42.6 us -> 37.2 us
    all_to_all x1, waiting for transfers between devices: 0.01 us -> 6.63 us  [local(): lax.all_to_all(grad_slots, DP, 0, 0, tiled=True).reshape(n_slots, 1536)]
    all_to_all x1, waiting for transfers between devices: 6.02 us -> 0.01 us  [local(): lax.all_to_all(e_out.reshape(experts, slots, 1536), DP, 0, 0, tiled=True)]
    unnamed x172 -> x152, local copies, waits for them, and re-layouts: 12.2 us -> 10.6 us
  transfers between devices with their start and end apart: 18 -> 18, of which waited for: 3 -> 3; matrix products, arithmetic and copies ran while one was open for 22% -> 20% of each run, Pallas kernels for 31% -> 53%
where the time goes in v5:
time: 516 us; the launch traced here: 509 us
  Pallas kernels  270 us (52%)
  waiting for transfers between devices  79.8 us (15%)
  matrix products  51.2 us (10%)
  local copies, waits for them, and re-layouts  37.2 us (7%)
  starting transfers between devices  35.2 us (7%)
  other arithmetic  32.8 us (6%)
    pallas_call x1, Pallas kernels, scatter(): pl.pallas_call(scatter_kernel, out_shape=[jax.ShapeDtypeStruct(v, f32) fo...  103 us
    pallas_call x1, Pallas kernels, gather(): pl.pallas_call(gather_kernel, out_shape=outs, in_specs=[pl.BlockSpec(memo...  98.7 us
    dot_general x39, matrix products, dot(): return lax.dot_general(a, b, (dims, ((), ())), preferred_element_type=f32)  51.2 us
    all_to_all x1, waiting for transfers between devices, local(): arrived = lax.all_to_all(sent, DP, 0, 0, tiled=True).reshape(n_slots, 1664)  39.7 us
    all_to_all x1, waiting for transfers between devices, local(): lax.all_to_all(d_rows.reshape(experts, slots, 1664), DP, 0, 0, tiled=True)  33.4 us
    pallas_call x1, Pallas kernels, mixer_backward(): pl.pallas_call(backward_kernel, grid=(8,), out_shape=[jax.ShapeDtypeStruc...  31.4 us
    pallas_call x1, Pallas kernels, expert_grads(): pl.pallas_call(expert_kernel, grid=(n // block,), out_shape=[jax.ShapeDty...  18.7 us
    pallas_call x1, Pallas kernels, mixer_forward(): pl.pallas_call(forward_kernel, grid=(8,), out_shape=outs, in_specs=[fixed...  16.5 us
  transfers between devices with their start and end apart: 18, of which 3 were waited for; matrix products, arithmetic and copies ran while one was open for 20% of the time, Pallas kernels for 53%

profile of v5, /device:TPU:32, one launch (start us, length us, event | category | flops | bytes accessed | tf_op | source)
XLA Modules:
  0.0 508.8 jit_solution(6914472194697611340)
XLA Ops:
  2.8 3.5 convolution_convert_fusion.2
  7.0 98.7 %gather_weights.1 = (bf16[4,2,4,4,48,896]{5,4,3,2,1,0:T(8,128)(2,1)}, bf16[4,2,4,4,48,256]{5,4,3,2,1,0:T(8,128)(2,1)}, bf16[4,4,4,2,48,384]{5,4,3,2,1,0:T(8,128)...) custom-call(bf16[12,6448]{1,0:T(8,128)(2,1)} %in_ref.1, bf16[12,2048]{1,0:T(8,128)(2,1)} %gu_ref.1, ...), custom_call_target="tpu_custom_call" | custom-call | bytes 41943040 | tf_op jit(solution)/shard_map/gather_weights/pallas_call | solution.py:241
  105.8 7.4 %all-to-all-start = ((bf16[64,24,1536]{2,1,0:T(8,128)(2,1)}), bf16[64,24,1536]{2,1,0:T(8,128)(2,1)}, u32[]{:S(2)}, u32[]{:S(2)}) async-start(bf16[64,24,1536]{2,1,0:T(8,128)(2,1)} %bitcast.212), calls=%async_computation | async-start | bytes 9437184 | tf_op jit(solution)/shard_map/all_to_all | solution.py:981
  116.6 2.4 fusion.75
  119.0 2.0 slice_bitcast_fusion
  121.9 3.6 fusion.74
  126.9 16.5 %mixer_forward.1 = (bf16[256,1536]{1,0:T(8,128)(2,1)S(1)}, bf16[4,256,896]{2,1,0:T(8,128)(2,1)}, f32[4,256,384]{2,1,0:T(8,128)S(1)}, bf16[4,256,384]{2,1,0:T(8,1...) custom-call(bf16[256,1536]{1,0:T(8,128)(2,1)S(1)} %pad_maximum_fusion.6.x_ref, ...), custom_call_target="tpu_custom_call" | custom-call | flops 4026531840 | bytes 23068672 | tf_op jit(solution)/shard_map/mixer_forward/pallas_call | solution.py:673
  157.7 4.7 convolution_convert_fusion.1
  163.7 6.6 %all-to-all-done = bf16[64,24,1536]{2,1,0:T(8,128)(2,1)} async-done(((bf16[64,24,1536]{2,1,0:T(8,128)(2,1)}), bf16[64,24,1536]{2,1,0:T(8,128)(2,1)}, u32[]{:S(2)}, u32[]{:S(2)}) %all-to-all-start) | async-done | bytes 4718624 | tf_op jit(solution)/shard_map/all_to_all | solution.py:981
  170.3 6.9 %all-to-all-start.1 = ((bf16[64,24,1664]{2,1,0:T(8,128)(2,1)}), bf16[64,24,1664]{2,1,0:T(8,128)(2,1)}, u32[]{:S(2)}, u32[]{:S(2)}) async-start(bf16[64,24,1664]{2,1,0:T(8,128)(2,1)} %bitcast.211), calls=%async_computation.1 | async-start | bytes 10223616 | tf_op jit(solution)/shard_map/all_to_all | solution.py:1015
  177.3 1.6 convolution_bitcast_fusion.3
  195.3 2.1 broadcast_select_fusion.1
  197.4 2.0 pad_maximum_fusion.gu_ref
  199.3 39.7 %all-to-all-done.1 = bf16[64,24,1664]{2,1,0:T(8,128)(2,1)} async-done(((bf16[64,24,1664]{2,1,0:T(8,128)(2,1)}), bf16[64,24,1664]{2,1,0:T(8,128)(2,1)}, u32[]{:S(2)}, u32[]{:S(2)}) %all-to-all-start.1) | async-done | bytes 5111840 | tf_op jit(solution)/shard_map/all_to_all | solution.py:1015
  240.4 18.7 %expert_grads.1 = (bf16[1536,1664]{1,0:T(8,128)(2,1)}, bf16[1536,512]{1,0:T(8,128)(2,1)S(1)}, bf16[1536,512]{1,0:T(8,128)(2,1)S(1)}, bf16[1536,1024]{1,0:T(8,128)(2,1)}) custom-call(bf16[1536,1664]{1,0:T(8,128)(2,1)} %bitcast.44.rows_ref, bf16[1536,1536]{1,0:T(8,128)(2,1)} %bitcast.43.grad_ref, bf16[1536,1024]{1,0:T(8,128)(2,1)} %pad_maximum_fusion.gu_ref, ...), custom_call_target="tpu_custom_call" | custom-call | flops 12079595520 | bytes 27262976 | tf_op jit(solution)/shard_map/expert_grads/pallas_call | solution.py:532
  261.4 8.0 %all-to-all-start.2 = ((bf16[64,24,1664]{2,1,0:T(8,128)(2,1)}), bf16[64,24,1664]{2,1,0:T(8,128)(2,1)}, u32[]{:S(2)}, u32[]{:S(2)}) async-start(bf16[64,24,1664]{2,1,0:T(8,128)(2,1)} %bitcast.234), calls=%async_computation.2 | async-start | bytes 10223616 | tf_op jit(solution)/shard_map/all_to_all | solution.py:1040
  269.4 1.6 fusion.7
  273.6 1.8 pad_maximum_fusion.1
  275.7 4.7 fusion.82
  280.4 7.1 %fusion.2 = f32[1536,1024]{1,0:T(8,128)S(1)} fusion(bf16[1536,1024]{1,0:T(8,128)(2,1)S(1)} %copy-done.74, bf16[1536,1664]{1,0:T(8,128)(2,1)} %bitcast.44.rows_ref), kind=kOutput, calls=%fused_computation.5 | convolution fusion | flops 4831838208 | bytes 14155776 | tf_op jit(solution)/shard_map/dot_general | solution.py:31
  290.0 4.4 convolution_convert_fusion
  295.7 2.2 convert_add_fusion
  297.9 33.4 %all-to-all-done.2 = bf16[64,24,1664]{2,1,0:T(8,128)(2,1)} async-done(((bf16[64,24,1664]{2,1,0:T(8,128)(2,1)}), bf16[64,24,1664]{2,1,0:T(8,128)(2,1)}, u32[]{:S(2)}, u32[]{:S(2)}) %all-to-all-start.2) | async-done | bytes 5111840 | tf_op jit(solution)/shard_map/all_to_all | solution.py:1040
  333.9 3.1 fusion
  338.2 8.0 %all-to-all-start.3 = ((bf16[64,24,1536]{2,1,0:T(8,128)(2,1)}), bf16[64,24,1536]{2,1,0:T(8,128)(2,1)}, u32[]{:S(2)}, u32[]{:S(2)}) async-start(bf16[64,24,1536]{2,1,0:T(8,128)(2,1)} %bitcast.236), calls=%async_computation.3 | async-start | bytes 9437184 | tf_op jit(solution)/shard_map/all_to_all | solution.py:1052
  346.2 2.7 multiply_reduce_fusion.1
  350.0 1.9 dynamic-slice_convert_fusion.4
  354.9 31.4 %mixer_backward.1 = (bf16[4,1536,384]{2,1,0:T(8,128)(2,1)}, bf16[4,1536,896]{2,1,0:T(8,128)(2,1)}, f32[256,1536]{1,0:T(8,128)}, f32[4,8,384]{2,1,0:T(8,128)}, f3...) custom-call(bf16[256,1536]{1,0:T(8,128)(2,1)} %pad_maximum_fusion.9.dm_ref, ...), custom_call_target="tpu_custom_call" | custom-call | tf_op jit(solution)/shard_map/mixer_backward/pallas_call | solution.py:842
  394.6 102.7 %scatter_grads.1 = (f32[8,16,1152]{2,1,0:T(8,128)}, f32[4,32,384]{2,1,0:T(8,128)}, f32[8,128]{1,0:T(8,128)}) custom-call(bf16[4,2,4,4,48,896]{5,4,3,2,1,0:T(8,128)(2,1)} %bitcast.224, bf16[4,2,4,4,48,256]{5,4,3,2,1,0:T(8,128)(2,1)} %bitcast.223, bf16[4,4,4,2,48,384]{5,4,3,2,1,0:T(8,128)(2,1)} %bitcast.235, bf16[4,4,4,2,16,384]{5,4,3,2,1,0:T(8,128)(2,1)} %bitcast.233, ...), custom_call_target="tpu_custom_call" | custom-call | tf_op jit(solution)/shard_map/scatter_grads/pallas_call | solution.py:466
  497.5 2.2 finish_grads.1
  502.1 2.4 fusion.18
  504.5 4.1 add_convert_fusion
  (321 shorter events, 68.2 us)
Async XLA Ops:
  0.7 124.8 %collective-permute-start = (bf16[128,1536]{1,0:T(8,128)(2,1)}, bf16[128,1536]{1,0:T(8,128)(2,1)}, u32[]{:S(2)}, u32[]{:S(2)}) collective-permute-start(bf16[128,1536]{1,0:T(8,128)(2,1)} %param.17), channel_id=1, source_target_pairs={{0,64},{64,0},{1,65},{65,1},{2,66},{66,2},{3,67},{67,3},{4,68},{68... | collective-permute-start | bytes 1179656 | tf_op jit(solution)/shard_map/ppermute | solution.py:873
  0.8 124.8 %collective-permute-start.9 = (bf16[128,1536]{1,0:T(8,128)(2,1)}, bf16[128,1536]{1,0:T(8,128)(2,1)}, u32[]{:S(2)}, u32[]{:S(2)}) collective-permute-start(bf16[128,1536]{1,0:T(8,128)(2,1)} %param.18), channel_id=1, source_target_pairs={{0,64},{64,0},{1,65},{65,1},{2,66},{66,2},{3,67},{67,3},{4,68},{68... | collective-permute-start | bytes 1179656 | tf_op jit(solution)/shard_map/ppermute | solution.py:873
  105.8 8.5 %copy-start.57 = (bf16[2,4,4,4,16,128]{5,4,3,2,1,0:T(8,128)(2,1)S(1)}, bf16[2,4,4,4,16,128]{5,4,3,2,1,0:T(8,128)(2,1)}, u32[]{:S(2)}) copy-start(bf16[2,4,4,4,16,128]{5,4,3,2,1,0:T(8,128)(2,1)} %get-tuple-element.67) | copy-start | bytes 1572868
  105.8 64.6 %all-to-all-start = ((bf16[64,24,1536]{2,1,0:T(8,128)(2,1)}), bf16[64,24,1536]{2,1,0:T(8,128)(2,1)}, u32[]{:S(2)}, u32[]{:S(2)}) async-start(bf16[64,24,1536]{2,1,0:T(8,128)(2,1)} %bitcast.212), calls=%async_computation | async-start | bytes 9437184 | tf_op jit(solution)/shard_map/all_to_all | solution.py:981
  113.2 35.7 %collective-permute-start.6 = (bf16[256,1536]{1,0:T(8,128)(2,1)}, bf16[256,1536]{1,0:T(8,128)(2,1)}, u32[]{:S(2)}, u32[]{:S(2)}) collective-permute-start(bf16[256,1536]{1,0:T(8,128)(2,1)} %bitcast.46), channel_id=1, source_target_pairs={{0,64},{64,0},{1,65},{65,1},{2,66},{66,2},{3,67},{67,3},{4,68},{68... | collective-permute-start | bytes 2359304 | tf_op jit(solution)/shard_map/ppermute | solution.py:873
  113.3 82.0 %collective-permute-start.5 = (bf16[768,1024]{1,0:T(8,128)(2,1)}, bf16[768,1024]{1,0:T(8,128)(2,1)}, u32[]{:S(2)}, u32[]{:S(2)}) collective-permute-start(bf16[768,1024]{1,0:T(8,128)(2,1)} %bitcast.45), channel_id=1, source_target_pairs={{0,64},{64,0},{1,65},{65,1},{2,66},{66,2},{3,67},{67,3},{4,68},{68... | collective-permute-start | bytes 4718600 | tf_op jit(solution)/shard_map/ppermute | solution.py:873
  116.4 10.5 %copy-start.7 = (f32[4,8,128]{2,1,0:T(8,128)}, f32[4,8,128]{2,1,0:T(8,128)S(1)}, u32[]{:S(2)}) copy-start(f32[4,8,128]{2,1,0:T(8,128)S(1)} %pad.48.hp_ref) | copy-start | bytes 49156
  116.4 10.5 %copy-start.3 = (f32[256,128]{1,0:T(8,128)}, f32[256,128]{1,0:T(8,128)S(1)}, u32[]{:S(2)}) copy-start(f32[256,128]{1,0:T(8,128)S(1)} %pad.52.marks_ref) | copy-start | bytes 393220
  116.5 10.3 %copy-start.62 = (f32[1536]{0:T(1024)}, f32[1536]{0:T(1024)S(1)}, u32[]{:S(2)}) copy-start(f32[1536]{0:T(1024)S(1)} %broadcast_in_dim.89) | copy-start | bytes 18436
  116.5 10.4 %copy-start.8 = (f32[2,8,128]{2,1,0:T(8,128)}, f32[2,8,128]{2,1,0:T(8,128)S(1)}, u32[]{:S(2)}) copy-start(f32[2,8,128]{2,1,0:T(8,128)S(1)} %pad_bitcast_fusion.cbc_ref) | copy-start | bytes 24580
  119.0 28.4 %copy-start.28 = (bf16[1,4,4,2,16,384]{5,4,3,2,1,0:T(8,128)(2,1)}, bf16[1,4,4,2,16,384]{5,4,3,2,1,0:T(8,128)(2,1)S(1)}, u32[]{:S(2)}) copy-start(bf16[1,4,4,2,16,384]{5,4,3,2,1,0:T(8,128)(2,1)S(1)} %get-tuple-element.222) | copy-start | bytes 1179652
  126.8 16.5 %copy-start = (bf16[256,1536]{1,0:T(8,128)(2,1)}, bf16[256,1536]{1,0:T(8,128)(2,1)S(1)}, u32[]{:S(2)}) copy-start(bf16[256,1536]{1,0:T(8,128)(2,1)S(1)} %pad_maximum_fusion.6.x_ref) | copy-start | bytes 2359300
  126.9 16.5 %copy-start.9 = (f32[8,256]{1,0:T(8,128)}, f32[8,256]{1,0:T(8,128)S(1)}, u32[]{:S(2)}) copy-start(f32[8,256]{1,0:T(8,128)S(1)} %broadcast_in_dim.95.seg_ref) | copy-start | bytes 24580
  143.4 5.3 %collective-permute-start.1 = (f32[128,1]{1,0:T(8,128)S(1)}, f32[128,1]{1,0:T(8,128)S(1)}, u32[]{:S(2)}, u32[]{:S(2)}) collective-permute-start(f32[128,1]{1,0:T(8,128)S(1)} %constant_dynamic-slice_fusion.2), channel_id=1, source_target_pairs={{0,64},{64,0},{1,65},{65,1},{2,66},{66,2},{3,67},{67,3},{4,68},{68... | collective-permute-start | bytes 1544 | tf_op jit(solution)/shard_map/ppermute | solution.py:873
  144.8 7.2 %collective-permute-start.2 = (f32[128,1536]{1,0:T(8,128)}, f32[128,1536]{1,0:T(8,128)}, u32[]{:S(2)}, u32[]{:S(2)}) collective-permute-start(f32[128,1536]{1,0:T(8,128)} %constant_dynamic-slice_fusion.1), channel_id=1, source_target_pairs={{0,64},{64,0},{1,65},{65,1},{2,66},{66,2},{3,67},{67,3},{4,68},{68... | collective-permute-start | bytes 2359304 | tf_op jit(solution)/shard_map/ppermute | solution.py:873
  154.2 8.3 %collective-permute-start.3 = (bf16[128,1536]{1,0:T(8,128)(2,1)S(1)}, bf16[128,1536]{1,0:T(8,128)(2,1)}, u32[]{:S(2)}, u32[]{:S(2)}) collective-permute-start(bf16[128,1536]{1,0:T(8,128)(2,1)S(1)} %multiply_convert_fusion.1.ffn_ref), channel_id=1, source_target_pairs={{0,64},{64,0},{1,65},{65,1},{2,66},{66,2},{3,67},{67,3},{4,68},{68... | collective-permute-start | bytes 1179656 | tf_op jit(solution)/shard_map/ppermute | solution.py:873
  163.7 16.8 %copy-start.16 = (bf16[128,1536]{1,0:T(8,128)(2,1)}, bf16[128,1536]{1,0:T(8,128)(2,1)S(1)}, u32[]{:S(2)}) copy-start(bf16[128,1536]{1,0:T(8,128)(2,1)S(1)} %get-tuple-element.233) | copy-start | bytes 1179652
  163.7 16.8 %copy-start.18 = (bf16[128,1536]{1,0:T(8,128)(2,1)}, bf16[128,1536]{1,0:T(8,128)(2,1)S(1)}, u32[]{:S(2)}) copy-start(bf16[128,1536]{1,0:T(8,128)(2,1)S(1)} %get-tuple-element.234) | copy-start | bytes 1179652
  170.3 68.7 %all-to-all-start.1 = ((bf16[64,24,1664]{2,1,0:T(8,128)(2,1)}), bf16[64,24,1664]{2,1,0:T(8,128)(2,1)}, u32[]{:S(2)}, u32[]{:S(2)}) async-start(bf16[64,24,1664]{2,1,0:T(8,128)(2,1)} %bitcast.211), calls=%async_computation.1 | async-start | bytes 10223616 | tf_op jit(solution)/shard_map/all_to_all | solution.py:1015
  185.1 103.5 %collective-permute-start.10 = (bf16[128,1536]{1,0:T(8,128)(2,1)}, bf16[128,1536]{1,0:T(8,128)(2,1)}, u32[]{:S(2)}, u32[]{:S(2)}) collective-permute-start(bf16[128,1536]{1,0:T(8,128)(2,1)} %dynamic-slice_convert_fusion.3), channel_id=1, source_target_pairs={{0,64},{64,0},{1,65},{65,1},{2,66},{66,2},{3,67},{67,3},{4,68},{68... | collective-permute-start | bytes 1179656 | tf_op jit(solution)/shard_map/ppermute | solution.py:873
  261.4 69.9 %all-to-all-start.2 = ((bf16[64,24,1664]{2,1,0:T(8,128)(2,1)}), bf16[64,24,1664]{2,1,0:T(8,128)(2,1)}, u32[]{:S(2)}, u32[]{:S(2)}) async-start(bf16[64,24,1664]{2,1,0:T(8,128)(2,1)} %bitcast.234), calls=%async_computation.2 | async-start | bytes 10223616 | tf_op jit(solution)/shard_map/all_to_all | solution.py:1040
  287.8 8.0 %collective-permute-start.7 = (bf16[768,1024]{1,0:T(8,128)(2,1)S(1)}, bf16[768,1024]{1,0:T(8,128)(2,1)S(1)}, u32[]{:S(2)}, u32[]{:S(2)}) collective-permute-start(bf16[768,1024]{1,0:T(8,128)(2,1)S(1)} %dynamic-slice_convert_fusion), channel_id=1, source_target_pairs={{0,64},{64,0},{1,65},{65,1},{2,66},{66,2},{3,67},{67,3},{4,68},{68... | collective-permute-start | bytes 4718600 | tf_op jit(solution)/shard_map/ppermute | solution.py:873
  288.0 6.4 %collective-permute-start.8 = (bf16[256,1536]{1,0:T(8,128)(2,1)S(1)}, bf16[256,1536]{1,0:T(8,128)(2,1)S(1)}, u32[]{:S(2)}, u32[]{:S(2)}) collective-permute-start(bf16[256,1536]{1,0:T(8,128)(2,1)S(1)} %dynamic-slice_convert_fusion.1), channel_id=1, source_target_pairs={{0,64},{64,0},{1,65},{65,1},{2,66},{66,2},{3,67},{67,3},{4,68},{68... | collective-permute-start | bytes 2359304 | tf_op jit(solution)/shard_map/ppermute | solution.py:873
  297.9 35.3 %copy-start.60 = (f32[128,64]{1,0:T(8,128)S(1)}, f32[128,64]{1,0:T(8,128)}, u32[]{:S(2)}) copy-start(f32[128,64]{1,0:T(8,128)} %get-tuple-element.211) | copy-start | bytes 98308
  338.2 8.0 %copy-start.70 = (f32[128]{0:T(128)S(1)}, f32[128]{0:T(128)}, u32[]{:S(2)}) copy-start(f32[128]{0:T(128)} %copy-done.69) | copy-start | bytes 1540
  338.2 8.0 %copy-start.72 = (f32[128]{0:T(128)S(1)}, f32[128]{0:T(128)}, u32[]{:S(2)}) copy-start(f32[128]{0:T(128)} %get-tuple-element.246) | copy-start | bytes 1540
  338.2 166.3 %all-to-all-start.3 = ((bf16[64,24,1536]{2,1,0:T(8,128)(2,1)}), bf16[64,24,1536]{2,1,0:T(8,128)(2,1)}, u32[]{:S(2)}, u32[]{:S(2)}) async-start(bf16[64,24,1536]{2,1,0:T(8,128)(2,1)} %bitcast.236), calls=%async_computation.3 | async-start | bytes 9437184 | tf_op jit(solution)/shard_map/all_to_all | solution.py:1052
  349.1 4.1 collective-permute-start.12
  349.1 4.7 collective-permute-start.11
  351.9 152.5 %collective-permute-start.4 = (bf16[128,1536]{1,0:T(8,128)(2,1)}, bf16[128,1536]{1,0:T(8,128)(2,1)}, u32[]{:S(2)}, u32[]{:S(2)}) collective-permute-start(bf16[128,1536]{1,0:T(8,128)(2,1)} %dynamic-slice_convert_fusion.4), channel_id=1, source_target_pairs={{0,64},{64,0},{1,65},{65,1},{2,66},{66,2},{3,67},{67,3},{4,68},{68... | collective-permute-start | bytes 1179656 | tf_op jit(solution)/shard_map/ppermute | solution.py:873
  389.6 111.4 %collective-permute-start.13 = (bf16[128,1536]{1,0:T(8,128)(2,1)S(1)}, bf16[128,1536]{1,0:T(8,128)(2,1)S(1)}, u32[]{:S(2)}, u32[]{:S(2)}) collective-permute-start(bf16[128,1536]{1,0:T(8,128)(2,1)S(1)} %dynamic-slice_convert_fusion.2), channel_id=1, source_target_pairs={{0,64},{64,0},{1,65},{65,1},{2,66},{66,2},{3,67},{67,3},{4,68},{68... | collective-permute-start | bytes 1179656 | tf_op jit(solution)/shard_map/ppermute | solution.py:873
  394.6 102.8 %copy-start.55 = (f32[256,1536]{1,0:T(8,128)S(1)}, f32[256,1536]{1,0:T(8,128)}, u32[]{:S(2)}) copy-start(f32[256,1536]{1,0:T(8,128)} %get-tuple-element.88) | copy-start | bytes 4718596
  (61 other events, 136.4 us)

commit v6 on v5

--- a/solution.py
+++ b/solution.py
@@ -695,12 +695,17 @@
     dm_ref, kappa_ref, w_out_ref, w_in_ref, normed_ref, ffn_ref, drout_ref, proj_ref, y_ref,
     scaled_ref, cx_ref, cbc_ref, hp_ref, marks_ref, seg_ref, x_ref,
     gout_ref, gin_ref, dn_ref, gcx_ref, gcbc_ref, gheads_ref, gnorm_ref,
-    dproj_ref, scores_ref, dscores_ref, bc_ref,
+    dproj_ref, scores_ref, dscores_ref, bc_ref, w_ref, fetched,
 ):
     i = pl.program_id(0)
 
+    def fetch(j):
+        return pltpu.make_async_copy(w_in_ref.at[j], w_ref.at[j], fetched.at[j])
+
     @pl.when(i == 0)
     def _():
+        for j in range(4):
+            fetch(j).start()
         marks = marks_ref[...]
         for k in (0, 1):
             bc_ref[k] = jax.nn.silu(taps_pre(bc_raw(proj_ref, k), marks, cbc_ref[k])).astype(bf16)
@@ -711,13 +716,13 @@
     def _():
         j = i
         marks, cx = marks_ref[...], cx_ref[j]
-        scaled = scaled_ref[j]
+        scaled = scaled_ref[0]
         d_scaled = jnp.zeros((256, 384), f32)
         for c in range(4):
             dm = dm_ref[:, c * 384 : c * 384 + 384]
             d_scaled = d_scaled + dot(dm, w_out_ref[c], ((1,), (1,)))
             gout_ref[c] = dot(scaled, dm, ((0,), (0,))).astype(bf16)
-        y = y_ref[j]
+        y = y_ref[0]
         z = proj_ref[j, :, :384].astype(f32)
         sig = jax.nn.sigmoid(z)
         gate = z * sig
@@ -810,7 +815,8 @@
     def _():
         j = i - 4
         d_proj = dproj_ref[j]
-        dn_ref[...] += dot(d_proj, w_in_ref[0], ((1,), (1,)))
+        fetch(j).wait()
+        dn_ref[...] += dot(d_proj, w_ref[j], ((1,), (1,)))
         gin_ref[0, :, :768] = dot(normed_ref[...], d_proj[:, :768], ((0,), (0,))).astype(bf16)
         last = dot(normed_ref[...], d_proj[:, 768:], ((0,), (0,)))
         last = last + dot(ffn_ref[...], drout_ref[j], ((0,), (0,)))
@@ -823,7 +829,7 @@
         gnorm_ref[...] = jnp.broadcast_to(total, gnorm_ref.shape)
 
 
-def mixer_backward(dm, kappa, w_out, w_in, *rest):
+def mixer_backward(dm, kappa, w_out, w_in, normed, ffn_in, drout, proj, y, scaled, *rest):
     def late(i):
         return jnp.maximum(i - 4, 0)
 
@@ -851,7 +857,9 @@
             fixed(dm),
             fixed(kappa),
             w_out_spec,
-            w_in_spec,
+            pl.BlockSpec(memory_space=pl.ANY),
+            *[fixed(v) for v in (normed, ffn_in, drout, proj)],
+            *[pl.BlockSpec((1, 256, 384), lambda i: (early(i), 0, 0))] * 2,
             *[fixed(v) for v in rest],
         ],
         out_specs=[w_out_spec, w_in_spec, *[fixed(o) for o in small]],
@@ -860,13 +868,15 @@
             pltpu.VMEM((256, 256), f32),
             pltpu.VMEM((256, 256), f32),
             pltpu.VMEM((2, 256, 128), bf16),
+            pltpu.VMEM((4, 1536, 896), bf16),
+            pltpu.SemaphoreType.DMA((4,)),
         ],
         compiler_params=pltpu.CompilerParams(vmem_limit_bytes=56 * 2**20),
         cost_estimate=pl.CostEstimate(
             flops=0, bytes_accessed=0, transcendentals=0
         ),
         name="mixer_backward",
-    )(dm, kappa, w_out, w_in, *rest)
+    )(dm, kappa, w_out, w_in, normed, ffn_in, drout, proj, y, scaled, *rest)
 
 
 def swap(v):

time: 516 us -> 515 us (level)
  no operation moved by 1% of the time
where the time goes in v6:
time: 515 us; the launch traced here: 509 us
  Pallas kernels  270 us (52%)
  waiting for transfers between devices  79.8 us (15%)
  matrix products  51.2 us (10%)
  local copies, waits for them, and re-layouts  37.2 us (7%)
  starting transfers between devices  35.2 us (7%)
  other arithmetic  32.8 us (6%)
    pallas_call x1, Pallas kernels, scatter(): pl.pallas_call(scatter_kernel, out_shape=[jax.ShapeDtypeStruct(v, f32) fo...  105 us
    pallas_call x1, Pallas kernels, gather(): pl.pallas_call(gather_kernel, out_shape=outs, in_specs=[pl.BlockSpec(memo...  98.7 us
    dot_general x39, matrix products, dot(): return lax.dot_general(a, b, (dims, ((), ())), preferred_element_type=f32)  51.2 us
    all_to_all x1, waiting for transfers between devices, local(): arrived = lax.all_to_all(sent, DP, 0, 0, tiled=True).reshape(n_slots, 1664)  39.7 us
    all_to_all x1, waiting for transfers between devices, local(): lax.all_to_all(d_rows.reshape(experts, slots, 1664), DP, 0, 0, tiled=True)  33.4 us
    pallas_call x1, Pallas kernels, mixer_backward(): pl.pallas_call(backward_kernel, grid=(8,), out_shape=[jax.ShapeDtypeStruc...  29.5 us
    pallas_call x1, Pallas kernels, expert_grads(): pl.pallas_call(expert_kernel, grid=(n // block,), out_shape=[jax.ShapeDty...  18.7 us
    pallas_call x1, Pallas kernels, mixer_forward(): pl.pallas_call(forward_kernel, grid=(8,), out_shape=outs, in_specs=[fixed...  16.5 us
  transfers between devices with their start and end apart: 18, of which 3 were waited for; matrix products, arithmetic and copies ran while one was open for 20% of the time, Pallas kernels for 53%

profile of v6, /device:TPU:32, one launch (start us, length us, event | category | flops | bytes accessed | tf_op | source)
XLA Modules:
  0.0 508.9 jit_solution(9437832209647106677)
XLA Ops:
  2.8 3.5 convolution_convert_fusion.2
  7.0 98.7 %gather_weights.1 = (bf16[4,2,4,4,48,896]{5,4,3,2,1,0:T(8,128)(2,1)}, bf16[4,2,4,4,48,256]{5,4,3,2,1,0:T(8,128)(2,1)}, bf16[4,4,4,2,48,384]{5,4,3,2,1,0:T(8,128)...) custom-call(bf16[12,6448]{1,0:T(8,128)(2,1)} %in_ref.1, bf16[12,2048]{1,0:T(8,128)(2,1)} %gu_ref.1, ...), custom_call_target="tpu_custom_call" | custom-call | bytes 41943040 | tf_op jit(solution)/shard_map/gather_weights/pallas_call | solution.py:241
  105.8 7.4 %all-to-all-start = ((bf16[64,24,1536]{2,1,0:T(8,128)(2,1)}), bf16[64,24,1536]{2,1,0:T(8,128)(2,1)}, u32[]{:S(2)}, u32[]{:S(2)}) async-start(bf16[64,24,1536]{2,1,0:T(8,128)(2,1)} %bitcast.212), calls=%async_computation | async-start | bytes 9437184 | tf_op jit(solution)/shard_map/all_to_all | solution.py:991
  116.6 2.4 fusion.75
  119.0 2.0 slice_bitcast_fusion
  121.9 3.6 fusion.74
  126.9 16.5 %mixer_forward.1 = (bf16[256,1536]{1,0:T(8,128)(2,1)S(1)}, bf16[4,256,896]{2,1,0:T(8,128)(2,1)}, f32[4,256,384]{2,1,0:T(8,128)S(1)}, bf16[4,256,384]{2,1,0:T(8,1...) custom-call(bf16[256,1536]{1,0:T(8,128)(2,1)S(1)} %pad_maximum_fusion.6.x_ref, ...), custom_call_target="tpu_custom_call" | custom-call | flops 4026531840 | bytes 23068672 | tf_op jit(solution)/shard_map/mixer_forward/pallas_call | solution.py:673
  157.7 4.7 convolution_convert_fusion.1
  163.7 6.6 %all-to-all-done = bf16[64,24,1536]{2,1,0:T(8,128)(2,1)} async-done(((bf16[64,24,1536]{2,1,0:T(8,128)(2,1)}), bf16[64,24,1536]{2,1,0:T(8,128)(2,1)}, u32[]{:S(2)}, u32[]{:S(2)}) %all-to-all-start) | async-done | bytes 4718624 | tf_op jit(solution)/shard_map/all_to_all | solution.py:991
  170.3 6.9 %all-to-all-start.1 = ((bf16[64,24,1664]{2,1,0:T(8,128)(2,1)}), bf16[64,24,1664]{2,1,0:T(8,128)(2,1)}, u32[]{:S(2)}, u32[]{:S(2)}) async-start(bf16[64,24,1664]{2,1,0:T(8,128)(2,1)} %bitcast.211), calls=%async_computation.1 | async-start | bytes 10223616 | tf_op jit(solution)/shard_map/all_to_all | solution.py:1025
  177.3 1.6 convolution_bitcast_fusion.3
  195.3 2.1 broadcast_select_fusion.1
  197.4 2.0 pad_maximum_fusion.gu_ref
  199.3 39.7 %all-to-all-done.1 = bf16[64,24,1664]{2,1,0:T(8,128)(2,1)} async-done(((bf16[64,24,1664]{2,1,0:T(8,128)(2,1)}), bf16[64,24,1664]{2,1,0:T(8,128)(2,1)}, u32[]{:S(2)}, u32[]{:S(2)}) %all-to-all-start.1) | async-done | bytes 5111840 | tf_op jit(solution)/shard_map/all_to_all | solution.py:1025
  240.4 18.7 %expert_grads.1 = (bf16[1536,1664]{1,0:T(8,128)(2,1)}, bf16[1536,512]{1,0:T(8,128)(2,1)S(1)}, bf16[1536,512]{1,0:T(8,128)(2,1)S(1)}, bf16[1536,1024]{1,0:T(8,128)(2,1)}) custom-call(bf16[1536,1664]{1,0:T(8,128)(2,1)} %bitcast.44.rows_ref, bf16[1536,1536]{1,0:T(8,128)(2,1)} %bitcast.43.grad_ref, bf16[1536,1024]{1,0:T(8,128)(2,1)} %pad_maximum_fusion.gu_ref, ...), custom_call_target="tpu_custom_call" | custom-call | flops 12079595520 | bytes 27262976 | tf_op jit(solution)/shard_map/expert_grads/pallas_call | solution.py:532
  261.4 8.0 %all-to-all-start.2 = ((bf16[64,24,1664]{2,1,0:T(8,128)(2,1)}), bf16[64,24,1664]{2,1,0:T(8,128)(2,1)}, u32[]{:S(2)}, u32[]{:S(2)}) async-start(bf16[64,24,1664]{2,1,0:T(8,128)(2,1)} %bitcast.234), calls=%async_computation.2 | async-start | bytes 10223616 | tf_op jit(solution)/shard_map/all_to_all | solution.py:1050
  269.4 1.6 fusion.7
  273.6 1.8 pad_maximum_fusion.1
  275.7 4.7 fusion.82
  280.4 7.1 %fusion.2 = f32[1536,1024]{1,0:T(8,128)S(1)} fusion(bf16[1536,1024]{1,0:T(8,128)(2,1)S(1)} %copy-done.74, bf16[1536,1664]{1,0:T(8,128)(2,1)} %bitcast.44.rows_ref), kind=kOutput, calls=%fused_computation.5 | convolution fusion | flops 4831838208 | bytes 14155776 | tf_op jit(solution)/shard_map/dot_general | solution.py:31
  290.0 4.4 convolution_convert_fusion
  295.7 2.2 convert_add_fusion
  297.9 33.4 %all-to-all-done.2 = bf16[64,24,1664]{2,1,0:T(8,128)(2,1)} async-done(((bf16[64,24,1664]{2,1,0:T(8,128)(2,1)}), bf16[64,24,1664]{2,1,0:T(8,128)(2,1)}, u32[]{:S(2)}, u32[]{:S(2)}) %all-to-all-start.2) | async-done | bytes 5111840 | tf_op jit(solution)/shard_map/all_to_all | solution.py:1050
  333.9 3.1 fusion
  338.2 8.0 %all-to-all-start.3 = ((bf16[64,24,1536]{2,1,0:T(8,128)(2,1)}), bf16[64,24,1536]{2,1,0:T(8,128)(2,1)}, u32[]{:S(2)}, u32[]{:S(2)}) async-start(bf16[64,24,1536]{2,1,0:T(8,128)(2,1)} %bitcast.236), calls=%async_computation.3 | async-start | bytes 9437184 | tf_op jit(solution)/shard_map/all_to_all | solution.py:1062
  346.2 2.7 multiply_reduce_fusion.1
  350.0 1.9 dynamic-slice_convert_fusion.4
  354.9 29.5 %mixer_backward.1 = (bf16[4,1536,384]{2,1,0:T(8,128)(2,1)}, bf16[4,1536,896]{2,1,0:T(8,128)(2,1)}, f32[256,1536]{1,0:T(8,128)}, f32[4,8,384]{2,1,0:T(8,128)}, f3...) custom-call(bf16[256,1536]{1,0:T(8,128)(2,1)} %pad_maximum_fusion.9.dm_ref, ...), custom_call_target="tpu_custom_call" | custom-call | tf_op jit(solution)/shard_map/mixer_backward/pallas_call | solution.py:848
  392.7 104.7 %scatter_grads.1 = (f32[8,16,1152]{2,1,0:T(8,128)}, f32[4,32,384]{2,1,0:T(8,128)}, f32[8,128]{1,0:T(8,128)}) custom-call(bf16[4,2,4,4,48,896]{5,4,3,2,1,0:T(8,128)(2,1)} %bitcast.224, bf16[4,2,4,4,48,256]{5,4,3,2,1,0:T(8,128)(2,1)} %bitcast.223, bf16[4,4,4,2,48,384]{5,4,3,2,1,0:T(8,128)(2,1)} %bitcast.235, bf16[4,4,4,2,16,384]{5,4,3,2,1,0:T(8,128)(2,1)} %bitcast.233, ...), custom_call_target="tpu_custom_call" | custom-call | tf_op jit(solution)/shard_map/scatter_grads/pallas_call | solution.py:466
  497.6 2.2 finish_grads.1
  502.2 2.4 fusion.18
  504.6 4.1 add_convert_fusion
  (321 shorter events, 68.2 us)
Async XLA Ops:
  0.7 124.8 %collective-permute-start = (bf16[128,1536]{1,0:T(8,128)(2,1)}, bf16[128,1536]{1,0:T(8,128)(2,1)}, u32[]{:S(2)}, u32[]{:S(2)}) collective-permute-start(bf16[128,1536]{1,0:T(8,128)(2,1)} %param.17), channel_id=1, source_target_pairs={{0,64},{64,0},{1,65},{65,1},{2,66},{66,2},{3,67},{67,3},{4,68},{68... | collective-permute-start | bytes 1179656 | tf_op jit(solution)/shard_map/ppermute | solution.py:883
  0.8 124.8 %collective-permute-start.9 = (bf16[128,1536]{1,0:T(8,128)(2,1)}, bf16[128,1536]{1,0:T(8,128)(2,1)}, u32[]{:S(2)}, u32[]{:S(2)}) collective-permute-start(bf16[128,1536]{1,0:T(8,128)(2,1)} %param.18), channel_id=1, source_target_pairs={{0,64},{64,0},{1,65},{65,1},{2,66},{66,2},{3,67},{67,3},{4,68},{68... | collective-permute-start | bytes 1179656 | tf_op jit(solution)/shard_map/ppermute | solution.py:883
  105.8 8.5 %copy-start.57 = (bf16[2,4,4,4,16,128]{5,4,3,2,1,0:T(8,128)(2,1)S(1)}, bf16[2,4,4,4,16,128]{5,4,3,2,1,0:T(8,128)(2,1)}, u32[]{:S(2)}) copy-start(bf16[2,4,4,4,16,128]{5,4,3,2,1,0:T(8,128)(2,1)} %get-tuple-element.67) | copy-start | bytes 1572868
  105.8 64.6 %all-to-all-start = ((bf16[64,24,1536]{2,1,0:T(8,128)(2,1)}), bf16[64,24,1536]{2,1,0:T(8,128)(2,1)}, u32[]{:S(2)}, u32[]{:S(2)}) async-start(bf16[64,24,1536]{2,1,0:T(8,128)(2,1)} %bitcast.212), calls=%async_computation | async-start | bytes 9437184 | tf_op jit(solution)/shard_map/all_to_all | solution.py:991
  113.2 35.7 %collective-permute-start.6 = (bf16[256,1536]{1,0:T(8,128)(2,1)}, bf16[256,1536]{1,0:T(8,128)(2,1)}, u32[]{:S(2)}, u32[]{:S(2)}) collective-permute-start(bf16[256,1536]{1,0:T(8,128)(2,1)} %bitcast.46), channel_id=1, source_target_pairs={{0,64},{64,0},{1,65},{65,1},{2,66},{66,2},{3,67},{67,3},{4,68},{68... | collective-permute-start | bytes 2359304 | tf_op jit(solution)/shard_map/ppermute | solution.py:883
  113.3 82.0 %collective-permute-start.5 = (bf16[768,1024]{1,0:T(8,128)(2,1)}, bf16[768,1024]{1,0:T(8,128)(2,1)}, u32[]{:S(2)}, u32[]{:S(2)}) collective-permute-start(bf16[768,1024]{1,0:T(8,128)(2,1)} %bitcast.45), channel_id=1, source_target_pairs={{0,64},{64,0},{1,65},{65,1},{2,66},{66,2},{3,67},{67,3},{4,68},{68... | collective-permute-start | bytes 4718600 | tf_op jit(solution)/shard_map/ppermute | solution.py:883
  116.4 10.5 %copy-start.7 = (f32[4,8,128]{2,1,0:T(8,128)}, f32[4,8,128]{2,1,0:T(8,128)S(1)}, u32[]{:S(2)}) copy-start(f32[4,8,128]{2,1,0:T(8,128)S(1)} %pad.48.hp_ref) | copy-start | bytes 49156
  116.4 10.5 %copy-start.3 = (f32[256,128]{1,0:T(8,128)}, f32[256,128]{1,0:T(8,128)S(1)}, u32[]{:S(2)}) copy-start(f32[256,128]{1,0:T(8,128)S(1)} %pad.52.marks_ref) | copy-start | bytes 393220
  116.5 10.3 %copy-start.62 = (f32[1536]{0:T(1024)}, f32[1536]{0:T(1024)S(1)}, u32[]{:S(2)}) copy-start(f32[1536]{0:T(1024)S(1)} %broadcast_in_dim.89) | copy-start | bytes 18436
  116.5 10.4 %copy-start.8 = (f32[2,8,128]{2,1,0:T(8,128)}, f32[2,8,128]{2,1,0:T(8,128)S(1)}, u32[]{:S(2)}) copy-start(f32[2,8,128]{2,1,0:T(8,128)S(1)} %pad_bitcast_fusion.cbc_ref) | copy-start | bytes 24580
  119.0 28.4 %copy-start.28 = (bf16[1,4,4,2,16,384]{5,4,3,2,1,0:T(8,128)(2,1)}, bf16[1,4,4,2,16,384]{5,4,3,2,1,0:T(8,128)(2,1)S(1)}, u32[]{:S(2)}) copy-start(bf16[1,4,4,2,16,384]{5,4,3,2,1,0:T(8,128)(2,1)S(1)} %get-tuple-element.222) | copy-start | bytes 1179652
  126.8 16.5 %copy-start = (bf16[256,1536]{1,0:T(8,128)(2,1)}, bf16[256,1536]{1,0:T(8,128)(2,1)S(1)}, u32[]{:S(2)}) copy-start(bf16[256,1536]{1,0:T(8,128)(2,1)S(1)} %pad_maximum_fusion.6.x_ref) | copy-start | bytes 2359300
  126.9 16.5 %copy-start.9 = (f32[8,256]{1,0:T(8,128)}, f32[8,256]{1,0:T(8,128)S(1)}, u32[]{:S(2)}) copy-start(f32[8,256]{1,0:T(8,128)S(1)} %broadcast_in_dim.95.seg_ref) | copy-start | bytes 24580
  143.4 5.3 %collective-permute-start.1 = (f32[128,1]{1,0:T(8,128)S(1)}, f32[128,1]{1,0:T(8,128)S(1)}, u32[]{:S(2)}, u32[]{:S(2)}) collective-permute-start(f32[128,1]{1,0:T(8,128)S(1)} %constant_dynamic-slice_fusion.2), channel_id=1, source_target_pairs={{0,64},{64,0},{1,65},{65,1},{2,66},{66,2},{3,67},{67,3},{4,68},{68... | collective-permute-start | bytes 1544 | tf_op jit(solution)/shard_map/ppermute | solution.py:883
  144.8 7.2 %collective-permute-start.2 = (f32[128,1536]{1,0:T(8,128)}, f32[128,1536]{1,0:T(8,128)}, u32[]{:S(2)}, u32[]{:S(2)}) collective-permute-start(f32[128,1536]{1,0:T(8,128)} %constant_dynamic-slice_fusion.1), channel_id=1, source_target_pairs={{0,64},{64,0},{1,65},{65,1},{2,66},{66,2},{3,67},{67,3},{4,68},{68... | collective-permute-start | bytes 2359304 | tf_op jit(solution)/shard_map/ppermute | solution.py:883
  154.2 8.3 %collective-permute-start.3 = (bf16[128,1536]{1,0:T(8,128)(2,1)S(1)}, bf16[128,1536]{1,0:T(8,128)(2,1)}, u32[]{:S(2)}, u32[]{:S(2)}) collective-permute-start(bf16[128,1536]{1,0:T(8,128)(2,1)S(1)} %multiply_convert_fusion.1.ffn_ref), channel_id=1, source_target_pairs={{0,64},{64,0},{1,65},{65,1},{2,66},{66,2},{3,67},{67,3},{4,68},{68... | collective-permute-start | bytes 1179656 | tf_op jit(solution)/shard_map/ppermute | solution.py:883
  163.7 16.8 %copy-start.16 = (bf16[128,1536]{1,0:T(8,128)(2,1)}, bf16[128,1536]{1,0:T(8,128)(2,1)S(1)}, u32[]{:S(2)}) copy-start(bf16[128,1536]{1,0:T(8,128)(2,1)S(1)} %get-tuple-element.233) | copy-start | bytes 1179652
  163.7 16.8 %copy-start.18 = (bf16[128,1536]{1,0:T(8,128)(2,1)}, bf16[128,1536]{1,0:T(8,128)(2,1)S(1)}, u32[]{:S(2)}) copy-start(bf16[128,1536]{1,0:T(8,128)(2,1)S(1)} %get-tuple-element.234) | copy-start | bytes 1179652
  170.3 68.7 %all-to-all-start.1 = ((bf16[64,24,1664]{2,1,0:T(8,128)(2,1)}), bf16[64,24,1664]{2,1,0:T(8,128)(2,1)}, u32[]{:S(2)}, u32[]{:S(2)}) async-start(bf16[64,24,1664]{2,1,0:T(8,128)(2,1)} %bitcast.211), calls=%async_computation.1 | async-start | bytes 10223616 | tf_op jit(solution)/shard_map/all_to_all | solution.py:1025
  185.1 103.5 %collective-permute-start.10 = (bf16[128,1536]{1,0:T(8,128)(2,1)}, bf16[128,1536]{1,0:T(8,128)(2,1)}, u32[]{:S(2)}, u32[]{:S(2)}) collective-permute-start(bf16[128,1536]{1,0:T(8,128)(2,1)} %dynamic-slice_convert_fusion.3), channel_id=1, source_target_pairs={{0,64},{64,0},{1,65},{65,1},{2,66},{66,2},{3,67},{67,3},{4,68},{68... | collective-permute-start | bytes 1179656 | tf_op jit(solution)/shard_map/ppermute | solution.py:883
  261.4 69.9 %all-to-all-start.2 = ((bf16[64,24,1664]{2,1,0:T(8,128)(2,1)}), bf16[64,24,1664]{2,1,0:T(8,128)(2,1)}, u32[]{:S(2)}, u32[]{:S(2)}) async-start(bf16[64,24,1664]{2,1,0:T(8,128)(2,1)} %bitcast.234), calls=%async_computation.2 | async-start | bytes 10223616 | tf_op jit(solution)/shard_map/all_to_all | solution.py:1050
  287.8 8.0 %collective-permute-start.7 = (bf16[768,1024]{1,0:T(8,128)(2,1)S(1)}, bf16[768,1024]{1,0:T(8,128)(2,1)S(1)}, u32[]{:S(2)}, u32[]{:S(2)}) collective-permute-start(bf16[768,1024]{1,0:T(8,128)(2,1)S(1)} %dynamic-slice_convert_fusion), channel_id=1, source_target_pairs={{0,64},{64,0},{1,65},{65,1},{2,66},{66,2},{3,67},{67,3},{4,68},{68... | collective-permute-start | bytes 4718600 | tf_op jit(solution)/shard_map/ppermute | solution.py:883
  288.0 6.4 %collective-permute-start.8 = (bf16[256,1536]{1,0:T(8,128)(2,1)S(1)}, bf16[256,1536]{1,0:T(8,128)(2,1)S(1)}, u32[]{:S(2)}, u32[]{:S(2)}) collective-permute-start(bf16[256,1536]{1,0:T(8,128)(2,1)S(1)} %dynamic-slice_convert_fusion.1), channel_id=1, source_target_pairs={{0,64},{64,0},{1,65},{65,1},{2,66},{66,2},{3,67},{67,3},{4,68},{68... | collective-permute-start | bytes 2359304 | tf_op jit(solution)/shard_map/ppermute | solution.py:883
  297.9 35.3 %copy-start.60 = (f32[128,64]{1,0:T(8,128)S(1)}, f32[128,64]{1,0:T(8,128)}, u32[]{:S(2)}) copy-start(f32[128,64]{1,0:T(8,128)} %get-tuple-element.211) | copy-start | bytes 98308
  338.2 8.0 %copy-start.70 = (f32[128]{0:T(128)S(1)}, f32[128]{0:T(128)}, u32[]{:S(2)}) copy-start(f32[128]{0:T(128)} %copy-done.69) | copy-start | bytes 1540
  338.2 8.0 %copy-start.72 = (f32[128]{0:T(128)S(1)}, f32[128]{0:T(128)}, u32[]{:S(2)}) copy-start(f32[128]{0:T(128)} %get-tuple-element.246) | copy-start | bytes 1540
  338.2 166.4 %all-to-all-start.3 = ((bf16[64,24,1536]{2,1,0:T(8,128)(2,1)}), bf16[64,24,1536]{2,1,0:T(8,128)(2,1)}, u32[]{:S(2)}, u32[]{:S(2)}) async-start(bf16[64,24,1536]{2,1,0:T(8,128)(2,1)} %bitcast.236), calls=%async_computation.3 | async-start | bytes 9437184 | tf_op jit(solution)/shard_map/all_to_all | solution.py:1062
  349.1 4.1 collective-permute-start.12
  349.1 4.7 collective-permute-start.11
  351.9 152.7 %collective-permute-start.4 = (bf16[128,1536]{1,0:T(8,128)(2,1)}, bf16[128,1536]{1,0:T(8,128)(2,1)}, u32[]{:S(2)}, u32[]{:S(2)}) collective-permute-start(bf16[128,1536]{1,0:T(8,128)(2,1)} %dynamic-slice_convert_fusion.4), channel_id=1, source_target_pairs={{0,64},{64,0},{1,65},{65,1},{2,66},{66,2},{3,67},{67,3},{4,68},{68... | collective-permute-start | bytes 1179656 | tf_op jit(solution)/shard_map/ppermute | solution.py:883
  387.7 113.4 %collective-permute-start.13 = (bf16[128,1536]{1,0:T(8,128)(2,1)S(1)}, bf16[128,1536]{1,0:T(8,128)(2,1)S(1)}, u32[]{:S(2)}, u32[]{:S(2)}) collective-permute-start(bf16[128,1536]{1,0:T(8,128)(2,1)S(1)} %dynamic-slice_convert_fusion.2), channel_id=1, source_target_pairs={{0,64},{64,0},{1,65},{65,1},{2,66},{66,2},{3,67},{67,3},{4,68},{68... | collective-permute-start | bytes 1179656 | tf_op jit(solution)/shard_map/ppermute | solution.py:883
  392.7 104.8 %copy-start.55 = (f32[256,1536]{1,0:T(8,128)S(1)}, f32[256,1536]{1,0:T(8,128)}, u32[]{:S(2)}) copy-start(f32[256,1536]{1,0:T(8,128)} %get-tuple-element.88) | copy-start | bytes 4718596
  (61 other events, 136.4 us)

commit v7 on v6

--- a/solution.py
+++ b/solution.py
@@ -332,11 +332,18 @@
             return
         cp[i, a, 0] = remote(i, st, a, 0, source(i, st, a, opp[ax], 0), ax, right[ax])
         cp[i, a, 1] = remote(i, st, a, 1, source(i, st, a, opp[ax], 1), ax, left[ax])
+        if st:
+            direct(i, a, st)
+
+    def direct(i, a, st):
+        ax = ORDER[a][2 - st]
         cp[i, a, 2] = remote(i, st, a, 2, source(i, st, a, right[ax], 1), ax, right[ax])
         cp[i, a, 3] = remote(i, st, a, 3, source(i, st, a, left[ax], 0), ax, left[ax])
 
     for i, a in every:
         begin(i, a, 0)
+    for i, a in every:
+        direct(i, a, 0)
     for st in range(2):
         lead = ((4, 4), (4,))[st]
         for i, a in every:

time: 515 us -> 515 us (level)
  no operation moved by 1% of the time
where the time goes in v7:
time: 515 us; the launch traced here: 509 us
  Pallas kernels  270 us (52%)
  waiting for transfers between devices  79.8 us (15%)
  matrix products  51.2 us (10%)
  local copies, waits for them, and re-layouts  37.2 us (7%)
  starting transfers between devices  35.2 us (7%)
  other arithmetic  32.8 us (6%)
    pallas_call x1, Pallas kernels, scatter(): pl.pallas_call(scatter_kernel, out_shape=[jax.ShapeDtypeStruct(v, f32) fo...  105 us
    pallas_call x1, Pallas kernels, gather(): pl.pallas_call(gather_kernel, out_shape=outs, in_specs=[pl.BlockSpec(memo...  98.7 us
    dot_general x39, matrix products, dot(): return lax.dot_general(a, b, (dims, ((), ())), preferred_element_type=f32)  51.2 us
    all_to_all x1, waiting for transfers between devices, local(): arrived = lax.all_to_all(sent, DP, 0, 0, tiled=True).reshape(n_slots, 1664)  39.7 us
    all_to_all x1, waiting for transfers between devices, local(): lax.all_to_all(d_rows.reshape(experts, slots, 1664), DP, 0, 0, tiled=True)  33.4 us
    pallas_call x1, Pallas kernels, mixer_backward(): pl.pallas_call(backward_kernel, grid=(8,), out_shape=[jax.ShapeDtypeStruc...  29.5 us
    pallas_call x1, Pallas kernels, expert_grads(): pl.pallas_call(expert_kernel, grid=(n // block,), out_shape=[jax.ShapeDty...  18.7 us
    pallas_call x1, Pallas kernels, mixer_forward(): pl.pallas_call(forward_kernel, grid=(8,), out_shape=outs, in_specs=[fixed...  16.5 us
  transfers between devices with their start and end apart: 18, of which 3 were waited for; matrix products, arithmetic and copies ran while one was open for 20% of the time, Pallas kernels for 53%

profile of v7, /device:TPU:32, one launch (start us, length us, event | category | flops | bytes accessed | tf_op | source)
XLA Modules:
  0.0 508.9 jit_solution(453680619920233903)
XLA Ops:
  2.8 3.5 convolution_convert_fusion.2
  7.0 98.7 %gather_weights.1 = (bf16[4,2,4,4,48,896]{5,4,3,2,1,0:T(8,128)(2,1)}, bf16[4,2,4,4,48,256]{5,4,3,2,1,0:T(8,128)(2,1)}, bf16[4,4,4,2,48,384]{5,4,3,2,1,0:T(8,128)...) custom-call(bf16[12,6448]{1,0:T(8,128)(2,1)} %in_ref.1, bf16[12,2048]{1,0:T(8,128)(2,1)} %gu_ref.1, ...), custom_call_target="tpu_custom_call" | custom-call | bytes 41943040 | tf_op jit(solution)/shard_map/gather_weights/pallas_call | solution.py:241
  105.8 7.4 %all-to-all-start = ((bf16[64,24,1536]{2,1,0:T(8,128)(2,1)}), bf16[64,24,1536]{2,1,0:T(8,128)(2,1)}, u32[]{:S(2)}, u32[]{:S(2)}) async-start(bf16[64,24,1536]{2,1,0:T(8,128)(2,1)} %bitcast.212), calls=%async_computation | async-start | bytes 9437184 | tf_op jit(solution)/shard_map/all_to_all | solution.py:998
  116.6 2.4 fusion.75
  119.0 2.0 slice_bitcast_fusion
  121.9 3.6 fusion.74
  126.9 16.5 %mixer_forward.1 = (bf16[256,1536]{1,0:T(8,128)(2,1)S(1)}, bf16[4,256,896]{2,1,0:T(8,128)(2,1)}, f32[4,256,384]{2,1,0:T(8,128)S(1)}, bf16[4,256,384]{2,1,0:T(8,1...) custom-call(bf16[256,1536]{1,0:T(8,128)(2,1)S(1)} %pad_maximum_fusion.6.x_ref, ...), custom_call_target="tpu_custom_call" | custom-call | flops 4026531840 | bytes 23068672 | tf_op jit(solution)/shard_map/mixer_forward/pallas_call | solution.py:680
  157.7 4.7 convolution_convert_fusion.1
  163.7 6.6 %all-to-all-done = bf16[64,24,1536]{2,1,0:T(8,128)(2,1)} async-done(((bf16[64,24,1536]{2,1,0:T(8,128)(2,1)}), bf16[64,24,1536]{2,1,0:T(8,128)(2,1)}, u32[]{:S(2)}, u32[]{:S(2)}) %all-to-all-start) | async-done | bytes 4718624 | tf_op jit(solution)/shard_map/all_to_all | solution.py:998
  170.3 6.9 %all-to-all-start.1 = ((bf16[64,24,1664]{2,1,0:T(8,128)(2,1)}), bf16[64,24,1664]{2,1,0:T(8,128)(2,1)}, u32[]{:S(2)}, u32[]{:S(2)}) async-start(bf16[64,24,1664]{2,1,0:T(8,128)(2,1)} %bitcast.211), calls=%async_computation.1 | async-start | bytes 10223616 | tf_op jit(solution)/shard_map/all_to_all | solution.py:1032
  177.3 1.6 convolution_bitcast_fusion.3
  195.3 2.1 broadcast_select_fusion.1
  197.4 2.0 pad_maximum_fusion.gu_ref
  199.3 39.7 %all-to-all-done.1 = bf16[64,24,1664]{2,1,0:T(8,128)(2,1)} async-done(((bf16[64,24,1664]{2,1,0:T(8,128)(2,1)}), bf16[64,24,1664]{2,1,0:T(8,128)(2,1)}, u32[]{:S(2)}, u32[]{:S(2)}) %all-to-all-start.1) | async-done | bytes 5111840 | tf_op jit(solution)/shard_map/all_to_all | solution.py:1032
  240.4 18.7 %expert_grads.1 = (bf16[1536,1664]{1,0:T(8,128)(2,1)}, bf16[1536,512]{1,0:T(8,128)(2,1)S(1)}, bf16[1536,512]{1,0:T(8,128)(2,1)S(1)}, bf16[1536,1024]{1,0:T(8,128)(2,1)}) custom-call(bf16[1536,1664]{1,0:T(8,128)(2,1)} %bitcast.44.rows_ref, bf16[1536,1536]{1,0:T(8,128)(2,1)} %bitcast.43.grad_ref, bf16[1536,1024]{1,0:T(8,128)(2,1)} %pad_maximum_fusion.gu_ref, ...), custom_call_target="tpu_custom_call" | custom-call | flops 12079595520 | bytes 27262976 | tf_op jit(solution)/shard_map/expert_grads/pallas_call | solution.py:539
  261.4 8.0 %all-to-all-start.2 = ((bf16[64,24,1664]{2,1,0:T(8,128)(2,1)}), bf16[64,24,1664]{2,1,0:T(8,128)(2,1)}, u32[]{:S(2)}, u32[]{:S(2)}) async-start(bf16[64,24,1664]{2,1,0:T(8,128)(2,1)} %bitcast.234), calls=%async_computation.2 | async-start | bytes 10223616 | tf_op jit(solution)/shard_map/all_to_all | solution.py:1057
  269.4 1.6 fusion.7
  273.6 1.8 pad_maximum_fusion.1
  275.7 4.7 fusion.82
  280.4 7.1 %fusion.2 = f32[1536,1024]{1,0:T(8,128)S(1)} fusion(bf16[1536,1024]{1,0:T(8,128)(2,1)S(1)} %copy-done.74, bf16[1536,1664]{1,0:T(8,128)(2,1)} %bitcast.44.rows_ref), kind=kOutput, calls=%fused_computation.5 | convolution fusion | flops 4831838208 | bytes 14155776 | tf_op jit(solution)/shard_map/dot_general | solution.py:31
  290.0 4.4 convolution_convert_fusion
  295.7 2.2 convert_add_fusion
  297.9 33.4 %all-to-all-done.2 = bf16[64,24,1664]{2,1,0:T(8,128)(2,1)} async-done(((bf16[64,24,1664]{2,1,0:T(8,128)(2,1)}), bf16[64,24,1664]{2,1,0:T(8,128)(2,1)}, u32[]{:S(2)}, u32[]{:S(2)}) %all-to-all-start.2) | async-done | bytes 5111840 | tf_op jit(solution)/shard_map/all_to_all | solution.py:1057
  333.9 3.1 fusion
  338.2 8.0 %all-to-all-start.3 = ((bf16[64,24,1536]{2,1,0:T(8,128)(2,1)}), bf16[64,24,1536]{2,1,0:T(8,128)(2,1)}, u32[]{:S(2)}, u32[]{:S(2)}) async-start(bf16[64,24,1536]{2,1,0:T(8,128)(2,1)} %bitcast.236), calls=%async_computation.3 | async-start | bytes 9437184 | tf_op jit(solution)/shard_map/all_to_all | solution.py:1069
  346.2 2.7 multiply_reduce_fusion.1
  350.0 1.9 dynamic-slice_convert_fusion.4
  354.9 29.5 %mixer_backward.1 = (bf16[4,1536,384]{2,1,0:T(8,128)(2,1)}, bf16[4,1536,896]{2,1,0:T(8,128)(2,1)}, f32[256,1536]{1,0:T(8,128)}, f32[4,8,384]{2,1,0:T(8,128)}, f3...) custom-call(bf16[256,1536]{1,0:T(8,128)(2,1)} %pad_maximum_fusion.9.dm_ref, ...), custom_call_target="tpu_custom_call" | custom-call | tf_op jit(solution)/shard_map/mixer_backward/pallas_call | solution.py:855
  392.7 104.7 %scatter_grads.1 = (f32[8,16,1152]{2,1,0:T(8,128)}, f32[4,32,384]{2,1,0:T(8,128)}, f32[8,128]{1,0:T(8,128)}) custom-call(bf16[4,2,4,4,48,896]{5,4,3,2,1,0:T(8,128)(2,1)} %bitcast.224, bf16[4,2,4,4,48,256]{5,4,3,2,1,0:T(8,128)(2,1)} %bitcast.223, bf16[4,4,4,2,48,384]{5,4,3,2,1,0:T(8,128)(2,1)} %bitcast.235, bf16[4,4,4,2,16,384]{5,4,3,2,1,0:T(8,128)(2,1)} %bitcast.233, ...), custom_call_target="tpu_custom_call" | custom-call | tf_op jit(solution)/shard_map/scatter_grads/pallas_call | solution.py:473
  497.6 2.2 finish_grads.1
  502.2 2.4 fusion.18
  504.6 4.1 add_convert_fusion
  (321 shorter events, 68.2 us)
Async XLA Ops:
  0.7 124.8 %collective-permute-start = (bf16[128,1536]{1,0:T(8,128)(2,1)}, bf16[128,1536]{1,0:T(8,128)(2,1)}, u32[]{:S(2)}, u32[]{:S(2)}) collective-permute-start(bf16[128,1536]{1,0:T(8,128)(2,1)} %param.17), channel_id=1, source_target_pairs={{0,64},{64,0},{1,65},{65,1},{2,66},{66,2},{3,67},{67,3},{4,68},{68... | collective-permute-start | bytes 1179656 | tf_op jit(solution)/shard_map/ppermute | solution.py:890
  0.8 124.8 %collective-permute-start.9 = (bf16[128,1536]{1,0:T(8,128)(2,1)}, bf16[128,1536]{1,0:T(8,128)(2,1)}, u32[]{:S(2)}, u32[]{:S(2)}) collective-permute-start(bf16[128,1536]{1,0:T(8,128)(2,1)} %param.18), channel_id=1, source_target_pairs={{0,64},{64,0},{1,65},{65,1},{2,66},{66,2},{3,67},{67,3},{4,68},{68... | collective-permute-start | bytes 1179656 | tf_op jit(solution)/shard_map/ppermute | solution.py:890
  105.8 8.5 %copy-start.57 = (bf16[2,4,4,4,16,128]{5,4,3,2,1,0:T(8,128)(2,1)S(1)}, bf16[2,4,4,4,16,128]{5,4,3,2,1,0:T(8,128)(2,1)}, u32[]{:S(2)}) copy-start(bf16[2,4,4,4,16,128]{5,4,3,2,1,0:T(8,128)(2,1)} %get-tuple-element.67) | copy-start | bytes 1572868
  105.8 64.6 %all-to-all-start = ((bf16[64,24,1536]{2,1,0:T(8,128)(2,1)}), bf16[64,24,1536]{2,1,0:T(8,128)(2,1)}, u32[]{:S(2)}, u32[]{:S(2)}) async-start(bf16[64,24,1536]{2,1,0:T(8,128)(2,1)} %bitcast.212), calls=%async_computation | async-start | bytes 9437184 | tf_op jit(solution)/shard_map/all_to_all | solution.py:998
  113.2 35.7 %collective-permute-start.6 = (bf16[256,1536]{1,0:T(8,128)(2,1)}, bf16[256,1536]{1,0:T(8,128)(2,1)}, u32[]{:S(2)}, u32[]{:S(2)}) collective-permute-start(bf16[256,1536]{1,0:T(8,128)(2,1)} %bitcast.46), channel_id=1, source_target_pairs={{0,64},{64,0},{1,65},{65,1},{2,66},{66,2},{3,67},{67,3},{4,68},{68... | collective-permute-start | bytes 2359304 | tf_op jit(solution)/shard_map/ppermute | solution.py:890
  113.3 82.0 %collective-permute-start.5 = (bf16[768,1024]{1,0:T(8,128)(2,1)}, bf16[768,1024]{1,0:T(8,128)(2,1)}, u32[]{:S(2)}, u32[]{:S(2)}) collective-permute-start(bf16[768,1024]{1,0:T(8,128)(2,1)} %bitcast.45), channel_id=1, source_target_pairs={{0,64},{64,0},{1,65},{65,1},{2,66},{66,2},{3,67},{67,3},{4,68},{68... | collective-permute-start | bytes 4718600 | tf_op jit(solution)/shard_map/ppermute | solution.py:890
  116.4 10.5 %copy-start.7 = (f32[4,8,128]{2,1,0:T(8,128)}, f32[4,8,128]{2,1,0:T(8,128)S(1)}, u32[]{:S(2)}) copy-start(f32[4,8,128]{2,1,0:T(8,128)S(1)} %pad.48.hp_ref) | copy-start | bytes 49156
  116.4 10.5 %copy-start.3 = (f32[256,128]{1,0:T(8,128)}, f32[256,128]{1,0:T(8,128)S(1)}, u32[]{:S(2)}) copy-start(f32[256,128]{1,0:T(8,128)S(1)} %pad.52.marks_ref) | copy-start | bytes 393220
  116.5 10.3 %copy-start.62 = (f32[1536]{0:T(1024)}, f32[1536]{0:T(1024)S(1)}, u32[]{:S(2)}) copy-start(f32[1536]{0:T(1024)S(1)} %broadcast_in_dim.89) | copy-start | bytes 18436
  116.5 10.4 %copy-start.8 = (f32[2,8,128]{2,1,0:T(8,128)}, f32[2,8,128]{2,1,0:T(8,128)S(1)}, u32[]{:S(2)}) copy-start(f32[2,8,128]{2,1,0:T(8,128)S(1)} %pad_bitcast_fusion.cbc_ref) | copy-start | bytes 24580
  119.0 28.4 %copy-start.28 = (bf16[1,4,4,2,16,384]{5,4,3,2,1,0:T(8,128)(2,1)}, bf16[1,4,4,2,16,384]{5,4,3,2,1,0:T(8,128)(2,1)S(1)}, u32[]{:S(2)}) copy-start(bf16[1,4,4,2,16,384]{5,4,3,2,1,0:T(8,128)(2,1)S(1)} %get-tuple-element.222) | copy-start | bytes 1179652
  126.8 16.5 %copy-start = (bf16[256,1536]{1,0:T(8,128)(2,1)}, bf16[256,1536]{1,0:T(8,128)(2,1)S(1)}, u32[]{:S(2)}) copy-start(bf16[256,1536]{1,0:T(8,128)(2,1)S(1)} %pad_maximum_fusion.6.x_ref) | copy-start | bytes 2359300
  126.9 16.5 %copy-start.9 = (f32[8,256]{1,0:T(8,128)}, f32[8,256]{1,0:T(8,128)S(1)}, u32[]{:S(2)}) copy-start(f32[8,256]{1,0:T(8,128)S(1)} %broadcast_in_dim.95.seg_ref) | copy-start | bytes 24580
  143.4 5.3 %collective-permute-start.1 = (f32[128,1]{1,0:T(8,128)S(1)}, f32[128,1]{1,0:T(8,128)S(1)}, u32[]{:S(2)}, u32[]{:S(2)}) collective-permute-start(f32[128,1]{1,0:T(8,128)S(1)} %constant_dynamic-slice_fusion.2), channel_id=1, source_target_pairs={{0,64},{64,0},{1,65},{65,1},{2,66},{66,2},{3,67},{67,3},{4,68},{68... | collective-permute-start | bytes 1544 | tf_op jit(solution)/shard_map/ppermute | solution.py:890
  144.8 7.2 %collective-permute-start.2 = (f32[128,1536]{1,0:T(8,128)}, f32[128,1536]{1,0:T(8,128)}, u32[]{:S(2)}, u32[]{:S(2)}) collective-permute-start(f32[128,1536]{1,0:T(8,128)} %constant_dynamic-slice_fusion.1), channel_id=1, source_target_pairs={{0,64},{64,0},{1,65},{65,1},{2,66},{66,2},{3,67},{67,3},{4,68},{68... | collective-permute-start | bytes 2359304 | tf_op jit(solution)/shard_map/ppermute | solution.py:890
  154.2 8.3 %collective-permute-start.3 = (bf16[128,1536]{1,0:T(8,128)(2,1)S(1)}, bf16[128,1536]{1,0:T(8,128)(2,1)}, u32[]{:S(2)}, u32[]{:S(2)}) collective-permute-start(bf16[128,1536]{1,0:T(8,128)(2,1)S(1)} %multiply_convert_fusion.1.ffn_ref), channel_id=1, source_target_pairs={{0,64},{64,0},{1,65},{65,1},{2,66},{66,2},{3,67},{67,3},{4,68},{68... | collective-permute-start | bytes 1179656 | tf_op jit(solution)/shard_map/ppermute | solution.py:890
  163.7 16.8 %copy-start.16 = (bf16[128,1536]{1,0:T(8,128)(2,1)}, bf16[128,1536]{1,0:T(8,128)(2,1)S(1)}, u32[]{:S(2)}) copy-start(bf16[128,1536]{1,0:T(8,128)(2,1)S(1)} %get-tuple-element.233) | copy-start | bytes 1179652
  163.7 16.8 %copy-start.18 = (bf16[128,1536]{1,0:T(8,128)(2,1)}, bf16[128,1536]{1,0:T(8,128)(2,1)S(1)}, u32[]{:S(2)}) copy-start(bf16[128,1536]{1,0:T(8,128)(2,1)S(1)} %get-tuple-element.234) | copy-start | bytes 1179652
  170.3 68.7 %all-to-all-start.1 = ((bf16[64,24,1664]{2,1,0:T(8,128)(2,1)}), bf16[64,24,1664]{2,1,0:T(8,128)(2,1)}, u32[]{:S(2)}, u32[]{:S(2)}) async-start(bf16[64,24,1664]{2,1,0:T(8,128)(2,1)} %bitcast.211), calls=%async_computation.1 | async-start | bytes 10223616 | tf_op jit(solution)/shard_map/all_to_all | solution.py:1032
  185.1 103.5 %collective-permute-start.10 = (bf16[128,1536]{1,0:T(8,128)(2,1)}, bf16[128,1536]{1,0:T(8,128)(2,1)}, u32[]{:S(2)}, u32[]{:S(2)}) collective-permute-start(bf16[128,1536]{1,0:T(8,128)(2,1)} %dynamic-slice_convert_fusion.3), channel_id=1, source_target_pairs={{0,64},{64,0},{1,65},{65,1},{2,66},{66,2},{3,67},{67,3},{4,68},{68... | collective-permute-start | bytes 1179656 | tf_op jit(solution)/shard_map/ppermute | solution.py:890
  261.4 69.9 %all-to-all-start.2 = ((bf16[64,24,1664]{2,1,0:T(8,128)(2,1)}), bf16[64,24,1664]{2,1,0:T(8,128)(2,1)}, u32[]{:S(2)}, u32[]{:S(2)}) async-start(bf16[64,24,1664]{2,1,0:T(8,128)(2,1)} %bitcast.234), calls=%async_computation.2 | async-start | bytes 10223616 | tf_op jit(solution)/shard_map/all_to_all | solution.py:1057
  287.8 8.0 %collective-permute-start.7 = (bf16[768,1024]{1,0:T(8,128)(2,1)S(1)}, bf16[768,1024]{1,0:T(8,128)(2,1)S(1)}, u32[]{:S(2)}, u32[]{:S(2)}) collective-permute-start(bf16[768,1024]{1,0:T(8,128)(2,1)S(1)} %dynamic-slice_convert_fusion), channel_id=1, source_target_pairs={{0,64},{64,0},{1,65},{65,1},{2,66},{66,2},{3,67},{67,3},{4,68},{68... | collective-permute-start | bytes 4718600 | tf_op jit(solution)/shard_map/ppermute | solution.py:890
  288.0 6.4 %collective-permute-start.8 = (bf16[256,1536]{1,0:T(8,128)(2,1)S(1)}, bf16[256,1536]{1,0:T(8,128)(2,1)S(1)}, u32[]{:S(2)}, u32[]{:S(2)}) collective-permute-start(bf16[256,1536]{1,0:T(8,128)(2,1)S(1)} %dynamic-slice_convert_fusion.1), channel_id=1, source_target_pairs={{0,64},{64,0},{1,65},{65,1},{2,66},{66,2},{3,67},{67,3},{4,68},{68... | collective-permute-start | bytes 2359304 | tf_op jit(solution)/shard_map/ppermute | solution.py:890
  297.9 35.3 %copy-start.60 = (f32[128,64]{1,0:T(8,128)S(1)}, f32[128,64]{1,0:T(8,128)}, u32[]{:S(2)}) copy-start(f32[128,64]{1,0:T(8,128)} %get-tuple-element.211) | copy-start | bytes 98308
  338.2 8.0 %copy-start.70 = (f32[128]{0:T(128)S(1)}, f32[128]{0:T(128)}, u32[]{:S(2)}) copy-start(f32[128]{0:T(128)} %copy-done.69) | copy-start | bytes 1540
  338.2 8.0 %copy-start.72 = (f32[128]{0:T(128)S(1)}, f32[128]{0:T(128)}, u32[]{:S(2)}) copy-start(f32[128]{0:T(128)} %get-tuple-element.246) | copy-start | bytes 1540
  338.2 166.4 %all-to-all-start.3 = ((bf16[64,24,1536]{2,1,0:T(8,128)(2,1)}), bf16[64,24,1536]{2,1,0:T(8,128)(2,1)}, u32[]{:S(2)}, u32[]{:S(2)}) async-start(bf16[64,24,1536]{2,1,0:T(8,128)(2,1)} %bitcast.236), calls=%async_computation.3 | async-start | bytes 9437184 | tf_op jit(solution)/shard_map/all_to_all | solution.py:1069
  349.1 4.1 collective-permute-start.12
  349.1 4.7 collective-permute-start.11
  351.9 152.7 %collective-permute-start.4 = (bf16[128,1536]{1,0:T(8,128)(2,1)}, bf16[128,1536]{1,0:T(8,128)(2,1)}, u32[]{:S(2)}, u32[]{:S(2)}) collective-permute-start(bf16[128,1536]{1,0:T(8,128)(2,1)} %dynamic-slice_convert_fusion.4), channel_id=1, source_target_pairs={{0,64},{64,0},{1,65},{65,1},{2,66},{66,2},{3,67},{67,3},{4,68},{68... | collective-permute-start | bytes 1179656 | tf_op jit(solution)/shard_map/ppermute | solution.py:890
  387.7 113.4 %collective-permute-start.13 = (bf16[128,1536]{1,0:T(8,128)(2,1)S(1)}, bf16[128,1536]{1,0:T(8,128)(2,1)S(1)}, u32[]{:S(2)}, u32[]{:S(2)}) collective-permute-start(bf16[128,1536]{1,0:T(8,128)(2,1)S(1)} %dynamic-slice_convert_fusion.2), channel_id=1, source_target_pairs={{0,64},{64,0},{1,65},{65,1},{2,66},{66,2},{3,67},{67,3},{4,68},{68... | collective-permute-start | bytes 1179656 | tf_op jit(solution)/shard_map/ppermute | solution.py:890
  392.7 104.8 %copy-start.55 = (f32[256,1536]{1,0:T(8,128)S(1)}, f32[256,1536]{1,0:T(8,128)}, u32[]{:S(2)}) copy-start(f32[256,1536]{1,0:T(8,128)} %get-tuple-element.88) | copy-start | bytes 4718596
  (61 other events, 136.4 us)
